TPU v7x, 128 devices: a whole 4x4x4 slice. The times are simulated.
128 devices in a mesh: fsdp: 16 (over y, z), ctx: 4 (over x_lo, core), tp: 2 (over x_hi).
Axes of the slice: x: 4 (x_hi: 2, x_lo: 2; x = x_hi * 2 + x_lo), y: 4, z: 4, core: 2. Of those that a mesh axis runs over, the one named last changes fastest.
Arguments:
- tokens: bfloat16 [16384, 1536], P(('fsdp', 'ctx')), may hold values from -16 to 16
- segments: int32 [4, 4096], replicated, may hold values from 0 to 3, as said below
- w_query: bfloat16 [1536, 1536], P('fsdp', 'tp'), may hold values from -0.15625 to 0.15625
- key_matrix: bfloat16 [1536, 256], P('fsdp', 'tp'), may hold values from -0.15625 to 0.15625
- value_matrix: bfloat16 [1536, 256], P('fsdp', 'tp'), may hold values from -0.15625 to 0.15625
- b_query: bfloat16 [1536], P('tp'), may hold values from -3 to 3
- key_bias_vector: bfloat16 [256], P('tp'), may hold values from -3 to 3
- value_bias_vector: bfloat16 [256], P('tp'), may hold values from -3 to 3
- w_out: bfloat16 [1536, 1536], P('tp', 'fsdp'), may hold values from -0.875 to 0.875
- norm_attn: bfloat16 [1536], replicated, may hold values from 0.5 to 1.5
- norm_ffn: bfloat16 [1536], replicated, may hold values from 0.5 to 1.5
- w_gate: bfloat16 [1536, 8960], P('fsdp', 'tp'), may hold values from -0.15625 to 0.15625
- w_up: bfloat16 [1536, 8960], P('fsdp', 'tp'), may hold values from -0.15625 to 0.15625
- w_down: bfloat16 [8960, 1536], P('tp', 'fsdp'), may hold values from -0.0625 to 0.0625
- cotangent: bfloat16 [16384, 1536], P(('fsdp', 'ctx')), may hold values from -16 to 16
Outputs:
- output: bfloat16 [16384, 1536], P(('fsdp', 'ctx'))
- grad_tokens: float32 [16384, 1536], P(('fsdp', 'ctx'))
- grad_query: float32 [1536, 1536], P(('fsdp', 'ctx'), 'tp')
- grad_key: float32 [1536, 256], P(('fsdp', 'ctx'), 'tp')
- grad_value: float32 [1536, 256], P(('fsdp', 'ctx'), 'tp')
- grad_query_bias: float32 [12, 128], P('tp', ('fsdp', 'ctx'))
- grad_key_bias: float32 [2, 128], P('tp', ('fsdp', 'ctx'))
- grad_value_bias: float32 [2, 128], P('tp', ('fsdp', 'ctx'))
- grad_out_proj: float32 [1536, 1536], P('tp', ('fsdp', 'ctx'))
- grad_norm_attn: float32 [1536], P(('fsdp', 'ctx'))
- grad_norm_ffn: float32 [1536], P(('fsdp', 'ctx'))
- grad_gate: float32 [1536, 8960], P(('fsdp', 'ctx'), 'tp')
- grad_up: float32 [1536, 8960], P(('fsdp', 'ctx'), 'tp')
- grad_down: float32 [8960, 1536], P('tp', ('fsdp', 'ctx'))
Inputs may be any that keep to these rules, and one draw needn't show every extreme that they name: `segments`: in each of the 4 sequences segment numbers start at 0 and rise by at most one from one token to the next. In every draw one sequence, chosen by the seed, has three documents, the first ending and the last beginning within 256 tokens of the sequence's ends; where there are several sequences, another has four documents.
All inputs are finite; a program needn't handle non-finite values.
Results may differ from a plain program's by a relative error of at most 0.025.
Values may be sent and summed in bfloat16 or wider, within the bound.
A program may use at most 256 MiB of HBM per device.

v0:
```python
import functools
import math

import jax
import jax.numpy as jnp
from jax import lax
from jax.experimental import pallas as pl
from jax.experimental.pallas import tpu as pltpu
from jax.sharding import PartitionSpec as P

MESH = pl.DeviceIdType.MESH
VM = pl.BlockSpec(memory_space=pltpu.VMEM)
DMA = pltpu.SemaphoreType.DMA
BF = jnp.bfloat16
F32 = jnp.float32

epsilon = 1e-06
rope_base = 1000000.0
masked_score = -1e30
KEYS = 512


class Place:
    def __init__(self):
        f = lax.axis_index("fsdp")
        c = lax.axis_index("ctx")
        self.y, self.z = f // 4, f % 4
        self.lo, self.k = c // 2, c % 2
        self.t = lax.axis_index("tp")

    def along_y(self, j):
        return {"fsdp": lax.rem(self.y + j, 4) * 4 + self.z}

    def along_z(self, j):
        return {"fsdp": self.y * 4 + lax.rem(self.z + j, 4)}

    @property
    def sibling(self):
        return {"ctx": self.lo * 2 + 1 - self.k}

    def in_ring(self, lo, t):
        return {"ctx": lo * 2 + self.k, "tp": t}

    @property
    def others(self):
        return [(self.lo, 1 - self.t), (1 - self.lo, self.t), (1 - self.lo, 1 - self.t)]


def greet(devices):
    barrier = pltpu.get_barrier_semaphore()
    for device in devices:
        pl.semaphore_signal(barrier, inc=1, device_id=device, device_id_type=MESH)
    pl.semaphore_wait(barrier, len(devices))


def describe(source, target, send_sem, recv_sem, device):
    return pltpu.make_async_remote_copy(
        src_ref=source,
        dst_ref=target,
        send_sem=send_sem,
        recv_sem=recv_sem,
        device_id=device,
        device_id_type=MESH,
    )


def send(source, target, send_sem, recv_sem, device):
    copy = describe(source, target, send_sem, recv_sem, device)
    copy.start()
    return copy


def comm_call(body, outs, scratch, collective_id, mib, *args):
    return pl.pallas_call(
        body,
        out_shape=outs,
        in_specs=[VM] * len(args),
        out_specs=[VM] * len(outs),
        scratch_shapes=scratch,
        compiler_params=pltpu.CompilerParams(
            collective_id=collective_id, has_side_effects=True, vmem_limit_bytes=mib << 20
        ),
    )(*args)


def shape(dims, kind):
    return jax.ShapeDtypeStruct(dims, kind)


def opening_kernel(w, tok, dy, w_all, tok2, dy_all, s1, r1, s2, r2, ts, tr, ds, dr, fs, fr):
    me = Place()
    y, z, lo, k, t = me.y, me.z, me.lo, me.k, me.t
    rows = w.shape[0] // 2
    halves = (pl.ds(0, rows), pl.ds(rows, rows))
    near = [me.in_ring(1 - lo, t), me.in_ring(1 - lo, 1 - t)]
    greet(
        [me.along_z(j) for j in (1, 2, 3)]
        + [me.along_y(j) for j in (1, 2, 3)]
        + [me.sibling]
        + near
    )
    first = []
    for half, along in ((0, me.along_z), (1, me.along_y)):
        part = halves[half]
        first.append(
            [
                send(
                    w.at[part],
                    w_all.at[y, z, part],
                    s1.at[half, j - 1],
                    r1.at[half, j - 1],
                    along(j),
                )
                for j in (2, 1, 3)
            ]
        )
    rest = []
    mine = dy.shape[0] // 2
    near_copies = [
        send(dy.at[pl.ds(t * mine, mine)], dy_all.at[lo, t, k], ds.at[i], dr.at[i], near[i])
        for i in (0, 1)
    ]
    rest.append(send(tok, tok2.at[k], ts, tr, me.sibling))
    own = [
        send(
            dy.at[pl.ds(h * mine, mine)], dy_all.at[lo, h, k], fs.at[2 + h], fr.at[2 + h], me.sibling
        )
        for h in (0, 1)
    ]
    rest += own
    for half, along in ((0, me.along_y), (1, me.along_z)):
        part = halves[half]
        for j in (2, 1, 3):
            rest.append(
                send(
                    w.at[part],
                    w_all.at[y, z, part],
                    s2.at[half, 0, j - 1],
                    r2.at[half, 0, j - 1],
                    along(j),
                )
            )
    w_all[y, z] = w[...]
    tok2[k] = tok[...]
    for h in (0, 1):
        dy_all[lo, h, k] = dy[pl.ds(h * mine, mine)]
    for order in range(3):
        for half, along in ((0, me.along_y), (1, me.along_z)):
            part = halves[half]
            offset = (2, 1, 3)[order]
            first[half][order].wait()
            if half == 0:
                block = w_all.at[y, lax.rem(z - offset + 4, 4), part]
            else:
                block = w_all.at[lax.rem(y - offset + 4, 4), z, part]
            for j in (2, 1, 3):
                rest.append(
                    send(
                        block,
                        block,
                        s2.at[half, offset, j - 1],
                        r2.at[half, offset, j - 1],
                        along(j),
                    )
                )
    for i, half in ((0, t), (1, 1 - t)):
        near_copies[i].wait()
        block = dy_all.at[1 - lo, half, k]
        rest.append(send(block, block, fs.at[i], fr.at[i], me.sibling))
    for copy in rest:
        copy.wait()


def opening(w, tok, dy):
    rows, width = w.shape
    count, model = tok.shape
    return comm_call(
        opening_kernel,
        [
            shape((4, 4, rows, width), BF),
            shape((2, count, model), BF),
            shape((2, 2, 2, count // 2, model), BF),
        ],
        [
            DMA((2, 3)),
            DMA((2, 3)),
            DMA((2, 4, 3)),
            DMA((2, 4, 3)),
            DMA,
            DMA,
            DMA((2,)),
            DMA((2,)),
            DMA((4,)),
            DMA((4,)),
        ],
        1,
        32,
        w,
        tok,
        dy,
    )


def keys_kernel(mine, kv, s1, r1, s2, r2):
    me = Place()
    k = me.k
    own = me.z * 2 + me.lo
    steps = [(dz, dl) for dz in (2, 1, 3, 0) for dl in (0, 1) if dz or dl]

    def partner(dz, dl):
        return {
            "fsdp": me.y * 4 + lax.rem(me.z + dz, 4),
            "ctx": lax.rem(me.lo + dl, 2) * 2 + k,
        }

    greet([partner(dz, dl) for dz, dl in steps] + [me.sibling])
    copies = [
        send(mine, kv.at[k, own], s1.at[i], r1.at[i], partner(dz, dl))
        for i, (dz, dl) in enumerate(steps)
    ]
    rest = [send(mine, kv.at[k, own], s2.at[7], r2.at[7], me.sibling)]
    kv[k, own] = mine[...]
    for i in (6, 2, 4, 3, 5, 0, 1):
        dz, dl = steps[i]
        copies[i].wait()
        block = kv.at[k, lax.rem(me.z - dz + 4, 4) * 2 + lax.rem(me.lo + dl, 2)]
        rest.append(send(block, block, s2.at[i], r2.at[i], me.sibling))
    for copy in rest:
        copy.wait()


def share_keys(mine):
    rows, width = mine.shape
    return comm_call(
        keys_kernel,
        [shape((2, 8, rows, width), BF)],
        [DMA((7,)), DMA((7,)), DMA((8,)), DMA((8,))],
        2,
        16,
        mine,
    )[0]


def over_rows(a, b):
    return lax.dot_general(a, b, (((0,), (0,)), ((), ())), preferred_element_type=F32)


def by_columns(a, b):
    return lax.dot_general(a, b, (((1,), (1,)), ((), ())), preferred_element_type=F32)


def plain(a, b):
    return lax.dot_general(a, b, (((1,), (0,)), ((), ())), preferred_element_type=F32)


def visible_pairs(block, first, start, rows):
    key = block * KEYS + lax.broadcasted_iota(jnp.int32, (KEYS, rows), 0)
    row = first + lax.broadcasted_iota(jnp.int32, (1, rows), 1)
    return (key >= start) & (key <= row)


def attend_kernel(heads, start_ref, q, kv, o, exact, lse, top, total, acc):
    me = Place()
    rows = q.shape[0]
    size = q.shape[1] // heads
    index = me.z * 2 + me.lo
    first = index * rows
    start = start_ref[...]
    top[...] = jnp.full_like(top, masked_score)
    total[...] = jnp.zeros_like(total)
    acc[...] = jnp.zeros_like(acc)

    def step(block, _):
        keys = kv[0, block]
        values = kv[1, block]
        seen = visible_pairs(block, first, start, rows)
        for h in range(heads):
            s = by_columns(keys, q[:, h * size : (h + 1) * size])
            s = jnp.where(seen, s, masked_score)
            before = top[h : h + 1]
            now = jnp.maximum(before, jnp.max(s, axis=0, keepdims=True))
            p = jnp.exp(s - now)
            shrink = jnp.exp(before - now)
            top[h : h + 1] = now
            total[h : h + 1] = total[h : h + 1] * shrink + jnp.sum(p, axis=0, keepdims=True)
            acc[h] = acc[h] * shrink + over_rows(values, p.astype(BF))
        return 0

    lax.fori_loop(0, index + 1, step, 0)
    lse[...] = jnp.zeros_like(lse)
    for h in range(heads):
        sums = total[h : h + 1]
        lse[h : h + 1] = top[h : h + 1] + jnp.log(sums)
        out = acc[h] / sums
        exact[h] = out
        o[:, h * size : (h + 1) * size] = out.T.astype(BF)


def attend(start, q, kv, heads):
    rows, width = q.shape
    return pl.pallas_call(
        functools.partial(attend_kernel, heads),
        out_shape=[
            shape((rows, width), BF),
            shape((heads, width // heads, rows), F32),
            shape((8, rows), F32),
        ],
        in_specs=[VM] * 3,
        out_specs=[VM] * 3,
        scratch_shapes=[
            pltpu.VMEM((8, rows), F32),
            pltpu.VMEM((8, rows), F32),
            pltpu.VMEM((heads, width // heads, rows), F32),
        ],
        compiler_params=pltpu.CompilerParams(vmem_limit_bytes=32 << 20),
    )(start, q, kv)


def attend_back_kernel(heads, start_ref, lse, q, kv, exact, do, dq, dkv, dots, acc):
    me = Place()
    rows = q.shape[0]
    size = q.shape[1] // heads
    index = me.z * 2 + me.lo
    first = index * rows
    start = start_ref[...]
    for h in range(heads):
        part = slice(h * size, (h + 1) * size)
        product = exact[h] * do[:, part].astype(F32).T
        dots[h : h + 1] = jnp.sum(product, axis=0, keepdims=True)
    acc[...] = jnp.zeros_like(acc)

    def step(block, _):
        keys = kv[0, block]
        values = kv[1, block]
        seen = visible_pairs(block, first, start, rows)
        dk = jnp.zeros((KEYS, size), F32)
        dv = jnp.zeros((KEYS, size), F32)
        for h in range(heads):
            q_h = q[:, h * size : (h + 1) * size]
            do_h = do[:, h * size : (h + 1) * size]
            s = jnp.where(seen, by_columns(keys, q_h), masked_score)
            p = jnp.exp(s - lse[h : h + 1])
            dv = dv + plain(p.astype(BF), do_h)
            dp = by_columns(values, do_h)
            ds = (p * (dp - dots[h : h + 1])).astype(BF)
            dk = dk + plain(ds, q_h)
            acc[h] = acc[h] + over_rows(keys, ds)
        dkv[0, block] = dk
        dkv[1, block] = dv
        return 0

    lax.fori_loop(0, index + 1, step, 0)

    def blank(block, _):
        dkv[0, block] = jnp.zeros((KEYS, size), F32)
        dkv[1, block] = jnp.zeros((KEYS, size), F32)
        return 0

    lax.fori_loop(index + 1, kv.shape[1], blank, 0)
    for h in range(heads):
        dq[:, h * size : (h + 1) * size] = acc[h].T


def attend_back(start, lse, q, kv, exact, do, heads):
    rows, width = q.shape
    return pl.pallas_call(
        functools.partial(attend_back_kernel, heads),
        out_shape=[shape((rows, width), F32), shape(kv.shape, F32)],
        in_specs=[VM] * 6,
        out_specs=[VM] * 2,
        scratch_shapes=[
            pltpu.VMEM((8, rows), F32),
            pltpu.VMEM((heads, width // heads, rows), F32),
        ],
        compiler_params=pltpu.CompilerParams(vmem_limit_bytes=40 << 20),
    )(start, lse, q, kv, exact, do)


def pair_sum(me, part, r1, s1, r2, sems):
    k, t = me.k, me.t
    copy = send(part.at[1 - k], r1, sems.at[0], sems.at[1], me.sibling)
    copy.wait()
    s1[...] = (part[k, 1 - t].astype(F32) + r1[1 - t].astype(F32)).astype(BF)
    copy = send(s1, r2, sems.at[2], sems.at[3], me.in_ring(me.lo, 1 - t))
    here = part[k, t].astype(F32) + r1[t].astype(F32)
    copy.wait()
    return here + r2[...].astype(F32)


def norm_back(grad_normed, normed, factor):
    return factor * (grad_normed - normed * jnp.mean(grad_normed * normed, axis=-1, keepdims=True))


def block_kernel(
    part, tok, gain, dy_hbm, w_hbm,
    x1, dx1, dxl, gnf, ysum, g_hbm,
    w, dy, dy_t, h2, h2_t, hid, gate_back, up_back, whole, m1, m2, m3, pb, s1, r1, r2, yb, ry,
    ls, ms, hs, hr, fs, fr, ps, pr, xs, xr, ys, yr, gs, gr, os,
):
    me = Place()
    lo, k, t = me.lo, me.k, me.t
    rows, model = tok.shape
    both = 2 * rows

    def chip(i):
        return lax.rem(lo + lax.rem((i + 1) // 2, 2), 2), lax.rem(t + i // 2, 2)

    def columns(i):
        return pl.ds(pl.multiple_of(i * both, both), both)

    loads = [pltpu.make_async_copy(dy_hbm, dy, ls.at[3])]
    loads += [pltpu.make_async_copy(w_hbm.at[i], w.at[i], ls.at[i]) for i in range(3)]
    for copy in loads:
        copy.start()
    greet([me.in_ring(*chip(i)) for i in (1, 2, 3)] + [me.sibling])
    cores = send(part.at[1 - k], m1, ms.at[0], ms.at[1], me.sibling)
    loads[0].wait()

    def turn_dy(i, _):
        lo_i, t_i = chip(i)
        dy_t[:, columns(i)] = dy[lo_i, t_i].reshape(both, model).T
        return 0

    cores.wait()
    m2[...] = (part[k, 1 - t].astype(F32) + m1[1 - t].astype(F32)).astype(BF)
    across = send(m2, m3, ms.at[2], ms.at[3], me.in_ring(lo, 1 - t))
    lax.fori_loop(0, 4, turn_dy, 0)
    x = tok[...].astype(F32) + part[k, t].astype(F32) + m1[t].astype(F32)
    across.wait()
    x = x + m3[...].astype(F32)
    x1[...] = x
    factor = lax.rsqrt(jnp.mean(x * x, axis=-1, keepdims=True) + epsilon)
    h2[lo, t, k] = (x * factor * gain[...]).astype(BF)

    def hidden_copy(i):
        block = h2.at[lo, t, k]
        return describe(block, block, hs.at[i - 1], hr.at[i - 1], me.in_ring(*chip(i)))

    def hidden_share(i):
        lo_i, t_i = chip(i)
        block = h2.at[lo_i, t_i, k]
        return describe(block, block, fs.at[i], fr.at[i], me.sibling)

    def part_share(i):
        return describe(pb.at[i], r1.at[i], ps.at[i], pr.at[i], me.sibling)

    def part_copy(i):
        return describe(
            s1.at[i], r2.at[i - 1], xs.at[i - 1], xr.at[i - 1], me.in_ring(*chip(i))
        )

    def result_share(i):
        return describe(yb.at[i], ry.at[i], ys.at[i], yr.at[i], me.sibling)

    for i in (1, 2, 3):
        hidden_copy(i).start()
    hidden_share(0).start()
    for copy in loads[1:]:
        copy.wait()

    def finish(i):
        part_share(i).wait_recv()
        s1[i] = (s1[i].astype(F32) + r1[i].astype(F32)).astype(BF)

        @pl.when(i > 0)
        def _():
            part_copy(i).start()

        whole[...] = by_columns(hid[i], w[2]).reshape(2, rows, model)
        yb[i] = whole[1 - k].astype(BF)
        ysum[i] = whole[k].astype(BF)
        result_share(i).start()
        lo_i, t_i = chip(i)
        h2_t[:, columns(i)] = h2[lo_i, t_i].reshape(both, model).T

    def step(i, _):
        lo_i, t_i = chip(i)

        @pl.when(i > 0)
        def _():
            hidden_copy(i).wait_recv()
            hidden_share(i).start()
            finish(i - 1)

        hidden_share(i).wait_recv()
        h = h2[lo_i, t_i].reshape(both, model)
        d = dy[lo_i, t_i].reshape(both, model)
        gate = plain(h, w[0])
        up = plain(h, w[1])
        sigmoid_gate = jax.nn.sigmoid(gate)
        silu_gate = gate * sigmoid_gate
        hid[i] = (silu_gate * up).astype(BF)
        grad_inner = plain(d, w[2])
        slope = sigmoid_gate * (1.0 + gate * (1.0 - sigmoid_gate))
        gate_back[i] = (grad_inner * up * slope).astype(BF)
        up_back[i] = (grad_inner * silu_gate).astype(BF)
        whole[...] = (by_columns(gate_back[i], w[0]) + by_columns(up_back[i], w[1])).reshape(
            2, rows, model
        )
        pb[i] = whole[1 - k].astype(BF)
        s1[i] = whole[k].astype(BF)
        part_share(i).start()
        return 0

    lax.fori_loop(0, 4, step, 0)
    finish(3)

    def gradient(i, left_t, right):
        flat = right.shape[0] * right.shape[1]
        step_rows = model // 3

        def some(m, _):
            r = pl.ds(pl.multiple_of(m * step_rows, step_rows), step_rows)
            w[i, r] = plain(left_t[r, :], right[...].reshape(flat, right.shape[2])).astype(BF)
            return 0

        lax.fori_loop(0, 3, some, 0)
        copy = pltpu.make_async_copy(w.at[i], g_hbm.at[i], os.at[i])
        copy.start()
        return copy

    outs = [gradient(2, dy_t, hid)]

    grad = s1[0].astype(F32)
    for i in (1, 2, 3):
        part_copy(i).wait_recv()
        grad = grad + r2[i - 1].astype(F32)
    x = x1[...]
    factor = lax.rsqrt(jnp.mean(x * x, axis=-1, keepdims=True) + epsilon)
    normed = x * factor
    gnf[...] = jnp.sum(grad * normed, axis=0, keepdims=True)
    back = dy[lo, t, k].astype(F32) + norm_back(grad * gain[...], normed, factor)
    dx1[...] = back
    dxl[k, t] = back.astype(BF)
    block = dxl.at[k, t]
    across = send(block, block, gs.at[0], gr.at[0], me.in_ring(lo, 1 - t))
    rest = [send(block, block, gs.at[1], gr.at[1], me.sibling)]
    outs.append(gradient(0, h2_t, gate_back))
    across.wait()
    block = dxl.at[k, 1 - t]
    rest.append(send(block, block, gs.at[2], gr.at[2], me.sibling))
    outs.append(gradient(1, h2_t, up_back))
    for i in range(4):
        result_share(i).wait()
        ysum[i] = (ysum[i].astype(F32) + ry[i].astype(F32)).astype(BF)
        hidden_share(i).wait_send()
        part_share(i).wait_send()
    for i in (1, 2, 3):
        hidden_copy(i).wait_send()
        part_copy(i).wait_send()
    for copy in rest + outs:
        copy.wait()


def block(part, tok, gain, dy, w):
    rows, model = tok.shape
    hidden = w.shape[2]
    any_place = pl.BlockSpec(memory_space=pl.ANY)
    quarter = pltpu.VMEM((4, rows, model), BF)
    inner = pltpu.VMEM((4, 2 * rows, hidden), BF)
    turned = pltpu.VMEM((model, 8 * rows), BF)
    return pl.pallas_call(
        block_kernel,
        out_shape=[
            shape((rows, model), F32),
            shape((rows, model), F32),
            shape((2, 2, rows, model), BF),
            shape((1, model), F32),
            shape((4, rows, model), BF),
            shape(w.shape, BF),
        ],
        in_specs=[VM] * 3 + [any_place] * 2,
        out_specs=[VM] * 5 + [any_place],
        scratch_shapes=[
            pltpu.VMEM(w.shape, BF),
            pltpu.VMEM(dy.shape, BF),
            turned,
            pltpu.VMEM(dy.shape, BF),
            turned,
            inner,
            inner,
            inner,
            pltpu.VMEM((2, rows, model), F32),
            pltpu.VMEM((2, rows, model), BF),
            pltpu.VMEM((rows, model), BF),
            pltpu.VMEM((rows, model), BF),
            quarter,
            quarter,
            quarter,
            pltpu.VMEM((3, rows, model), BF),
            quarter,
            quarter,
            DMA((4,)),
            DMA((4,)),
            DMA((3,)),
            DMA((3,)),
            DMA((4,)),
            DMA((4,)),
            DMA((4,)),
            DMA((4,)),
            DMA((3,)),
            DMA((3,)),
            DMA((4,)),
            DMA((4,)),
            DMA((3,)),
            DMA((3,)),
            DMA((3,)),
        ],
        compiler_params=pltpu.CompilerParams(
            collective_id=3, has_side_effects=True, vmem_limit_bytes=62 << 20
        ),
    )(part, tok, gain, dy, w)


def keys_back_kernel(dkv, mine, r1, s1, r2, as1, ar1, as2, ar2):
    me = Place()
    k = me.k
    own = me.z * 2 + me.lo
    steps = [(dz, dl) for dz in (2, 1, 3, 0) for dl in (0, 1) if dz or dl]

    def block(dz, dl):
        return lax.rem(me.z + dz, 4) * 2 + lax.rem(me.lo + dl, 2)

    def partner(dz, dl):
        return {
            "fsdp": me.y * 4 + lax.rem(me.z + dz, 4),
            "ctx": lax.rem(me.lo + dl, 2) * 2 + k,
        }

    greet([partner(dz, dl) for dz, dl in steps] + [me.sibling])
    cores = send(dkv.at[1 - k], r1, as1, ar1, me.sibling)
    cores.wait()
    s1[...] = (dkv[k] + r1[...]).astype(BF)
    copies = [
        send(s1.at[block(dz, dl)], r2.at[i], as2.at[i], ar2.at[i], partner(dz, dl))
        for i, (dz, dl) in enumerate(steps)
    ]
    total = s1[own].astype(F32)
    for i, copy in enumerate(copies):
        copy.wait()
        total = total + r2[i].astype(F32)
    mine[...] = total


def return_keys(dkv):
    _, count, rows, width = dkv.shape
    return comm_call(
        keys_back_kernel,
        [shape((rows, width), F32)],
        [
            pltpu.VMEM((count, rows, width), F32),
            pltpu.VMEM((count, rows, width), BF),
            pltpu.VMEM((count - 1, rows, width), BF),
            DMA,
            DMA,
            DMA((count - 1,)),
            DMA((count - 1,)),
        ],
        5,
        24,
        dkv,
    )[0]


def tokens_kernel(part, tok, dx1, gain, grad, gna, r1, s1, r2, sems, gs, gr):
    me = Place()
    t = me.t
    greet([me.in_ring(me.lo, 1 - t), me.sibling])
    dh1 = pair_sum(me, part, r1, s1, r2, sems)
    x = tok[...].astype(F32)
    factor = lax.rsqrt(jnp.mean(x * x, axis=-1, keepdims=True) + epsilon)
    normed = x * factor
    gna[...] = jnp.sum(dh1 * normed, axis=0, keepdims=True)
    grad[t] = (dx1[...] + norm_back(dh1 * gain[...], normed, factor)).astype(BF)
    block = grad.at[t]
    send(block, block, gs, gr, me.in_ring(me.lo, 1 - t)).wait()


def tokens_back(part, tok, dx1, gain):
    rows, model = tok.shape
    return comm_call(
        tokens_kernel,
        [shape((2, rows, model), BF), shape((1, model), F32)],
        [
            pltpu.VMEM((2, rows, model), BF),
            pltpu.VMEM((rows, model), BF),
            pltpu.VMEM((rows, model), BF),
            DMA((4,)),
            DMA,
            DMA,
        ],
        6,
        24,
        part,
        tok,
        dx1,
        gain,
    )


def closing_kernel(
    ga, ext, ffn, ysum, x1, a_all, ext_all, ffn_all, out,
    r1, sm, r2, fin, e1, esm, e2, yr2,
    as1, ar1, as2, ar2, as3, ar3, es, er, fs, fr, xs, xr, ys, yr,
):
    me = Place()
    y, z, lo, k, t = me.y, me.z, me.lo, me.k, me.t
    c = lo * 2 + k

    def in_ctx(j):
        return {"ctx": lax.rem(c + j, 4)}

    ring = [(dt, dc) for dt in (0, 1) for dc in range(4) if dt or dc]

    def in_x(dt, dc):
        return {"ctx": lax.rem(c + dc, 4), "tp": lax.rem(t + dt, 2)}

    greet(
        [me.along_z(j) for j in (1, 2, 3)]
        + [me.along_y(j) for j in (1, 2, 3)]
        + [in_x(dt, dc) for dt, dc in ring]
    )
    small = [
        send(ext.at[:, lax.rem(z + j, 4)], e1.at[j - 1], es.at[0, j - 1], er.at[0, j - 1], me.along_z(j))
        for j in (2, 1, 3)
    ]
    large = [
        [
            send(
                ga.at[:, lax.rem(z + j, 4), 0], r1.at[0, j - 1], as1.at[0, j - 1], ar1.at[0, j - 1], me.along_z(j)
            )
            for j in (2, 1, 3)
        ],
        [
            send(
                ga.at[lax.rem(y + j, 4), :, 1], r1.at[1, j - 1], as1.at[1, j - 1], ar1.at[1, j - 1], me.along_y(j)
            )
            for j in (2, 1, 3)
        ],
    ]
    rest = [
        send(ffn.at[lax.rem(c + j, 4)], ffn_all.at[c], fs.at[j - 1], fr.at[j - 1], in_ctx(j))
        for j in (1, 2, 3)
    ]
    ffn_all[c] = ffn[c]
    near = [(1 - lo, t), (1 - lo, 1 - t), (lo, 1 - t)]
    results = [
        send(ysum.at[i + 1], yr2.at[i], ys.at[i], yr.at[i], me.in_ring(*near[i])) for i in range(3)
    ]
    for copy in small:
        copy.wait()
    esm[...] = (ext[:, z] + e1[0]) + (e1[1] + e1[2])
    small = [
        send(esm.at[lax.rem(y + j, 4)], e2.at[j - 1], es.at[1, j - 1], er.at[1, j - 1], me.along_y(j))
        for j in (2, 1, 3)
    ]
    for copy in small:
        copy.wait()
    ext_all[t, c] = (esm[y] + e2[0]) + (e2[1] + e2[2])
    block = ext_all.at[t, c]
    rest += [
        send(block, block, xs.at[i], xr.at[i], in_x(dt, dc)) for i, (dt, dc) in enumerate(ring)
    ]
    for half in (0, 1):
        for copy in large[half]:
            copy.wait()
        here = ga[:, z, 0] if half == 0 else ga[y, :, 1]
        total = here.astype(F32)
        for j in range(3):
            total = total + r1[half, j].astype(F32)
        sm[half] = total.astype(BF)
    last = [
        [
            send(
                sm.at[0, lax.rem(y + j, 4)], r2.at[0, j - 1], as2.at[0, j - 1], ar2.at[0, j - 1], me.along_y(j)
            )
            for j in (2, 1, 3)
        ],
        [
            send(
                sm.at[1, lax.rem(z + j, 4)], r2.at[1, j - 1], as2.at[1, j - 1], ar2.at[1, j - 1], me.along_z(j)
            )
            for j in (2, 1, 3)
        ],
    ]
    result = x1[...] + ysum[0].astype(F32)
    for i in range(3):
        results[i].wait()
        result = result + yr2[i].astype(F32)
    out[t] = result.astype(BF)
    block = out.at[t]
    rest.append(send(block, block, ys.at[3], yr.at[3], me.in_ring(lo, 1 - t)))
    half_rows = sm.shape[2]
    quarter = half_rows // 2
    for half in (0, 1):
        for copy in last[half]:
            copy.wait()
        here = sm[0, y] if half == 0 else sm[1, z]
        total = here.astype(F32)
        for j in range(3):
            total = total + r2[half, j].astype(F32)
        fin[2 * half] = total[:quarter]
        fin[2 * half + 1] = total[quarter:]
    a_all[c] = fin[c]
    rest += [
        send(fin.at[lax.rem(c + j, 4)], a_all.at[c], as3.at[j - 1], ar3.at[j - 1], in_ctx(j))
        for j in (1, 2, 3)
    ]
    for copy in rest:
        copy.wait()


def closing(ga, ext, ffn, ysum, x1):
    _, _, _, rows, width = ga.shape
    slice_rows, model = x1.shape
    return comm_call(
        closing_kernel,
        [
            shape((4, rows // 2, width), F32),
            shape((2, 4) + ext.shape[2:], F32),
            shape(ffn.shape, BF),
            shape((2, slice_rows, model), BF),
        ],
        [
            pltpu.VMEM((2, 3, 4, rows, width), BF),
            pltpu.VMEM((2, 4, rows, width), BF),
            pltpu.VMEM((2, 3, rows, width), BF),
            pltpu.VMEM((4, rows // 2, width), F32),
            pltpu.VMEM((3, 4) + ext.shape[2:], F32),
            pltpu.VMEM((4,) + ext.shape[2:], F32),
            pltpu.VMEM((3,) + ext.shape[2:], F32),
            pltpu.VMEM((3, slice_rows, model), BF),
            DMA((2, 3)),
            DMA((2, 3)),
            DMA((2, 3)),
            DMA((2, 3)),
            DMA((3,)),
            DMA((3,)),
            DMA((2, 3)),
            DMA((2, 3)),
            DMA((3,)),
            DMA((3,)),
            DMA((7,)),
            DMA((7,)),
            DMA((4,)),
            DMA((4,)),
        ],
        7,
        40,
        ga,
        ext,
        ffn,
        ysum,
        x1,
    )


def rotate(values_in, cosine, sine):
    half_size = values_in.shape[-1] // 2
    front, back = values_in[..., :half_size], values_in[..., half_size:]
    return jnp.concatenate([front * cosine - back * sine, back * cosine + front * sine], axis=-1)


def shards(
    tokens,
    segments,
    w_query,
    key_matrix,
    value_matrix,
    b_query,
    key_bias_vector,
    value_bias_vector,
    w_out,
    norm_attn,
    norm_ffn,
    w_gate,
    w_up,
    w_down,
    cotangent,
):
    f = lax.axis_index("fsdp")
    c = lax.axis_index("ctx")
    t = lax.axis_index("tp")
    seq, quarter = f // 4, f % 4
    lo, k = c // 2, c % 2
    is_key = k == 0
    size = key_matrix.shape[1]
    query_width = w_query.shape[1] // 2
    heads = query_width // size
    own_width = query_width + size
    model = tokens.shape[1]
    count = tokens.shape[0]
    slice_rows = count // 2
    shard_rows = w_query.shape[0]
    hidden = w_gate.shape[1] // 4
    padded = -(-hidden // 128) * 128

    def hidden_slice(w, axis):
        return lax.dynamic_slice_in_dim(w, c * hidden, hidden, axis)

    own_ffn = jnp.stack(
        [hidden_slice(w_gate, 1), hidden_slice(w_up, 1), hidden_slice(w_down, 0).T]
    )
    own_ffn = jnp.pad(own_ffn, ((0, 0), (0, 0), (0, padded - hidden)))
    ffn_weights = lax.all_gather(own_ffn, "fsdp", axis=1, tiled=True)

    own_attn = jnp.concatenate(
        [
            lax.dynamic_slice_in_dim(w_query, k * query_width, query_width, 1),
            jnp.where(is_key, key_matrix, value_matrix),
            lax.dynamic_slice_in_dim(w_out, k * query_width, query_width, 0).T,
        ],
        axis=1,
    )
    attn_all, tok2, dy_all = opening(own_attn, tokens, cotangent)
    attn_all = attn_all.reshape(model, own_width + query_width)
    in_all, out_all = attn_all[:, :own_width], attn_all[:, own_width:]
    own_tokens = lax.dynamic_slice_in_dim(tokens, t * slice_rows, slice_rows, 0)

    seg_row = lax.dynamic_index_in_dim(segments, seq, 0, keepdims=False)
    rows = 2 * count
    first = (quarter * 2 + lo) * rows
    seg_mine = lax.dynamic_slice_in_dim(seg_row, first, rows)
    starts = jnp.zeros((rows,), jnp.int32)
    for number in range(1, 4):
        begin = jnp.sum((seg_row < number).astype(jnp.int32))
        starts = jnp.where(seg_mine == number, begin, starts)
    pos = (first + jnp.arange(rows, dtype=jnp.int32) - starts).astype(F32)
    frequency = jnp.exp(
        jnp.arange(size // 2, dtype=F32) * (-2.0 * math.log(rope_base) / size)
    )
    angles = pos[:, None, None] * frequency
    cosine, sine = jnp.cos(angles), jnp.sin(angles)
    kv_cosine = jnp.where(is_key, cosine[:, 0], 1.0)
    kv_sine = jnp.where(is_key, sine[:, 0], 0.0)
    starts = starts[None, :]
    query_scale = 1.0 / math.sqrt(size)

    gain_attn = norm_attn.astype(F32)
    gain_ffn = norm_ffn.astype(F32)
    x = tok2.reshape(rows, model).astype(F32)
    h1 = (x * lax.rsqrt(jnp.mean(x * x, axis=-1, keepdims=True) + epsilon) * gain_attn).astype(BF)
    bias = jnp.concatenate(
        [
            lax.dynamic_slice_in_dim(b_query, k * query_width, query_width, 0),
            jnp.where(is_key, key_bias_vector, value_bias_vector),
        ]
    ).astype(F32)
    linear = plain(h1, in_all) + bias
    q_lin = linear[:, :query_width].reshape(rows, heads, size)
    q = (rotate(q_lin, cosine, sine) * query_scale).astype(BF).reshape(rows, query_width)
    kv = share_keys(rotate(linear[:, query_width:], kv_cosine, kv_sine).astype(BF))
    ob, exact, lse = attend(starts, q, kv, heads)
    part = by_columns(ob, out_all).astype(BF).reshape(2, 2, slice_rows, model)
    x1, dx1, dxl, grad_norm_two, ysum, ffn_grads = block(
        part, own_tokens, gain_ffn[None], dy_all, ffn_weights
    )
    ffn_grads = lax.psum_scatter(ffn_grads, "fsdp", scatter_dimension=1, tiled=True)
    dxl = dxl.reshape(rows, model)

    grad_out = over_rows(dxl, ob)
    do = plain(dxl, out_all).astype(BF)
    dq, dkv = attend_back(starts, lse, q, kv, exact, do, heads)
    dkv = return_keys(dkv)
    dq = rotate(dq.reshape(rows, heads, size) * query_scale, cosine, -sine).reshape(
        rows, query_width
    )
    dkv = rotate(dkv, kv_cosine, -kv_sine)
    back = jnp.concatenate([dq, dkv], axis=1)
    grad_bias = jnp.sum(back, axis=0)
    back = back.astype(BF)
    grad_in = over_rows(h1, back)
    part_one = by_columns(back, in_all).astype(BF).reshape(2, 2, slice_rows, model)
    grad_tokens, grad_norm_one = tokens_back(part_one, own_tokens, dx1, gain_attn[None])

    grad_attn = jnp.concatenate([grad_in, grad_out], axis=1).astype(BF)
    owner_rows = shard_rows // 4
    ext = jnp.concatenate(
        [
            grad_norm_one.reshape(16, 4, owner_rows),
            grad_norm_two.reshape(16, 4, owner_rows),
            grad_bias.reshape(heads + 1, 16, 4, 2).transpose(1, 2, 0, 3).reshape(16, 4, -1),
        ],
        axis=2,
    )
    ext = jnp.pad(ext, ((0, 0), (0, 4), (0, 128 - ext.shape[2]))).reshape(4, 4, 8, 128)
    ffn_blocks = ffn_grads.reshape(3, 4, owner_rows, padded).transpose(1, 0, 2, 3)
    ffn_blocks = jnp.pad(
        ffn_blocks.reshape(4, 3 * owner_rows, padded), ((0, 0), (0, -3 * owner_rows % 16), (0, 0))
    )
    a_all, ext_all, ffn_all, output = closing(
        grad_attn.reshape(4, 4, 2, shard_rows // 2, own_width + query_width),
        ext,
        ffn_blocks,
        ysum,
        x1,
    )
    a_all = a_all[:2] + a_all[2:]
    ffn_all = ffn_all[:, : 3 * owner_rows, :hidden].astype(F32)
    ffn_all = ffn_all.reshape(4, 3, owner_rows, hidden).transpose(1, 2, 0, 3)
    ffn_all = ffn_all.reshape(3, owner_rows, 4 * hidden)
    own_ext = lax.dynamic_index_in_dim(ext_all, c, 2, keepdims=False)
    norms = jnp.sum(own_ext.reshape(8, 128), axis=0)
    biases = lax.dynamic_index_in_dim(own_ext, t, 0, keepdims=False)
    biases = biases[:2] + biases[2:]
    biases = biases[:, 2 * owner_rows : 2 * owner_rows + 2 * (heads + 1)].reshape(2, heads + 1, 2)
    return (
        output.reshape(count, model),
        grad_tokens.reshape(count, model).astype(F32),
        jnp.concatenate([a_all[0, :, :query_width], a_all[1, :, :query_width]], axis=1),
        a_all[0, :, query_width:own_width],
        a_all[1, :, query_width:own_width],
        biases[:, :heads].reshape(2 * heads, 2),
        biases[0, heads:],
        biases[1, heads:],
        jnp.concatenate([a_all[0, :, own_width:], a_all[1, :, own_width:]], axis=1).T,
        norms[:owner_rows],
        norms[owner_rows : 2 * owner_rows],
        ffn_all[0],
        ffn_all[1],
        ffn_all[2].T,
    )


def solution(mesh):
    both = ("fsdp", "ctx")
    in_specs = (
        P(both, None),
        P(),
        P("fsdp", "tp"),
        P("fsdp", "tp"),
        P("fsdp", "tp"),
        P("tp"),
        P("tp"),
        P("tp"),
        P("tp", "fsdp"),
        P(),
        P(),
        P("fsdp", "tp"),
        P("fsdp", "tp"),
        P("tp", "fsdp"),
        P(both, None),
    )
    out_specs = (
        P(both, None),
        P(both, None),
        P(both, "tp"),
        P(both, "tp"),
        P(both, "tp"),
        P("tp", both),
        P("tp", both),
        P("tp", both),
        P("tp", both),
        P(both),
        P(both),
        P(both, "tp"),
        P(both, "tp"),
        P("tp", both),
    )
    return jax.shard_map(shards, mesh=mesh, in_specs=in_specs, out_specs=out_specs, check_vma=False)
```

profile of v0, /device:TPU:1, one launch (start us, length us, event | category | flops | bytes accessed | tf_op | source)
XLA Modules:
  0.0 363.5 jit_solution(16351574861667329582)
XLA Ops:
  7.2 1.1 copy-done
  8.6 1.4 dynamic-slice_bitcast_fusion.1
  10.0 1.0 fusion.15
  11.1 0.6 reshape.306.gain
  11.9 34.9 %shard_map.254 = (bf16[4,4,96,896]{3,2,1,0:T(8,128)(2,1)}, bf16[2,256,1536]{2,1,0:T(8,128)(2,1)S(1)}, bf16[2,2,2,128,1536]{4,3,2,1,0:T(8,128)(2,1)S(1)}) custom-call(bf16[96,896]{1,0:T(8,128)(2,1)S(1)} %pad_maximum_fusion.3.w, bf16[256,1536]{1,0:T(8,128)(2,1)S(1)} %copy-done.8, bf16[256,1536]{1,0:T(8,128)(2,1)S(1)} %copy-done.10), custom_call_target="tpu_custom_call" | custom-call | tf_op jit(solution)/shard_map/pallas_call | solution.py:74
  47.7 0.7 copy-done.7
  48.5 3.9 %fusion.8 = f32[512,512]{1,0:T(8,128)} fusion(bf16[512,1536]{1,0:T(8,128)(2,1)S(1)} %fusion.1, bf16[1536,896]{1,0:T(8,128)(2,1)} %bitcast.4, f32[512]{0:T(512)S(1)} %maximum_convert_fusion), kind=kOutput, calls=%fused_computation.17 | convolution fusion | flops 805568512 | bytes 4196352 | tf_op jit(solution)/shard_map/dot_general | solution.py:253
  52.4 1.2 slice.133
  53.9 1.6 fusion.21
  55.5 2.8 compare_select_fusion.2.start_ref
  58.2 2.9 fusion.20
  61.8 0.6 copy-done.27
  62.5 25.5 %shard_map.255.kv = bf16[2,8,512,128]{3,2,1,0:T(8,128)(2,1)S(1)} custom-call(bf16[512,128]{1,0:T(8,128)(2,1)S(1)} %pad_maximum_fusion.4.mine), custom_call_target="tpu_custom_call" | custom-call | tf_op jit(solution)/shard_map/pallas_call | solution.py:74
  88.1 2.2 shard_map.256
  90.3 0.9 constant_dynamic-slice_fusion.2.tok
  91.4 3.4 convolution_convert_fusion.1
  94.8 19.6 %all-gather.2.cloned.1.call-done.w_hbm = bf16[3,1536,1152]{2,1,0:T(8,128)(2,1)} async-done(((bf16[3,96,1152]{2,1,0:T(8,128)(2,1)}), bf16[3,1536,1152]{2,1,0:T(8,128)(2,1)}) %all-gather.2.cloned.1.call-update) | async-done | bytes 10616848 | tf_op jit(solution)/shard_map/all_gather | solution.py:905
  114.4 86.9 %shard_map.257 = (f32[128,1536]{1,0:T(8,128)}, f32[128,1536]{1,0:T(8,128)}, bf16[2,2,128,1536]{3,2,1,0:T(8,128)(2,1)}, f32[1,1536]{1,0:T(1,128)}, bf16[4,128,153...) custom-call(bf16[2,2,128,1536]{3,2,1,0:T(8,128)(2,1)} %bitcast.96, bf16[128,1536]{1,0:T(8,128)(2,1)} %constant_dynamic-slice_fusion.2.tok, ...), custom_call_target="tpu_custom_call" | custom-call | tf_op jit(solution)/shard_map/pallas_call | solution.py:562
  201.3 0.9 copy-done.26
  202.8 1.6 copy.37
  204.5 2.9 convolution_convert_fusion.4.do
  207.4 3.0 shard_map.258
  210.4 2.1 copy-done.4
  213.3 2.2 copy-done.5
  215.5 39.8 %shard_map.259 = f32[512,128]{1,0:T(8,128)S(1)} custom-call(f32[2,8,512,128]{3,2,1,0:T(8,128)S(1)} %copy-done.5), custom_call_target="tpu_custom_call" | custom-call | tf_op jit(solution)/shard_map/pallas_call | solution.py:74
  255.4 1.2 multiply_subtract_fusion.2
  256.7 2.7 convolution_convert_fusion
  259.4 26.9 %shard_map.260 = (bf16[2,128,1536]{2,1,0:T(8,128)(2,1)S(1)}, f32[1,1536]{1,0:T(1,128)S(1)}) custom-call(bf16[2,2,128,1536]{3,2,1,0:T(8,128)(2,1)S(1)} %bitcast.86, bf16[128,1536]{1,0:T(8,128)(2,1)S(1)} %copy-done.6, f32[128,1536]{1,0:T(8,128)S(1)} %copy-done.11, f32[1,1536]{1,0:T(1,128)S(1)} %broadcast_in_dim.42.gain), custom_call_target="tpu_custom_call" | custom-call | tf_op jit(solution)/shard_map/pallas_call | solution.py:74
  286.4 1.2 fusion.16
  288.1 1.6 copy.47
  289.7 0.7 select_maximum_fusion
  290.4 2.6 convolution_convert_fusion.2
  293.1 1.0 convolution_convert_fusion.3
  294.4 1.4 bitcast_convert_fusion
  295.7 5.1 %reduce-scatter.2.cloned.1.call-done = bf16[3,96,1152]{2,1,0:T(8,128)(2,1)} async-done(((bf16[3,1536,1152]{2,1,0:T(8,128)(2,1)}), bf16[3,96,1152]{2,1,0:T(8,128)(2,1)}) %reduce-scatter.2.cloned.1.call-update) | async-done | bytes 663568 | tf_op jit(solution)/shard_map/reduce_scatter | solution.py:958
  300.8 1.3 copy.50
  302.6 43.6 %shard_map.261 = (f32[4,24,896]{2,1,0:T(8,128)S(1)}, f32[2,4,8,128]{3,2,1,0:T(8,128)S(1)}, bf16[4,80,1152]{2,1,0:T(8,128)(2,1)S(1)}, bf16[2,128,1536]{2,1,0:T(8,128)(2,1)S(1)}) custom-call(bf16[4,4,2,48,896]{4,3,2,1,0:T(8,128)(2,1)S(1)} %pad_maximum_fusion.ga, f32[4,4,8,128]{3,2,1,0:T(8,128)S(1)} %bitcast.88, bf16[4,80,1152]{2,1,0:T(8,128)(2,1)S(1)} %pad.14.ffn, ...), custom_call_target="tpu_custom_call" | custom-call | tf_op jit(solution)/shard_map/pallas_call | solution.py:74
  346.3 0.9 copy-done.15
  347.1 0.6 slice_bitcast_fusion.4
  347.9 0.6 fusion.28
  349.2 0.6 reshape.303
  349.8 1.1 slice.128
  351.3 1.0 squeeze.51
  352.4 1.0 squeeze.50
  353.5 1.0 squeeze.49
  354.5 0.6 maximum_bitcast_fusion
  355.2 0.6 pad_maximum_fusion.5
  355.8 0.9 copy.60
  (124 shorter events, 6.8 us)
Async XLA Ops:
  7.2 1.2 copy-start
  7.2 107.2 %all-gather.2.cloned.1.call-start = ((), (), s32[]{:S(2)}) async-start(), calls=%async_computation.1 | async-start | bytes 11280384 | tf_op jit(solution)/shard_map/all_gather | solution.py:905
  8.5 2.6 copy-start.34
  8.5 3.2 copy-start.32
  8.5 3.2 copy-start.35
  8.5 3.2 copy-start.28
  8.5 3.3 copy-start.29
  8.5 3.3 copy-start.30
  8.6 3.3 copy-start.31
  9.9 1.9 copy-start.8
  9.9 1.9 copy-start.10
  11.0 289.9 %reduce-scatter.2.cloned.1.call-start = ((), (), s32[]{:S(2)}) async-start(), calls=%async_computation.2 | async-start | bytes 11280384 | tf_op jit(solution)/shard_map/reduce_scatter | solution.py:958
  11.9 35.4 %copy-start.36 = (bf16[128]{0:T(256)(128)(2,1)S(1)}, bf16[128]{0:T(256)(128)(2,1)}, u32[]{:S(2)}) copy-start(bf16[128]{0:T(256)(128)(2,1)} %param.21) | copy-start | bytes 772
  11.9 35.4 %copy-start.37 = (bf16[128]{0:T(256)(128)(2,1)S(1)}, bf16[128]{0:T(256)(128)(2,1)}, u32[]{:S(2)}) copy-start(bf16[128]{0:T(256)(128)(2,1)} %param.22) | copy-start | bytes 772
  46.8 1.6 copy-start.7
  48.5 3.9 %copy-start.19 = (bf16[512,1536]{1,0:T(8,128)(2,1)}, bf16[512,1536]{1,0:T(8,128)(2,1)S(1)}, u32[]{:S(2)}) copy-start(bf16[512,1536]{1,0:T(8,128)(2,1)S(1)} %fusion.1) | copy-start | bytes 4718596
  61.5 0.9 copy-start.27
  88.0 3.1 copy-start.2
  90.2 1.0 copy-start.12
  90.2 1.1 copy-start.17
  201.3 1.0 copy-start.26
  201.3 1.5 copy-start.20
  202.8 1.6 copy-start.33
  204.5 2.9 copy-start.3
  204.5 2.9 copy-start.13
  210.4 2.1 copy-start.4
  213.3 2.2 copy-start.5
  256.6 2.7 copy-start.23
  256.6 2.7 copy-start.25
  256.6 2.7 copy-start.6
  256.7 2.7 copy-start.11
  259.4 28.7 %copy-start.21 = (bf16[2,2,128,1536]{3,2,1,0:T(8,128)(2,1)S(1)}, bf16[2,2,128,1536]{3,2,1,0:T(8,128)(2,1)}, u32[]{:S(2)}) copy-start(bf16[2,2,128,1536]{3,2,1,0:T(8,128)(2,1)} %get-tuple-element.40) | copy-start | bytes 4718596
  288.1 2.3 copy-start.24
  290.4 2.7 copy-start.18
  290.4 2.7 copy-start.22
  300.8 1.6 copy-start.9
  300.8 1.8 copy-start.14
  300.8 1.8 copy-start.16
  346.2 0.9 copy-start.15
  353.4 3.3 copy-start.1
Sparse Core Ops, SparseCore 0:
  11.1 103.2 all-gather.1
  201.5 99.3 reduce-scatter.1
where the time goes:
time: 364 us
  Pallas kernels  263 us (72%)
  local copies, waits for them, and re-layouts  28.5 us (8%)
  waiting for transfers between devices  24.7 us (7%)
  matrix products  16.5 us (5%)
  other arithmetic  15.9 us (4%)
  between operations  14.9 us (4%)
    pallas_call x5, Pallas kernels, comm_call(): pl.pallas_call(body, out_shape=outs, in_specs=[VM] * len(args), out_specs...  171 us
    pallas_call x1, Pallas kernels, block(): pl.pallas_call(block_kernel, out_shape=[shape((rows, model), F32), shape(...  86.9 us
    all_gather x1, waiting for transfers between devices, shards(): ffn_weights = lax.all_gather(own_ffn, 'fsdp', axis=1, tiled=True)  19.6 us
    unnamed x78, local copies, waits for them, and re-layouts  10.6 us
  transfers between devices with their start and end apart: 2, of which 2 were waited for; matrix products, arithmetic and copies ran while one was open for 10% of the time, Pallas kernels for 36%

commit v1 on v0

--- a/solution.py
+++ b/solution.py
@@ -87,7 +87,9 @@
     return jax.ShapeDtypeStruct(dims, kind)
 
 
-def opening_kernel(w, tok, dy, w_all, tok2, dy_all, s1, r1, s2, r2, ts, tr, ds, dr, fs, fr):
+def opening_kernel(
+    w, down, tok, dy, w_all, downs, tok2, dy_all, s1, r1, s2, r2, s3, r3, ts, tr, ds, dr, fs, fr
+):
     me = Place()
     y, z, lo, k, t = me.y, me.z, me.lo, me.k, me.t
     rows = w.shape[0] // 2
@@ -140,6 +142,18 @@
                     along(j),
                 )
             )
+    for half, along, here in ((0, me.along_z, z), (1, me.along_y, y)):
+        for j in (2, 1, 3):
+            rest.append(
+                send(
+                    down.at[halves[half]],
+                    downs.at[half, here],
+                    s3.at[half, j - 1],
+                    r3.at[half, j - 1],
+                    along(j),
+                )
+            )
+        downs[half, here] = down[halves[half]]
     w_all[y, z] = w[...]
     tok2[k] = tok[...]
     for h in (0, 1):
@@ -171,13 +185,14 @@
         copy.wait()
 
 
-def opening(w, tok, dy):
+def opening(w, down, tok, dy):
     rows, width = w.shape
     count, model = tok.shape
     return comm_call(
         opening_kernel,
         [
             shape((4, 4, rows, width), BF),
+            shape((2, 4, rows // 2, down.shape[1]), BF),
             shape((2, count, model), BF),
             shape((2, 2, 2, count // 2, model), BF),
         ],
@@ -186,6 +201,8 @@
             DMA((2, 3)),
             DMA((2, 4, 3)),
             DMA((2, 4, 3)),
+            DMA((2, 3)),
+            DMA((2, 3)),
             DMA,
             DMA,
             DMA((2,)),
@@ -196,6 +213,7 @@
         1,
         32,
         w,
+        down,
         tok,
         dy,
     )
@@ -316,91 +334,22 @@
     )(start, q, kv)
 
 
-def attend_back_kernel(heads, start_ref, lse, q, kv, exact, do, dq, dkv, dots, acc):
-    me = Place()
-    rows = q.shape[0]
-    size = q.shape[1] // heads
-    index = me.z * 2 + me.lo
-    first = index * rows
-    start = start_ref[...]
-    for h in range(heads):
-        part = slice(h * size, (h + 1) * size)
-        product = exact[h] * do[:, part].astype(F32).T
-        dots[h : h + 1] = jnp.sum(product, axis=0, keepdims=True)
-    acc[...] = jnp.zeros_like(acc)
-
-    def step(block, _):
-        keys = kv[0, block]
-        values = kv[1, block]
-        seen = visible_pairs(block, first, start, rows)
-        dk = jnp.zeros((KEYS, size), F32)
-        dv = jnp.zeros((KEYS, size), F32)
-        for h in range(heads):
-            q_h = q[:, h * size : (h + 1) * size]
-            do_h = do[:, h * size : (h + 1) * size]
-            s = jnp.where(seen, by_columns(keys, q_h), masked_score)
-            p = jnp.exp(s - lse[h : h + 1])
-            dv = dv + plain(p.astype(BF), do_h)
-            dp = by_columns(values, do_h)
-            ds = (p * (dp - dots[h : h + 1])).astype(BF)
-            dk = dk + plain(ds, q_h)
-            acc[h] = acc[h] + over_rows(keys, ds)
-        dkv[0, block] = dk
-        dkv[1, block] = dv
-        return 0
-
-    lax.fori_loop(0, index + 1, step, 0)
-
-    def blank(block, _):
-        dkv[0, block] = jnp.zeros((KEYS, size), F32)
-        dkv[1, block] = jnp.zeros((KEYS, size), F32)
-        return 0
-
-    lax.fori_loop(index + 1, kv.shape[1], blank, 0)
-    for h in range(heads):
-        dq[:, h * size : (h + 1) * size] = acc[h].T
-
-
-def attend_back(start, lse, q, kv, exact, do, heads):
-    rows, width = q.shape
-    return pl.pallas_call(
-        functools.partial(attend_back_kernel, heads),
-        out_shape=[shape((rows, width), F32), shape(kv.shape, F32)],
-        in_specs=[VM] * 6,
-        out_specs=[VM] * 2,
-        scratch_shapes=[
-            pltpu.VMEM((8, rows), F32),
-            pltpu.VMEM((heads, width // heads, rows), F32),
-        ],
-        compiler_params=pltpu.CompilerParams(vmem_limit_bytes=40 << 20),
-    )(start, lse, q, kv, exact, do)
-
-
-def pair_sum(me, part, r1, s1, r2, sems):
-    k, t = me.k, me.t
-    copy = send(part.at[1 - k], r1, sems.at[0], sems.at[1], me.sibling)
-    copy.wait()
-    s1[...] = (part[k, 1 - t].astype(F32) + r1[1 - t].astype(F32)).astype(BF)
-    copy = send(s1, r2, sems.at[2], sems.at[3], me.in_ring(me.lo, 1 - t))
-    here = part[k, t].astype(F32) + r1[t].astype(F32)
-    copy.wait()
-    return here + r2[...].astype(F32)
-
-
 def norm_back(grad_normed, normed, factor):
     return factor * (grad_normed - normed * jnp.mean(grad_normed * normed, axis=-1, keepdims=True))
 
 
 def block_kernel(
-    part, tok, gain, dy_hbm, w_hbm,
-    x1, dx1, dxl, gnf, ysum, g_hbm,
-    w, dy, dy_t, h2, h2_t, hid, gate_back, up_back, whole, m1, m2, m3, pb, s1, r1, r2, yb, ry,
-    ls, ms, hs, hr, fs, fr, ps, pr, xs, xr, ys, yr, gs, gr, os,
+    part, tok, gain, downs, dy_hbm, w_hbm,
+    x1, dx1, dxl, gnf, ysum, down_sum, g_hbm,
+    w, dy, dy_t, h2, h2_t, hid, gate_back, up_back, whole, m1, m2, m3, pb, s1, r1, r2, yb, ry, pd,
+    bs, br, cs, cr, ls, ms, hs, hr, fs, fr, ps, pr, xs, xr, ys, yr, gs, gr,
 ):
     me = Place()
-    lo, k, t = me.lo, me.k, me.t
+    y, z, lo, k, t = me.y, me.z, me.lo, me.k, me.t
     rows, model = tok.shape
     both = 2 * rows
+    inner = w.shape[-1]
+    offsets = (2, 1, 3)
 
     def chip(i):
         return lax.rem(lo + lax.rem((i + 1) // 2, 2), 2), lax.rem(t + i // 2, 2)
@@ -409,12 +358,32 @@
         return pl.ds(pl.multiple_of(i * both, both), both)
 
     loads = [pltpu.make_async_copy(dy_hbm, dy, ls.at[3])]
-    loads += [pltpu.make_async_copy(w_hbm.at[i], w.at[i], ls.at[i]) for i in range(3)]
+    loads += [pltpu.make_async_copy(w_hbm.at[i], w.at[i], ls.at[i]) for i in range(2)]
     for copy in loads:
         copy.start()
-    greet([me.in_ring(*chip(i)) for i in (1, 2, 3)] + [me.sibling])
+    greet(
+        [me.in_ring(*chip(i)) for i in (1, 2, 3)]
+        + [me.sibling]
+        + [me.along_z(j) for j in (1, 2, 3)]
+        + [me.along_y(j) for j in (1, 2, 3)]
+    )
     cores = send(part.at[1 - k], m1, ms.at[0], ms.at[1], me.sibling)
+    here = w.at[2]
+    downs_out = []
+    for j in offsets:
+        downs_out.append(
+            send(downs.at[0], here.at[y, :, 0], bs.at[0, j - 1], br.at[0, j - 1], me.along_y(j))
+        )
+        downs_out.append(
+            send(downs.at[1], here.at[:, z, 1], bs.at[1, j - 1], br.at[1, j - 1], me.along_z(j))
+        )
+    w[2, y, :, 0] = downs[0]
+    w[2, :, z, 1] = downs[1]
     loads[0].wait()
+
+    def weight(i):
+        return w[i].reshape(model, inner)
+
 
     def turn_dy(i, _):
         lo_i, t_i = chip(i)
@@ -455,7 +424,7 @@
     for i in (1, 2, 3):
         hidden_copy(i).start()
     hidden_share(0).start()
-    for copy in loads[1:]:
+    for copy in loads[1:] + downs_out:
         copy.wait()
 
     def finish(i):
@@ -466,7 +435,7 @@
         def _():
             part_copy(i).start()
 
-        whole[...] = by_columns(hid[i], w[2]).reshape(2, rows, model)
+        whole[...] = by_columns(hid[i], weight(2)).reshape(2, rows, model)
         yb[i] = whole[1 - k].astype(BF)
         ysum[i] = whole[k].astype(BF)
         result_share(i).start()
@@ -485,18 +454,18 @@
         hidden_share(i).wait_recv()
         h = h2[lo_i, t_i].reshape(both, model)
         d = dy[lo_i, t_i].reshape(both, model)
-        gate = plain(h, w[0])
-        up = plain(h, w[1])
+        gate = plain(h, weight(0))
+        up = plain(h, weight(1))
         sigmoid_gate = jax.nn.sigmoid(gate)
         silu_gate = gate * sigmoid_gate
         hid[i] = (silu_gate * up).astype(BF)
-        grad_inner = plain(d, w[2])
+        grad_inner = plain(d, weight(2))
         slope = sigmoid_gate * (1.0 + gate * (1.0 - sigmoid_gate))
         gate_back[i] = (grad_inner * up * slope).astype(BF)
         up_back[i] = (grad_inner * silu_gate).astype(BF)
-        whole[...] = (by_columns(gate_back[i], w[0]) + by_columns(up_back[i], w[1])).reshape(
-            2, rows, model
-        )
+        whole[...] = (
+            by_columns(gate_back[i], weight(0)) + by_columns(up_back[i], weight(1))
+        ).reshape(2, rows, model)
         pb[i] = whole[1 - k].astype(BF)
         s1[i] = whole[k].astype(BF)
         part_share(i).start()
@@ -507,19 +476,34 @@
 
     def gradient(i, left_t, right):
         flat = right.shape[0] * right.shape[1]
-        step_rows = model // 3
+        step_rows = model // 4
 
         def some(m, _):
             r = pl.ds(pl.multiple_of(m * step_rows, step_rows), step_rows)
-            w[i, r] = plain(left_t[r, :], right[...].reshape(flat, right.shape[2])).astype(BF)
+            value = plain(left_t[r, :], right[...].reshape(flat, inner))
+            w[i, m] = value.astype(BF).reshape(w.shape[2:])
             return 0
 
-        lax.fori_loop(0, 3, some, 0)
-        copy = pltpu.make_async_copy(w.at[i], g_hbm.at[i], os.at[i])
+        lax.fori_loop(0, 4, some, 0)
+
+    def gradient_out(i):
+        copy = pltpu.make_async_copy(w.at[i], g_hbm.at[i], ls.at[i])
         copy.start()
         return copy
 
-    outs = [gradient(2, dy_t, hid)]
+    gradient(2, dy_t, hid)
+    downs_back = []
+    for j in offsets:
+        downs_back.append(
+            send(
+                here.at[:, lax.rem(z + j, 4), 0], pd.at[0, j - 1], cs.at[0, j - 1], cr.at[0, j - 1], me.along_z(j)
+            )
+        )
+        downs_back.append(
+            send(
+                here.at[lax.rem(y + j, 4), :, 1], pd.at[1, j - 1], cs.at[1, j - 1], cr.at[1, j - 1], me.along_y(j)
+            )
+        )
 
     grad = s1[0].astype(F32)
     for i in (1, 2, 3):
@@ -535,11 +519,13 @@
     block = dxl.at[k, t]
     across = send(block, block, gs.at[0], gr.at[0], me.in_ring(lo, 1 - t))
     rest = [send(block, block, gs.at[1], gr.at[1], me.sibling)]
-    outs.append(gradient(0, h2_t, gate_back))
+    gradient(0, h2_t, gate_back)
+    outs = [gradient_out(0)]
     across.wait()
     block = dxl.at[k, 1 - t]
     rest.append(send(block, block, gs.at[2], gr.at[2], me.sibling))
-    outs.append(gradient(1, h2_t, up_back))
+    gradient(1, h2_t, up_back)
+    outs.append(gradient_out(1))
     for i in range(4):
         result_share(i).wait()
         ysum[i] = (ysum[i].astype(F32) + ry[i].astype(F32)).astype(BF)
@@ -548,13 +534,23 @@
     for i in (1, 2, 3):
         hidden_copy(i).wait_send()
         part_copy(i).wait_send()
+    for copy in downs_back:
+        copy.wait()
+    for half in (0, 1):
+        mine = w[2, :, z, 0] if half == 0 else w[2, y, :, 1]
+        total = mine.astype(F32)
+        for j in range(3):
+            total = total + pd[half, j].astype(F32)
+        down_sum[half] = total.astype(BF)
     for copy in rest + outs:
         copy.wait()
 
 
-def block(part, tok, gain, dy, w):
+def block(part, tok, gain, downs, dy, w):
     rows, model = tok.shape
     hidden = w.shape[2]
+    half_rows = model // 32
+    w = w.reshape(2, 4, 4, 2, half_rows, hidden)
     any_place = pl.BlockSpec(memory_space=pl.ANY)
     quarter = pltpu.VMEM((4, rows, model), BF)
     inner = pltpu.VMEM((4, 2 * rows, hidden), BF)
@@ -567,12 +563,13 @@
             shape((2, 2, rows, model), BF),
             shape((1, model), F32),
             shape((4, rows, model), BF),
+            shape(downs.shape, BF),
             shape(w.shape, BF),
         ],
-        in_specs=[VM] * 3 + [any_place] * 2,
-        out_specs=[VM] * 5 + [any_place],
+        in_specs=[VM] * 4 + [any_place] * 2,
+        out_specs=[VM] * 6 + [any_place],
         scratch_shapes=[
-            pltpu.VMEM(w.shape, BF),
+            pltpu.VMEM((3,) + w.shape[1:], BF),
             pltpu.VMEM(dy.shape, BF),
             turned,
             pltpu.VMEM(dy.shape, BF),
@@ -590,6 +587,11 @@
             pltpu.VMEM((3, rows, model), BF),
             quarter,
             quarter,
+            pltpu.VMEM((2, 3) + downs.shape[1:], BF),
+            DMA((2, 3)),
+            DMA((2, 3)),
+            DMA((2, 3)),
+            DMA((2, 3)),
             DMA((4,)),
             DMA((4,)),
             DMA((3,)),
@@ -604,255 +606,420 @@
             DMA((4,)),
             DMA((3,)),
             DMA((3,)),
-            DMA((3,)),
         ],
         compiler_params=pltpu.CompilerParams(
             collective_id=3, has_side_effects=True, vmem_limit_bytes=62 << 20
         ),
-    )(part, tok, gain, dy, w)
-
-
-def keys_back_kernel(dkv, mine, r1, s1, r2, as1, ar1, as2, ar2):
-    me = Place()
-    k = me.k
-    own = me.z * 2 + me.lo
-    steps = [(dz, dl) for dz in (2, 1, 3, 0) for dl in (0, 1) if dz or dl]
-
-    def block(dz, dl):
-        return lax.rem(me.z + dz, 4) * 2 + lax.rem(me.lo + dl, 2)
-
-    def partner(dz, dl):
-        return {
-            "fsdp": me.y * 4 + lax.rem(me.z + dz, 4),
-            "ctx": lax.rem(me.lo + dl, 2) * 2 + k,
-        }
-
-    greet([partner(dz, dl) for dz, dl in steps] + [me.sibling])
-    cores = send(dkv.at[1 - k], r1, as1, ar1, me.sibling)
-    cores.wait()
-    s1[...] = (dkv[k] + r1[...]).astype(BF)
-    copies = [
-        send(s1.at[block(dz, dl)], r2.at[i], as2.at[i], ar2.at[i], partner(dz, dl))
-        for i, (dz, dl) in enumerate(steps)
-    ]
-    total = s1[own].astype(F32)
-    for i, copy in enumerate(copies):
-        copy.wait()
-        total = total + r2[i].astype(F32)
-    mine[...] = total
-
-
-def return_keys(dkv):
-    _, count, rows, width = dkv.shape
-    return comm_call(
-        keys_back_kernel,
-        [shape((rows, width), F32)],
-        [
-            pltpu.VMEM((count, rows, width), F32),
-            pltpu.VMEM((count, rows, width), BF),
-            pltpu.VMEM((count - 1, rows, width), BF),
-            DMA,
-            DMA,
-            DMA((count - 1,)),
-            DMA((count - 1,)),
-        ],
-        5,
-        24,
-        dkv,
-    )[0]
-
-
-def tokens_kernel(part, tok, dx1, gain, grad, gna, r1, s1, r2, sems, gs, gr):
-    me = Place()
-    t = me.t
-    greet([me.in_ring(me.lo, 1 - t), me.sibling])
-    dh1 = pair_sum(me, part, r1, s1, r2, sems)
-    x = tok[...].astype(F32)
-    factor = lax.rsqrt(jnp.mean(x * x, axis=-1, keepdims=True) + epsilon)
-    normed = x * factor
-    gna[...] = jnp.sum(dh1 * normed, axis=0, keepdims=True)
-    grad[t] = (dx1[...] + norm_back(dh1 * gain[...], normed, factor)).astype(BF)
-    block = grad.at[t]
-    send(block, block, gs, gr, me.in_ring(me.lo, 1 - t)).wait()
-
-
-def tokens_back(part, tok, dx1, gain):
-    rows, model = tok.shape
-    return comm_call(
-        tokens_kernel,
-        [shape((2, rows, model), BF), shape((1, model), F32)],
-        [
-            pltpu.VMEM((2, rows, model), BF),
-            pltpu.VMEM((rows, model), BF),
-            pltpu.VMEM((rows, model), BF),
-            DMA((4,)),
-            DMA,
-            DMA,
-        ],
-        6,
-        24,
-        part,
-        tok,
-        dx1,
-        gain,
-    )
-
-
-def closing_kernel(
-    ga, ext, ffn, ysum, x1, a_all, ext_all, ffn_all, out,
-    r1, sm, r2, fin, e1, esm, e2, yr2,
-    as1, ar1, as2, ar2, as3, ar3, es, er, fs, fr, xs, xr, ys, yr,
+    )(part, tok, gain, downs, dy, w)
+
+
+def turned(values, cosines, sines):
+    return values * cosines - pltpu.roll(values, values.shape[-1] // 2, 1) * sines
+
+
+def rear_kernel(
+    heads,
+    g_hbm, down_sum, dxl, attn, q, kv, exact, lse, start_ref, ob, h1, cosines, sines, ysum, x1, dx1, tok, gain, gnf,
+    a_all, ext_all, ffn_all, down_all, out, grad,
+    do, dots, acc, keep, give, arrived, sums, landed, back, part, m1, m2, m3, left_t, ga,
+    own, p1, p2, q1, sm, q2, fin, fin_d, wide, narrow, e0, e1, es, e2, y2,
+    ls, d1, d2, d3, d4, ms, fs1, fr1, fs2, fr2, as1, ar1, as2, ar2, as3, ar3, xs, xr, ss, sr, ts, tr, us, ur, ys, yr,
+    gs, gr,
 ):
     me = Place()
     y, z, lo, k, t = me.y, me.z, me.lo, me.k, me.t
     c = lo * 2 + k
-
-    def in_ctx(j):
-        return {"ctx": lax.rem(c + j, 4)}
-
-    ring = [(dt, dc) for dt in (0, 1) for dc in range(4) if dt or dc]
+    index = z * 2 + lo
+    rows, width = q.shape
+    size = width // heads
+    slice_rows, model = tok.shape
+    rowed = width + size
+    offsets = (2, 1, 3)
 
     def in_x(dt, dc):
         return {"ctx": lax.rem(c + dc, 4), "tp": lax.rem(t + dt, 2)}
+
+    def owner(b):
+        return {"fsdp": y * 4 + b // 2, "ctx": lax.rem(b, 2) * 2 + k}
+
+    ring = [(dt, dc) for dt in (0, 1) for dc in range(4) if dt or dc]
+
+    def first_hop(w, half, j):
+        if half == 0:
+            source, device = g_hbm.at[w, :, lax.rem(z + j, 4), 0], me.along_z(j)
+        else:
+            source, device = g_hbm.at[w, lax.rem(y + j, 4), :, 1], me.along_y(j)
+        return describe(
+            source, p1.at[w, half, j - 1], fs1.at[w, half, j - 1], fr1.at[w, half, j - 1], device
+        )
+
+    def second_hop(w, half, j):
+        if half == 0:
+            source, device = own.at[w, 0, lax.rem(y + j, 4)], me.along_y(j)
+        else:
+            source, device = own.at[w, 1, lax.rem(z + j, 4)], me.along_z(j)
+        return describe(
+            source, p2.at[w, half, j - 1], fs2.at[w, half, j - 1], fr2.at[w, half, j - 1], device
+        )
+
+    def own_load(w, half):
+        source = g_hbm.at[w, :, z, 0] if half == 0 else g_hbm.at[w, y, :, 1]
+        return pltpu.make_async_copy(source, own.at[w, half], ls.at[w, half])
+
+    def start_hop(half, *span):
+        def some(w, _):
+            for j in offsets:
+                first_hop(w, half, j).start()
+            own_load(w, half).start()
+            return 0
+
+        lax.fori_loop(*span, some, 0)
 
     greet(
         [me.along_z(j) for j in (1, 2, 3)]
         + [me.along_y(j) for j in (1, 2, 3)]
         + [in_x(dt, dc) for dt, dc in ring]
-    )
+        + [{"fsdp": y * 4 + lax.rem(z + j, 4), "ctx": (1 - lo) * 2 + k} for j in (1, 2, 3)]
+    )
+    own[2] = down_sum[...]
+    for half in (0, 1):
+        for j in offsets:
+            second_hop(2, half, j).start()
+    start_hop(1, 0, 2)
+    start_hop(0, 0, 1)
+    near = [(1 - lo, t), (1 - lo, 1 - t), (lo, 1 - t)]
+    results = [
+        send(ysum.at[i + 1], y2.at[i], ys.at[i], yr.at[i], me.in_ring(*near[i])) for i in range(3)
+    ]
+
+    do[...] = plain(dxl[...], attn[:, rowed:]).astype(BF)
+    for h in range(heads):
+        product = exact[h] * do[:, h * size : (h + 1) * size].astype(F32).T
+        dots[h : h + 1] = jnp.sum(product, axis=0, keepdims=True)
+    acc[...] = jnp.zeros_like(acc)
+    start = start_ref[...]
+    first = index * rows
+
+    def core_share(b):
+        return describe(give.at[b], arrived.at[b], d1.at[b], d2.at[b], me.sibling)
+
+    def home(b):
+        return describe(sums.at[b], landed.at[index], d3.at[b], d4.at[index], owner(b))
+
+    def step(b, _):
+        keys = kv[0, b]
+        values = kv[1, b]
+        seen = visible_pairs(b, first, start, rows)
+        dk = jnp.zeros((KEYS, size), F32)
+        dv = jnp.zeros((KEYS, size), F32)
+        for h in range(heads):
+            q_h = q[:, h * size : (h + 1) * size]
+            do_h = do[:, h * size : (h + 1) * size]
+            s = jnp.where(seen, by_columns(keys, q_h), masked_score)
+            p = jnp.exp(s - lse[h : h + 1])
+            dv = dv + plain(p.astype(BF), do_h)
+            dp = by_columns(values, do_h)
+            ds = (p * (dp - dots[h : h + 1])).astype(BF)
+            dk = dk + plain(ds, q_h)
+            acc[h] = acc[h] + over_rows(keys, ds)
+        keep[b] = jnp.where(k == 0, dk, dv)
+        give[b] = jnp.where(k == 0, dv, dk)
+        core_share(b).start()
+
+        @pl.when(b > 0)
+        def _():
+            core_share(b - 1).wait_recv()
+            sums[b - 1] = (keep[b - 1] + arrived[b - 1]).astype(BF)
+            home(b - 1).start()
+
+        return 0
+
+    lax.fori_loop(0, index + 1, step, 0)
+    start_hop(0, 1, 2)
+
+    scale = 1.0 / math.sqrt(size)
+    for h in range(heads):
+        dq = turned(acc[h].T * scale, cosines[...], -sines[...])
+        e0[2:3, h * size : (h + 1) * size] = jnp.sum(dq, axis=0, keepdims=True)
+        back[:, h * size : (h + 1) * size] = dq.astype(BF)
+    left_t[...] = dxl[...].T
+    blocks = ga.shape[:4]
+
+    def spread(value):
+        return value.astype(BF).reshape(blocks + (value.shape[1],))
+
+    ga[:, :, :, :, rowed:] = spread(plain(left_t[...], ob[...]))
+    left_t[...] = h1[...].T
+    ga[:, :, :, :, :width] = spread(plain(left_t[...], back[:, :width]))
+
+    core_share(index).wait_recv()
+    dkv = keep[index] + arrived[index]
+    keep[index] = dkv
+    for b in range(1, 8):
+
+        @pl.when(b > index)
+        def _():
+            describe(sums.at[0], landed.at[b], d3.at[0], d4.at[b], owner(0)).wait_recv()
+            keep[index] = keep[index] + landed[b].astype(F32)
+
+    is_key = k == 0
+    dkv = turned(
+        keep[index], jnp.where(is_key, cosines[...], 1.0), jnp.where(is_key, -sines[...], 0.0)
+    )
+    e0[2:3, width:rowed] = jnp.sum(dkv, axis=0, keepdims=True)
+    back[:, width:] = dkv.astype(BF)
+    part[...] = (
+        by_columns(back[...], attn[:, :rowed]).astype(BF).reshape(2, 2, slice_rows, model)
+    )
+    cores = send(part.at[1 - k], m1, ms.at[0], ms.at[1], me.sibling)
+    ga[:, :, :, :, width:rowed] = spread(plain(left_t[...], back[:, width:]))
+
+    large = []
+    for j in offsets:
+        large.append(
+            send(
+                ga.at[:, lax.rem(z + j, 4), 0], q1.at[0, j - 1], as1.at[0, j - 1], ar1.at[0, j - 1], me.along_z(j)
+            )
+        )
+        large.append(
+            send(
+                ga.at[lax.rem(y + j, 4), :, 1], q1.at[1, j - 1], as1.at[1, j - 1], ar1.at[1, j - 1], me.along_y(j)
+            )
+        )
+
+    cores.wait()
+    m2[...] = (part[k, 1 - t].astype(F32) + m1[1 - t].astype(F32)).astype(BF)
+    across = send(m2, m3, ms.at[2], ms.at[3], me.in_ring(lo, 1 - t))
+    x = tok[...].astype(F32)
+    factor = lax.rsqrt(jnp.mean(x * x, axis=-1, keepdims=True) + epsilon)
+    normed = x * factor
+    dh1 = part[k, t].astype(F32) + m1[t].astype(F32)
+    across.wait()
+    dh1 = dh1 + m3[...].astype(F32)
+    e0[0:1] = jnp.sum(dh1 * normed, axis=0, keepdims=True)
+    e0[1:2] = gnf[...]
+    e0[2:3, rowed:] = jnp.zeros((1, model - rowed), F32)
+    e0[3:] = jnp.zeros((5, model), F32)
     small = [
-        send(ext.at[:, lax.rem(z + j, 4)], e1.at[j - 1], es.at[0, j - 1], er.at[0, j - 1], me.along_z(j))
+        send(e0, e1.at[j - 1], ss.at[0, j - 1], sr.at[0, j - 1], me.along_z(j)) for j in offsets
+    ]
+    grad[t] = (dx1[...] + norm_back(dh1 * gain[...], normed, factor)).astype(BF)
+    mine = grad.at[t]
+    rest = [send(mine, mine, gs.at[0], gr.at[0], me.in_ring(lo, 1 - t))]
+
+    quarter = sm.shape[2] // 2
+
+    def summed(w, half):
+        for j in offsets:
+            second_hop(w, half, j).wait()
+        here = own[w, 0, y] if half == 0 else own[w, 1, z]
+        total = here.astype(F32)
+        for j in range(3):
+            total = total + p2[w, half, j].astype(F32)
+        return total
+
+    for half in (0, 1):
+        total = summed(2, half)
+        fin_d[2 * half] = total[:quarter]
+        fin_d[2 * half + 1] = total[quarter:]
+    down_all[c] = fin_d[c]
+    rest += [
+        send(fin_d.at[lax.rem(c + j, 4)], down_all.at[c], us.at[j - 1], ur.at[j - 1], in_x(0, j))
         for j in (2, 1, 3)
     ]
-    large = [
-        [
-            send(
-                ga.at[:, lax.rem(z + j, 4), 0], r1.at[0, j - 1], as1.at[0, j - 1], ar1.at[0, j - 1], me.along_z(j)
-            )
-            for j in (2, 1, 3)
-        ],
-        [
-            send(
-                ga.at[lax.rem(y + j, 4), :, 1], r1.at[1, j - 1], as1.at[1, j - 1], ar1.at[1, j - 1], me.along_y(j)
-            )
-            for j in (2, 1, 3)
-        ],
-    ]
-    rest = [
-        send(ffn.at[lax.rem(c + j, 4)], ffn_all.at[c], fs.at[j - 1], fr.at[j - 1], in_ctx(j))
-        for j in (1, 2, 3)
-    ]
-    ffn_all[c] = ffn[c]
-    near = [(1 - lo, t), (1 - lo, 1 - t), (lo, 1 - t)]
-    results = [
-        send(ysum.at[i + 1], yr2.at[i], ys.at[i], yr.at[i], me.in_ring(*near[i])) for i in range(3)
-    ]
+
+    result = x1[...] + ysum[0].astype(F32)
+    for i in range(3):
+        results[i].wait()
+        result = result + y2[i].astype(F32)
+    out[t] = result.astype(BF)
+    mine = out.at[t]
+    rest.append(send(mine, mine, gs.at[1], gr.at[1], me.in_ring(lo, 1 - t)))
+
     for copy in small:
         copy.wait()
-    esm[...] = (ext[:, z] + e1[0]) + (e1[1] + e1[2])
+    es[...] = (e0[...] + e1[0]) + (e1[1] + e1[2])
     small = [
-        send(esm.at[lax.rem(y + j, 4)], e2.at[j - 1], es.at[1, j - 1], er.at[1, j - 1], me.along_y(j))
-        for j in (2, 1, 3)
+        send(es, e2.at[j - 1], ss.at[1, j - 1], sr.at[1, j - 1], me.along_y(j)) for j in offsets
     ]
+
+    def first_sum(w, _):
+        for half in (0, 1):
+            own_load(w, half).wait()
+            for j in offsets:
+                first_hop(w, half, j).wait()
+            total = own[w, half].astype(F32)
+            for j in range(3):
+                total = total + p1[w, half, j].astype(F32)
+            own[w, half] = total.astype(BF)
+            for j in offsets:
+                second_hop(w, half, j).start()
+        return 0
+
+    lax.fori_loop(0, 2, first_sum, 0)
+
     for copy in small:
         copy.wait()
-    ext_all[t, c] = (esm[y] + e2[0]) + (e2[1] + e2[2])
-    block = ext_all.at[t, c]
+    ext_all[t, c] = (es[...] + e2[0]) + (e2[1] + e2[2])
+    mine = ext_all.at[t, c]
     rest += [
-        send(block, block, xs.at[i], xr.at[i], in_x(dt, dc)) for i, (dt, dc) in enumerate(ring)
+        send(mine, mine, xs.at[i], xr.at[i], in_x(dt, dc)) for i, (dt, dc) in enumerate(ring)
     ]
+    for copy in large:
+        copy.wait()
     for half in (0, 1):
-        for copy in large[half]:
-            copy.wait()
         here = ga[:, z, 0] if half == 0 else ga[y, :, 1]
         total = here.astype(F32)
         for j in range(3):
-            total = total + r1[half, j].astype(F32)
+            total = total + q1[half, j].astype(F32)
         sm[half] = total.astype(BF)
-    last = [
-        [
+    last = []
+    for j in offsets:
+        last.append(
             send(
-                sm.at[0, lax.rem(y + j, 4)], r2.at[0, j - 1], as2.at[0, j - 1], ar2.at[0, j - 1], me.along_y(j)
+                sm.at[0, lax.rem(y + j, 4)], q2.at[0, j - 1], as2.at[0, j - 1], ar2.at[0, j - 1], me.along_y(j)
             )
-            for j in (2, 1, 3)
-        ],
-        [
+        )
+        last.append(
             send(
-                sm.at[1, lax.rem(z + j, 4)], r2.at[1, j - 1], as2.at[1, j - 1], ar2.at[1, j - 1], me.along_z(j)
+                sm.at[1, lax.rem(z + j, 4)], q2.at[1, j - 1], as2.at[1, j - 1], ar2.at[1, j - 1], me.along_z(j)
             )
-            for j in (2, 1, 3)
-        ],
+        )
+
+    def second_sum(w, _):
+        for half in (0, 1):
+            total = summed(w, half)
+            place = pl.ds(pl.multiple_of(w * quarter, 8), quarter)
+            wide[2 * half, place] = total[:quarter]
+            wide[2 * half + 1, place] = total[quarter:]
+        return 0
+
+    lax.fori_loop(0, 2, second_sum, 0)
+    narrow[...] = wide[...].astype(BF)
+    ffn_all[c] = narrow[c]
+    rest += [
+        send(narrow.at[lax.rem(c + j, 4)], ffn_all.at[c], ts.at[j - 1], tr.at[j - 1], in_x(0, j))
+        for j in (2, 1, 3)
     ]
-    result = x1[...] + ysum[0].astype(F32)
-    for i in range(3):
-        results[i].wait()
-        result = result + yr2[i].astype(F32)
-    out[t] = result.astype(BF)
-    block = out.at[t]
-    rest.append(send(block, block, ys.at[3], yr.at[3], me.in_ring(lo, 1 - t)))
-    half_rows = sm.shape[2]
-    quarter = half_rows // 2
+    for copy in last:
+        copy.wait()
     for half in (0, 1):
-        for copy in last[half]:
-            copy.wait()
         here = sm[0, y] if half == 0 else sm[1, z]
         total = here.astype(F32)
         for j in range(3):
-            total = total + r2[half, j].astype(F32)
+            total = total + q2[half, j].astype(F32)
         fin[2 * half] = total[:quarter]
         fin[2 * half + 1] = total[quarter:]
     a_all[c] = fin[c]
     rest += [
-        send(fin.at[lax.rem(c + j, 4)], a_all.at[c], as3.at[j - 1], ar3.at[j - 1], in_ctx(j))
-        for j in (1, 2, 3)
+        send(fin.at[lax.rem(c + j, 4)], a_all.at[c], as3.at[j - 1], ar3.at[j - 1], in_x(0, j))
+        for j in (2, 1, 3)
     ]
+
+    def sent(b, _):
+        core_share(b).wait_send()
+
+        @pl.when(b < index)
+        def _():
+            home(b).wait_send()
+
+        return 0
+
+    lax.fori_loop(0, index + 1, sent, 0)
     for copy in rest:
         copy.wait()
 
 
-def closing(ga, ext, ffn, ysum, x1):
-    _, _, _, rows, width = ga.shape
-    slice_rows, model = x1.shape
-    return comm_call(
-        closing_kernel,
-        [
-            shape((4, rows // 2, width), F32),
-            shape((2, 4) + ext.shape[2:], F32),
-            shape(ffn.shape, BF),
-            shape((2, slice_rows, model), BF),
-        ],
-        [
-            pltpu.VMEM((2, 3, 4, rows, width), BF),
-            pltpu.VMEM((2, 4, rows, width), BF),
-            pltpu.VMEM((2, 3, rows, width), BF),
-            pltpu.VMEM((4, rows // 2, width), F32),
-            pltpu.VMEM((3, 4) + ext.shape[2:], F32),
-            pltpu.VMEM((4,) + ext.shape[2:], F32),
-            pltpu.VMEM((3,) + ext.shape[2:], F32),
+def rear(heads, g, down_sum, dxl, attn, q, kv, exact, lse, start, ob, h1, cosines, sines, ysum, x1, dx1, tok, gain, gnf):
+    rows, width = q.shape
+    size = width // heads
+    slice_rows, model = tok.shape
+    hidden = g.shape[-1]
+    total = attn.shape[1]
+    half_rows = model // 32
+    quarter = half_rows // 2
+    packed = 2 * quarter
+    shared = pltpu.VMEM(kv.shape[1:], F32)
+    shared_low = pltpu.VMEM(kv.shape[1:], BF)
+    slab = pltpu.VMEM((slice_rows, model), BF)
+    args = (down_sum, dxl, attn, q, kv, exact, lse, start, ob, h1, cosines, sines, ysum, x1, dx1, tok, gain, gnf)
+    outs = [
+        shape((4, quarter, total), F32),
+        shape((2, 4, 8, model), F32),
+        shape((4, packed, hidden), BF),
+        shape((4, quarter, hidden), F32),
+        shape((2, slice_rows, model), BF),
+        shape((2, slice_rows, model), BF),
+    ]
+    return pl.pallas_call(
+        functools.partial(rear_kernel, heads),
+        out_shape=outs,
+        in_specs=[pl.BlockSpec(memory_space=pl.ANY)] + [VM] * len(args),
+        out_specs=[VM] * len(outs),
+        scratch_shapes=[
+            pltpu.VMEM((rows, width), BF),
+            pltpu.VMEM((8, rows), F32),
+            pltpu.VMEM((heads, size, rows), F32),
+            shared,
+            shared,
+            shared,
+            shared_low,
+            shared_low,
+            pltpu.VMEM((rows, width + size), BF),
+            pltpu.VMEM((2, 2, slice_rows, model), BF),
+            pltpu.VMEM((2, slice_rows, model), BF),
+            slab,
+            slab,
+            pltpu.VMEM((model, rows), BF),
+            pltpu.VMEM((4, 4, 2, half_rows, total), BF),
+            pltpu.VMEM((3, 2, 4, half_rows, hidden), BF),
+            pltpu.VMEM((2, 2, 3, 4, half_rows, hidden), BF),
+            pltpu.VMEM((3, 2, 3, half_rows, hidden), BF),
+            pltpu.VMEM((2, 3, 4, half_rows, total), BF),
+            pltpu.VMEM((2, 4, half_rows, total), BF),
+            pltpu.VMEM((2, 3, half_rows, total), BF),
+            pltpu.VMEM((4, quarter, total), F32),
+            pltpu.VMEM((4, quarter, hidden), F32),
+            pltpu.VMEM((4, packed, hidden), F32),
+            pltpu.VMEM((4, packed, hidden), BF),
+            pltpu.VMEM((8, model), F32),
+            pltpu.VMEM((3, 8, model), F32),
+            pltpu.VMEM((8, model), F32),
+            pltpu.VMEM((3, 8, model), F32),
             pltpu.VMEM((3, slice_rows, model), BF),
-            DMA((2, 3)),
-            DMA((2, 3)),
-            DMA((2, 3)),
-            DMA((2, 3)),
-            DMA((3,)),
-            DMA((3,)),
+            DMA((2, 2)),
+            DMA((8,)),
+            DMA((8,)),
+            DMA((8,)),
+            DMA((8,)),
+            DMA((4,)),
+            DMA((2, 2, 3)),
+            DMA((2, 2, 3)),
+            DMA((3, 2, 3)),
+            DMA((3, 2, 3)),
+            DMA((2, 3)),
+            DMA((2, 3)),
             DMA((2, 3)),
             DMA((2, 3)),
             DMA((3,)),
             DMA((3,)),
             DMA((7,)),
             DMA((7,)),
-            DMA((4,)),
-            DMA((4,)),
+            DMA((2, 3)),
+            DMA((2, 3)),
+            DMA((3,)),
+            DMA((3,)),
+            DMA((3,)),
+            DMA((3,)),
+            DMA((3,)),
+            DMA((3,)),
+            DMA((2,)),
+            DMA((2,)),
         ],
-        7,
-        40,
-        ga,
-        ext,
-        ffn,
-        ysum,
-        x1,
-    )
+        compiler_params=pltpu.CompilerParams(
+            collective_id=7, has_side_effects=True, vmem_limit_bytes=62 << 20
+        ),
+    )(g, *args)
 
 
 def rotate(values_in, cosine, sine):
@@ -898,11 +1065,12 @@
     def hidden_slice(w, axis):
         return lax.dynamic_slice_in_dim(w, c * hidden, hidden, axis)
 
-    own_ffn = jnp.stack(
-        [hidden_slice(w_gate, 1), hidden_slice(w_up, 1), hidden_slice(w_down, 0).T]
-    )
-    own_ffn = jnp.pad(own_ffn, ((0, 0), (0, 0), (0, padded - hidden)))
+    def widened(w):
+        return jnp.pad(w, ((0, 0), (0, padded - hidden)))
+
+    own_ffn = jnp.stack([widened(hidden_slice(w_gate, 1)), widened(hidden_slice(w_up, 1))])
     ffn_weights = lax.all_gather(own_ffn, "fsdp", axis=1, tiled=True)
+    own_down = widened(hidden_slice(w_down, 0).T)
 
     own_attn = jnp.concatenate(
         [
@@ -912,7 +1080,7 @@
         ],
         axis=1,
     )
-    attn_all, tok2, dy_all = opening(own_attn, tokens, cotangent)
+    attn_all, downs, tok2, dy_all = opening(own_attn, own_down, tokens, cotangent)
     attn_all = attn_all.reshape(model, own_width + query_width)
     in_all, out_all = attn_all[:, :own_width], attn_all[:, own_width:]
     own_tokens = lax.dynamic_slice_in_dim(tokens, t * slice_rows, slice_rows, 0)
@@ -952,58 +1120,44 @@
     kv = share_keys(rotate(linear[:, query_width:], kv_cosine, kv_sine).astype(BF))
     ob, exact, lse = attend(starts, q, kv, heads)
     part = by_columns(ob, out_all).astype(BF).reshape(2, 2, slice_rows, model)
-    x1, dx1, dxl, grad_norm_two, ysum, ffn_grads = block(
-        part, own_tokens, gain_ffn[None], dy_all, ffn_weights
-    )
-    ffn_grads = lax.psum_scatter(ffn_grads, "fsdp", scatter_dimension=1, tiled=True)
-    dxl = dxl.reshape(rows, model)
-
-    grad_out = over_rows(dxl, ob)
-    do = plain(dxl, out_all).astype(BF)
-    dq, dkv = attend_back(starts, lse, q, kv, exact, do, heads)
-    dkv = return_keys(dkv)
-    dq = rotate(dq.reshape(rows, heads, size) * query_scale, cosine, -sine).reshape(
-        rows, query_width
-    )
-    dkv = rotate(dkv, kv_cosine, -kv_sine)
-    back = jnp.concatenate([dq, dkv], axis=1)
-    grad_bias = jnp.sum(back, axis=0)
-    back = back.astype(BF)
-    grad_in = over_rows(h1, back)
-    part_one = by_columns(back, in_all).astype(BF).reshape(2, 2, slice_rows, model)
-    grad_tokens, grad_norm_one = tokens_back(part_one, own_tokens, dx1, gain_attn[None])
-
-    grad_attn = jnp.concatenate([grad_in, grad_out], axis=1).astype(BF)
-    owner_rows = shard_rows // 4
-    ext = jnp.concatenate(
-        [
-            grad_norm_one.reshape(16, 4, owner_rows),
-            grad_norm_two.reshape(16, 4, owner_rows),
-            grad_bias.reshape(heads + 1, 16, 4, 2).transpose(1, 2, 0, 3).reshape(16, 4, -1),
-        ],
-        axis=2,
-    )
-    ext = jnp.pad(ext, ((0, 0), (0, 4), (0, 128 - ext.shape[2]))).reshape(4, 4, 8, 128)
-    ffn_blocks = ffn_grads.reshape(3, 4, owner_rows, padded).transpose(1, 0, 2, 3)
-    ffn_blocks = jnp.pad(
-        ffn_blocks.reshape(4, 3 * owner_rows, padded), ((0, 0), (0, -3 * owner_rows % 16), (0, 0))
-    )
-    a_all, ext_all, ffn_all, output = closing(
-        grad_attn.reshape(4, 4, 2, shard_rows // 2, own_width + query_width),
-        ext,
-        ffn_blocks,
+    x1, dx1, dxl, grad_norm_two, ysum, down_sum, ffn_grads = block(
+        part, own_tokens, gain_ffn[None], downs, dy_all, ffn_weights
+    )
+    a_all, ext_all, ffn_all, down_all, output, grad_tokens = rear(
+        heads,
+        ffn_grads,
+        down_sum,
+        dxl.reshape(rows, model),
+        attn_all,
+        q,
+        kv,
+        exact,
+        lse,
+        starts,
+        ob,
+        h1,
+        jnp.concatenate([cosine[:, 0], cosine[:, 0]], axis=1),
+        jnp.concatenate([sine[:, 0], -sine[:, 0]], axis=1),
         ysum,
         x1,
-    )
+        dx1,
+        own_tokens,
+        gain_attn[None],
+        grad_norm_two,
+    )
+    owner_rows = shard_rows // 4
     a_all = a_all[:2] + a_all[2:]
-    ffn_all = ffn_all[:, : 3 * owner_rows, :hidden].astype(F32)
-    ffn_all = ffn_all.reshape(4, 3, owner_rows, hidden).transpose(1, 2, 0, 3)
-    ffn_all = ffn_all.reshape(3, owner_rows, 4 * hidden)
-    own_ext = lax.dynamic_index_in_dim(ext_all, c, 2, keepdims=False)
-    norms = jnp.sum(own_ext.reshape(8, 128), axis=0)
-    biases = lax.dynamic_index_in_dim(own_ext, t, 0, keepdims=False)
-    biases = biases[:2] + biases[2:]
-    biases = biases[:, 2 * owner_rows : 2 * owner_rows + 2 * (heads + 1)].reshape(2, heads + 1, 2)
+
+    def side_by_side(pieces):
+        return jnp.concatenate([pieces[i, :, :hidden].astype(F32) for i in range(4)], axis=1)
+
+    owner = f * 4 + c
+    norms = lax.dynamic_slice_in_dim(
+        jnp.sum(ext_all[:, :, :2].reshape(8, 2, model), axis=0), owner * owner_rows, owner_rows, 1
+    )
+    biases = lax.dynamic_index_in_dim(ext_all[:, :, 2, :own_width], t, 0, keepdims=False)
+    biases = (biases[:2] + biases[2:]).reshape(2, heads + 1, size)
+    biases = lax.dynamic_slice_in_dim(biases, owner * 2, 2, 2)
     return (
         output.reshape(count, model),
         grad_tokens.reshape(count, model).astype(F32),
@@ -1014,11 +1168,11 @@
         biases[0, heads:],
         biases[1, heads:],
         jnp.concatenate([a_all[0, :, own_width:], a_all[1, :, own_width:]], axis=1).T,
-        norms[:owner_rows],
-        norms[owner_rows : 2 * owner_rows],
-        ffn_all[0],
-        ffn_all[1],
-        ffn_all[2].T,
+        norms[0],
+        norms[1],
+        side_by_side(ffn_all[:, :owner_rows]),
+        side_by_side(ffn_all[:, owner_rows:]),
+        side_by_side(down_all).T,
     )
 
 

time: 364 us -> 342 us (0.940)
  waiting for transfers between devices: 24.7 us -> 0.02 us
  Pallas kernels: 263 us -> 278 us
  matrix products: 16.5 us -> 4.4 us
    pallas_call x5 -> x2, Pallas kernels: 171 us -> 63.5 us  [comm_call(): pl.pallas_call(body, out_shape=outs, in_specs=[VM] * len(args), out_specs...]
    pallas_call x1, Pallas kernels: 3.01 us -> 108 us  [rear(): pl.pallas_call(functools.partial(rear_kernel, heads), out_shape=outs, in_...]
    all_gather x1, waiting for transfers between devices: 19.6 us -> 0.01 us  [shards(): ffn_weights = lax.all_gather(own_ffn, 'fsdp', axis=1, tiled=True)]
    pallas_call x1, Pallas kernels: 86.9 us -> 104 us  [block(): pl.pallas_call(block_kernel, out_shape=[shape((rows, model), F32), shape(...]
    dot_general x2 -> x1, matrix products: 6.79 us -> 0.97 us  [plain(): lax.dot_general(a, b, (((1,), (0,)), ((), ())), preferred_element_type=F32)]
    reduce_scatter x1 -> x0, waiting for transfers between devices: 5.07 us -> none  [shards(): lax.psum_scatter(ffn_grads, 'fsdp', scatter_dimension=1, tiled=True)]
    unnamed x78 -> x60, local copies, waits for them, and re-layouts: 10.6 us -> 13 us
  transfers between devices with their start and end apart: 2 -> 1, of which waited for: 2 -> 0; matrix products, arithmetic and copies ran while one was open for 10% -> 6% of each run, Pallas kernels for 36% -> 19%
where the time goes in v1:
time: 342 us; the launch traced here: 341 us
  Pallas kernels  278 us (81%)
  local copies, waits for them, and re-layouts  25.7 us (8%)
  other arithmetic  18.6 us (5%)
  between operations  14.6 us (4%)
  matrix products  4.4 us (1%)
    pallas_call x1, Pallas kernels, rear(): pl.pallas_call(functools.partial(rear_kernel, heads), out_shape=outs, in_...  108 us
    pallas_call x1, Pallas kernels, block(): pl.pallas_call(block_kernel, out_shape=[shape((rows, model), F32), shape(...  104 us
    pallas_call x2, Pallas kernels, comm_call(): pl.pallas_call(body, out_shape=outs, in_specs=[VM] * len(args), out_specs...  63.5 us
    unnamed x60, local copies, waits for them, and re-layouts  13 us
  transfers between devices with their start and end apart: 1, of which 0 were waited for; matrix products, arithmetic and copies ran while one was open for 6% of the time, Pallas kernels for 19%

profile of v1, /device:TPU:1, one launch (start us, length us, event | category | flops | bytes accessed | tf_op | source)
XLA Modules:
  0.0 341.2 jit_solution(3839192810373781503)
XLA Ops:
  7.3 1.3 constant_dynamic-slice_fusion.3
  8.7 0.8 pad_maximum_fusion
  9.6 0.6 broadcast_in_dim.42.gain
  10.5 1.1 copy-done.10
  11.6 39.4 %shard_map.254 = (bf16[4,4,96,896]{3,2,1,0:T(8,128)(2,1)S(1)}, bf16[2,4,48,1152]{3,2,1,0:T(8,128)(2,1)S(1)}, bf16[2,256,1536]{2,1,0:T(8,128)(2,1)S(1)}, bf16[2,2,2,128,1536]{4,3,2,1,0:T(8,128)(2,1)S(1)}) custom-call(bf16[96,896]{1,0:T(8,128)(2,1)S(1)} %pad_maximum_fusion.3.w, bf16[96,1152]{1,0:T(8,128)(2,1)S(1)} %pad.10.down, ...), custom_call_target="tpu_custom_call" | custom-call | tf_op jit(solution)/shard_map/pallas_call | solution.py:74
  51.0 1.6 copy-done.4
  52.6 1.5 copy-done.5
  54.1 0.9 copy-done.8
  55.0 0.4 multiply_reduce_fusion
  55.6 0.4 fusion.1.h1
  56.0 2.2 copy-done.6
  58.2 1.0 fusion.4
  59.2 1.0 copy-done.16
  60.2 1.6 fusion.10
  61.8 2.7 compare_select_fusion.2.start_ref
  64.5 2.9 fusion.9
  67.6 24.1 %shard_map.255.kv = bf16[2,8,512,128]{3,2,1,0:T(8,128)(2,1)S(1)} custom-call(bf16[512,128]{1,0:T(8,128)(2,1)S(1)} %pad_maximum_fusion.4.mine), custom_call_target="tpu_custom_call" | custom-call | tf_op jit(solution)/shard_map/pallas_call | solution.py:74
  91.7 1.3 copy-done.1
  93.0 0.3 copy.32
  93.3 1.7 copy.33
  95.0 0.8 copy.34
  95.8 1.1 multiply_subtract_fusion
  97.0 0.2 copy.35.q
  97.2 0.7 reshape.242.gain
  97.9 1.6 copy-done.2
  99.5 2.2 shard_map.256
  101.7 0.9 copy-done.9
  102.6 2.1 pad_maximum_fusion.1
  104.7 0.8 constant_dynamic-slice_fusion.5.tok
  105.5 3.4 %convolution_convert_fusion = bf16[512,1536]{1,0:T(8,128)(2,1)} fusion(bf16[512,384]{1,0:T(8,128)(2,1)S(1)} %get-tuple-element.36.ob, bf16[1536,896]{1,0:T(8,128)(2,1)} %bitcast.80), kind=kOutput, calls=%fused_computation.4 | convolution fusion | flops 604766208 | bytes 3145728 | tf_op jit(solution)/shard_map/dot_general | solution.py:267
  108.9 103.8 %shard_map.257 = (f32[128,1536]{1,0:T(8,128)}, f32[128,1536]{1,0:T(8,128)}, bf16[2,2,128,1536]{3,2,1,0:T(8,128)(2,1)}, f32[1,1536]{1,0:T(1,128)}, bf16[4,128,153...) custom-call(bf16[2,2,128,1536]{3,2,1,0:T(8,128)(2,1)} %bitcast.87, ...), custom_call_target="tpu_custom_call" | custom-call | tf_op jit(solution)/shard_map/pallas_call | solution.py:558
  212.7 108.4 %shard_map.258 = (f32[4,24,896]{2,1,0:T(8,128)}, f32[2,4,8,1536]{3,2,1,0:T(8,128)}, bf16[4,48,1152]{2,1,0:T(8,128)(2,1)}, f32[4,24,1152]{2,1,0:T(8,128)}, bf16[2...) custom-call(bf16[2,4,4,2,48,1152]{5,4,3,2,1,0:T(8,128)(2,1)} %get-tuple-element.39.g_hbm, ...), custom_call_target="tpu_custom_call" | custom-call | tf_op jit(solution)/shard_map/pallas_call | solution.py:954
  321.1 1.1 slice_add_fusion
  322.2 0.6 slice_bitcast_fusion.16
  322.8 0.9 slice.136
  323.7 1.0 slice_reduce_fusion
  324.8 1.1 slice_bitcast_fusion
  325.9 0.2 concatenate.54
  326.1 0.8 concatenate.55
  327.1 0.8 concatenate.53
  327.9 1.4 bitcast_convert_fusion
  329.4 0.6 reshape.240
  330.2 0.5 slice_bitcast_fusion.18
  330.7 0.6 maximum_bitcast_fusion
  331.3 0.6 pad_maximum_fusion.5
  332.0 0.6 dynamic-slice_bitcast_fusion.2
  332.5 0.9 concatenate.56
  333.5 0.9 copy.41
  (78 shorter events, 1.3 us)
Async XLA Ops:
  7.2 3.0 copy-start
  7.2 101.7 %all-gather.2.cloned.1.call-start = ((), (), s32[]{:S(2)}) async-start(), calls=%async_computation | async-start | bytes 7520256 | tf_op jit(solution)/shard_map/all_gather | solution.py:1072
  7.2 2.3 copy-start.24
  8.6 1.8 copy-start.20
  8.6 1.8 copy-start.21
  8.6 1.8 copy-start.22
  8.7 1.8 copy-start.23
  8.7 1.8 copy-start.7
  10.5 1.1 copy-start.10
  11.6 43.8 %copy-start.26 = (bf16[768]{0:T(1024)(128)(2,1)S(1)}, bf16[768]{0:T(1024)(128)(2,1)}, u32[]{:S(2)}) copy-start(bf16[768]{0:T(1024)(128)(2,1)} %param.20) | copy-start | bytes 4612
  11.6 43.9 %copy-start.27 = (bf16[128]{0:T(256)(128)(2,1)S(1)}, bf16[128]{0:T(256)(128)(2,1)}, u32[]{:S(2)}) copy-start(bf16[128]{0:T(256)(128)(2,1)} %param.21) | copy-start | bytes 772
  11.6 43.9 %copy-start.28 = (bf16[128]{0:T(256)(128)(2,1)S(1)}, bf16[128]{0:T(256)(128)(2,1)}, u32[]{:S(2)}) copy-start(bf16[128]{0:T(256)(128)(2,1)} %param.22) | copy-start | bytes 772
  51.0 1.6 copy-start.4
  52.6 1.5 copy-start.5
  54.1 0.9 copy-start.8
  55.6 2.6 copy-start.6
  56.0 3.2 copy-start.14
  59.2 1.0 copy-start.16
  64.5 33.4 %copy-start.12 = (s32[1,512]{1,0:T(1,128)}, s32[1,512]{1,0:T(1,128)S(1)}, u32[]{:S(2)}) copy-start(s32[1,512]{1,0:T(1,128)S(1)} %compare_select_fusion.2.start_ref) | copy-start | bytes 6148
  91.7 1.3 copy-start.1
  95.8 1.4 copy-start.25
  97.0 5.6 %copy-start.15 = (f32[512,64]{1,0:T(8,128)S(1)}, f32[512,64]{1,0:T(8,128)}, u32[]{:S(2)}) copy-start(f32[512,64]{1,0:T(8,128)} %get-tuple-element.85) | copy-start | bytes 393220
  97.2 7.5 %copy-start.3 = (bf16[512,384]{1,0:T(8,128)(2,1)}, bf16[512,384]{1,0:T(8,128)(2,1)S(1)}, u32[]{:S(2)}) copy-start(bf16[512,384]{1,0:T(8,128)(2,1)S(1)} %copy.35.q) | copy-start | bytes 1179652
  97.9 1.6 copy-start.2
  101.7 0.9 copy-start.9
  102.6 6.3 %copy-start.11 = (bf16[512,384]{1,0:T(8,128)(2,1)}, bf16[512,384]{1,0:T(8,128)(2,1)S(1)}, u32[]{:S(2)}) copy-start(bf16[512,384]{1,0:T(8,128)(2,1)S(1)} %get-tuple-element.36.ob) | copy-start | bytes 1179652
  102.6 6.3 %copy-start.13 = (f32[8,512]{1,0:T(8,128)}, f32[8,512]{1,0:T(8,128)S(1)}, u32[]{:S(2)}) copy-start(f32[8,512]{1,0:T(8,128)S(1)} %get-tuple-element.43.lse) | copy-start | bytes 49156
  321.1 4.8 %copy-start.19 = (bf16[4,48,1152]{2,1,0:T(8,128)(2,1)S(1)}, bf16[4,48,1152]{2,1,0:T(8,128)(2,1)}, u32[]{:S(2)}) copy-start(bf16[4,48,1152]{2,1,0:T(8,128)(2,1)} %get-tuple-element.52) | copy-start | bytes 1327108
  325.9 2.0 copy-start.18
  327.9 5.6 %copy-start.17 = (bf16[2,128,1536]{2,1,0:T(8,128)(2,1)S(1)}, bf16[2,128,1536]{2,1,0:T(8,128)(2,1)}, u32[]{:S(2)}) copy-start(bf16[2,128,1536]{2,1,0:T(8,128)(2,1)} %get-tuple-element.48) | copy-start | bytes 2359300
Sparse Core Ops, SparseCore 0:
  10.2 89.3 all-gather.1

commit v2 on v1

--- a/solution.py
+++ b/solution.py
@@ -87,211 +87,279 @@
     return jax.ShapeDtypeStruct(dims, kind)
 
 
-def opening_kernel(
-    w, down, tok, dy, w_all, downs, tok2, dy_all, s1, r1, s2, r2, s3, r3, ts, tr, ds, dr, fs, fr
+def over_rows(a, b):
+    return lax.dot_general(a, b, (((0,), (0,)), ((), ())), preferred_element_type=F32)
+
+
+def by_columns(a, b):
+    return lax.dot_general(a, b, (((1,), (1,)), ((), ())), preferred_element_type=F32)
+
+
+def plain(a, b):
+    return lax.dot_general(a, b, (((1,), (0,)), ((), ())), preferred_element_type=F32)
+
+
+def visible_pairs(block, first, start, rows):
+    key = block * KEYS + lax.broadcasted_iota(jnp.int32, (KEYS, rows), 0)
+    row = first + lax.broadcasted_iota(jnp.int32, (1, rows), 1)
+    return (key >= start) & (key <= row)
+
+
+class RingGather:
+    def __init__(self, along, position, pieces, target, source, sems):
+        self.along, self.position, self.pieces = along, position, pieces
+        self.target, self.source, self.sems = target, source, sems
+
+    def hop(self, i, way):
+        s, r = self.sems[:2]
+        return describe(
+            self.source(i),
+            self.target(self.position, i),
+            s.at[i, way],
+            r.at[i, way],
+            self.along(1 if way == 0 else 3),
+        )
+
+    def onward(self, i):
+        s, r = self.sems[2:]
+        way = i // 2
+        block = self.target(lax.rem(self.position + (3 if way == 0 else 1), 4), i)
+        return describe(block, block, s.at[i], r.at[i], self.along(1 if way == 0 else 3))
+
+    def start(self, i):
+        self.hop(i, 0).start()
+        self.hop(i, 1).start()
+
+    def forward(self, i):
+        self.hop(i, i // 2).wait_recv()
+        self.onward(i).start()
+
+    def finish(self):
+        for i in range(4):
+            self.hop(i, 1 - i // 2).wait_recv()
+            self.onward(i).wait()
+            self.hop(i, 0).wait_send()
+            self.hop(i, 1).wait_send()
+
+
+def turned(values, cosines, sines):
+    return values * cosines - pltpu.roll(values, values.shape[-1] // 2, 1) * sines
+
+
+def front_kernel(
+    heads,
+    w, ffn, tok, dy, segments, gain, bias, frequency,
+    w_all, gate_all, halves, dy_all, h1, q, kv, exact, ob, lse, starts, cosines, sines, part,
+    tok2, top, total, acc,
+    s1, r1, wa, wb, wc, wd, s3, r3, ga, gb, gc, gd, ts, tr, ds, dr, fs, fr, ks, kr, cs, cr,
 ):
     me = Place()
     y, z, lo, k, t = me.y, me.z, me.lo, me.k, me.t
-    rows = w.shape[0] // 2
-    halves = (pl.ds(0, rows), pl.ds(rows, rows))
+    index = z * 2 + lo
+    count, model = tok.shape
+    rows = 2 * count
+    width, size = q.shape[1], exact.shape[1]
+    rowed = width + size
+    shard = w.shape[0] // 2
+    parts = (pl.ds(0, shard), pl.ds(shard, shard))
     near = [me.in_ring(1 - lo, t), me.in_ring(1 - lo, 1 - t)]
+    offsets = (1, 3, 2)
     greet(
         [me.along_z(j) for j in (1, 2, 3)]
         + [me.along_y(j) for j in (1, 2, 3)]
         + [me.sibling]
         + near
-    )
-    first = []
-    for half, along in ((0, me.along_z), (1, me.along_y)):
-        part = halves[half]
-        first.append(
-            [
-                send(
-                    w.at[part],
-                    w_all.at[y, z, part],
-                    s1.at[half, j - 1],
-                    r1.at[half, j - 1],
-                    along(j),
-                )
-                for j in (2, 1, 3)
-            ]
-        )
-    rest = []
-    mine = dy.shape[0] // 2
+        + [{"fsdp": y * 4 + lax.rem(z + j, 4), "ctx": (1 - lo) * 2 + k} for j in (1, 2, 3)]
+    )
+
+    def attn_place(half, position, i):
+        if half == 0:
+            return w_all.at[position, lax.rem(z + 4 - i, 4), parts[0]]
+        return w_all.at[lax.rem(y + 4 - i, 4), position, parts[1]]
+
+    def attn_source(half, i):
+        if i == 0:
+            return w.at[parts[half]]
+        return attn_place(half, y if half == 0 else z, i)
+
+    def first_hop(half, j):
+        along = me.along_z if half == 0 else me.along_y
+        return describe(
+            w.at[parts[half]],
+            w_all.at[y, z, parts[half]],
+            s1.at[half, j - 1],
+            r1.at[half, j - 1],
+            along(j),
+        )
+
+    rings = [
+        RingGather(
+            me.along_y if half == 0 else me.along_z,
+            y if half == 0 else z,
+            4,
+            functools.partial(attn_place, half),
+            functools.partial(attn_source, half),
+            [sem.at[half] for sem in (wa, wb, wc, wd)],
+        )
+        for half in (0, 1)
+    ]
+    for j in offsets:
+        for half in (0, 1):
+            first_hop(half, j).start()
+    for ring in rings:
+        ring.start(0)
+    tokens_share = send(tok, tok2, ts, tr, me.sibling)
+    slab = count // 2
     near_copies = [
-        send(dy.at[pl.ds(t * mine, mine)], dy_all.at[lo, t, k], ds.at[i], dr.at[i], near[i])
+        send(dy.at[pl.ds(t * slab, slab)], dy_all.at[lo, t, k], ds.at[i], dr.at[i], near[i])
         for i in (0, 1)
     ]
-    rest.append(send(tok, tok2.at[k], ts, tr, me.sibling))
-    own = [
-        send(
-            dy.at[pl.ds(h * mine, mine)], dy_all.at[lo, h, k], fs.at[2 + h], fr.at[2 + h], me.sibling
-        )
+    rest = [
+        send(dy.at[pl.ds(h * slab, slab)], dy_all.at[lo, h, k], fs.at[2 + h], fr.at[2 + h], me.sibling)
         for h in (0, 1)
     ]
-    rest += own
-    for half, along in ((0, me.along_y), (1, me.along_z)):
-        part = halves[half]
-        for j in (2, 1, 3):
-            rest.append(
-                send(
-                    w.at[part],
-                    w_all.at[y, z, part],
-                    s2.at[half, 0, j - 1],
-                    r2.at[half, 0, j - 1],
-                    along(j),
-                )
-            )
-    for half, along, here in ((0, me.along_z, z), (1, me.along_y, y)):
-        for j in (2, 1, 3):
-            rest.append(
-                send(
-                    down.at[halves[half]],
-                    downs.at[half, here],
-                    s3.at[half, j - 1],
-                    r3.at[half, j - 1],
-                    along(j),
-                )
-            )
-        downs[half, here] = down[halves[half]]
     w_all[y, z] = w[...]
-    tok2[k] = tok[...]
     for h in (0, 1):
-        dy_all[lo, h, k] = dy[pl.ds(h * mine, mine)]
-    for order in range(3):
-        for half, along in ((0, me.along_y), (1, me.along_z)):
-            part = halves[half]
-            offset = (2, 1, 3)[order]
-            first[half][order].wait()
-            if half == 0:
-                block = w_all.at[y, lax.rem(z - offset + 4, 4), part]
-            else:
-                block = w_all.at[lax.rem(y - offset + 4, 4), z, part]
-            for j in (2, 1, 3):
-                rest.append(
-                    send(
-                        block,
-                        block,
-                        s2.at[half, offset, j - 1],
-                        r2.at[half, offset, j - 1],
-                        along(j),
-                    )
-                )
+        dy_all[lo, h, k] = dy[pl.ds(h * slab, slab)]
+
+    first = pl.multiple_of(index * rows, rows)
+    everyone = segments[pl.ds(y, 1), :]
+    mine = segments[pl.ds(y, 1), pl.ds(first, rows)]
+    start = jnp.zeros((1, rows), jnp.int32)
+    for number in (1, 2, 3):
+        begin = jnp.sum(jnp.where(everyone < number, 1.0, 0.0), axis=1, keepdims=True)
+        start = jnp.where(mine == number, begin.astype(jnp.int32), start)
+    starts[...] = start
+    row = first + lax.broadcasted_iota(jnp.int32, (1, rows), 1)
+    pos = jnp.broadcast_to((row - start).astype(F32), (8, rows)).T[:, :1]
+    angles = pos * frequency[...]
+    lane = lax.broadcasted_iota(jnp.int32, (1, size), 1)
+    cosines[...] = jnp.cos(angles)
+    sines[...] = jnp.sin(angles) * jnp.where(lane < size // 2, 1.0, -1.0)
+
+    for j in offsets:
+        for half in (0, 1):
+            first_hop(half, j).wait()
+            rings[half].start(j)
+
+    def normed(x):
+        x = x.astype(F32)
+        factor = lax.rsqrt(jnp.mean(x * x, axis=-1, keepdims=True) + epsilon)
+        return (x * factor * gain[...]).astype(BF)
+
+    h1[pl.ds(pl.multiple_of(k * count, count), count)] = normed(tok[...])
+    tokens_share.wait()
+    h1[pl.ds(pl.multiple_of((1 - k) * count, count), count)] = normed(tok2[...])
+
+    for i in (0, 1, 3, 2):
+        for ring in rings:
+            ring.forward(i)
+
+    def ffn_hop(i, half, j):
+        along, here = (me.along_z, z) if half == 0 else (me.along_y, y)
+        return describe(
+            ffn.at[i, parts[half]],
+            halves.at[i, half, here],
+            s3.at[i, half, j - 1],
+            r3.at[i, half, j - 1],
+            along(j),
+        )
+
+    for i in range(3):
+        for half in (0, 1):
+            for j in offsets:
+                ffn_hop(i, half, j).start()
+            halves[i, half, z if half == 0 else y] = ffn[i, parts[half]]
+    for ring in rings:
+        ring.finish()
+
+    inward = w_all[:, :, :, :rowed].reshape(model, rowed)
+    linear = plain(h1[...], inward) + bias[...]
+    scale = 1.0 / math.sqrt(size)
+    is_key = k == 0
+    own = turned(
+        linear[:, width:],
+        jnp.where(is_key, cosines[...], 1.0),
+        jnp.where(is_key, sines[...], 0.0),
+    )
+    kv[k, index] = own.astype(BF)
+    block = kv.at[k, index]
+
+    def keys_copy(i, device):
+        return describe(block, block, ks.at[i], kr.at[index], device)
+
+    targets = [(dz, to) for dz in (1, 2, 3) for to in (0, 1)]
+
+    def target(dz, to):
+        return {"fsdp": y * 4 + lax.rem(z + dz, 4), "ctx": to * 2 + k}
+
+    for i, (dz, to) in enumerate(targets):
+
+        @pl.when(z + dz < 4)
+        def _():
+            keys_copy(i, target(dz, to)).start()
+
+    @pl.when(lo == 0)
+    def _():
+        keys_copy(6, {"ctx": 2 + k}).start()
+
+    def keys_share(b):
+        there = kv.at[k, b]
+        return describe(there, there, cs.at[b], cr.at[b], me.sibling)
+
+    keys_share(index).start()
+    for h in range(heads):
+        here = slice(h * size, (h + 1) * size)
+        q[:, here] = (turned(linear[:, here], cosines[...], sines[...]) * scale).astype(BF)
+
+    def gate_place(half, position, i):
+        if half == 0:
+            return gate_all.at[position, lax.rem(z + 4 - i, 4), 0]
+        return gate_all.at[lax.rem(y + 4 - i, 4), position, 1]
+
+    def gate_source(half, i):
+        return halves.at[0, half, lax.rem((z if half == 0 else y) + 4 - i, 4)]
+
+    gates = [
+        RingGather(
+            me.along_y if half == 0 else me.along_z,
+            y if half == 0 else z,
+            4,
+            functools.partial(gate_place, half),
+            functools.partial(gate_source, half),
+            [sem.at[half] for sem in (ga, gb, gc, gd)],
+        )
+        for half in (0, 1)
+    ]
+    for half in (0, 1):
+        for j in offsets:
+            ffn_hop(0, half, j).wait()
+        for i in range(4):
+            gates[half].start(i)
+    gate_all[y, :, 0] = halves[0, 0]
+    gate_all[:, z, 1] = halves[0, 1]
     for i, half in ((0, t), (1, 1 - t)):
         near_copies[i].wait()
-        block = dy_all.at[1 - lo, half, k]
-        rest.append(send(block, block, fs.at[i], fr.at[i], me.sibling))
-    for copy in rest:
-        copy.wait()
-
-
-def opening(w, down, tok, dy):
-    rows, width = w.shape
-    count, model = tok.shape
-    return comm_call(
-        opening_kernel,
-        [
-            shape((4, 4, rows, width), BF),
-            shape((2, 4, rows // 2, down.shape[1]), BF),
-            shape((2, count, model), BF),
-            shape((2, 2, 2, count // 2, model), BF),
-        ],
-        [
-            DMA((2, 3)),
-            DMA((2, 3)),
-            DMA((2, 4, 3)),
-            DMA((2, 4, 3)),
-            DMA((2, 3)),
-            DMA((2, 3)),
-            DMA,
-            DMA,
-            DMA((2,)),
-            DMA((2,)),
-            DMA((4,)),
-            DMA((4,)),
-        ],
-        1,
-        32,
-        w,
-        down,
-        tok,
-        dy,
-    )
-
-
-def keys_kernel(mine, kv, s1, r1, s2, r2):
-    me = Place()
-    k = me.k
-    own = me.z * 2 + me.lo
-    steps = [(dz, dl) for dz in (2, 1, 3, 0) for dl in (0, 1) if dz or dl]
-
-    def partner(dz, dl):
-        return {
-            "fsdp": me.y * 4 + lax.rem(me.z + dz, 4),
-            "ctx": lax.rem(me.lo + dl, 2) * 2 + k,
-        }
-
-    greet([partner(dz, dl) for dz, dl in steps] + [me.sibling])
-    copies = [
-        send(mine, kv.at[k, own], s1.at[i], r1.at[i], partner(dz, dl))
-        for i, (dz, dl) in enumerate(steps)
-    ]
-    rest = [send(mine, kv.at[k, own], s2.at[7], r2.at[7], me.sibling)]
-    kv[k, own] = mine[...]
-    for i in (6, 2, 4, 3, 5, 0, 1):
-        dz, dl = steps[i]
-        copies[i].wait()
-        block = kv.at[k, lax.rem(me.z - dz + 4, 4) * 2 + lax.rem(me.lo + dl, 2)]
-        rest.append(send(block, block, s2.at[i], r2.at[i], me.sibling))
-    for copy in rest:
-        copy.wait()
-
-
-def share_keys(mine):
-    rows, width = mine.shape
-    return comm_call(
-        keys_kernel,
-        [shape((2, 8, rows, width), BF)],
-        [DMA((7,)), DMA((7,)), DMA((8,)), DMA((8,))],
-        2,
-        16,
-        mine,
-    )[0]
-
-
-def over_rows(a, b):
-    return lax.dot_general(a, b, (((0,), (0,)), ((), ())), preferred_element_type=F32)
-
-
-def by_columns(a, b):
-    return lax.dot_general(a, b, (((1,), (1,)), ((), ())), preferred_element_type=F32)
-
-
-def plain(a, b):
-    return lax.dot_general(a, b, (((1,), (0,)), ((), ())), preferred_element_type=F32)
-
-
-def visible_pairs(block, first, start, rows):
-    key = block * KEYS + lax.broadcasted_iota(jnp.int32, (KEYS, rows), 0)
-    row = first + lax.broadcasted_iota(jnp.int32, (1, rows), 1)
-    return (key >= start) & (key <= row)
-
-
-def attend_kernel(heads, start_ref, q, kv, o, exact, lse, top, total, acc):
-    me = Place()
-    rows = q.shape[0]
-    size = q.shape[1] // heads
-    index = me.z * 2 + me.lo
-    first = index * rows
-    start = start_ref[...]
+        there = dy_all.at[1 - lo, half, k]
+        rest.append(send(there, there, fs.at[i], fr.at[i], me.sibling))
+
     top[...] = jnp.full_like(top, masked_score)
     total[...] = jnp.zeros_like(total)
     acc[...] = jnp.zeros_like(acc)
 
-    def step(block, _):
-        keys = kv[0, block]
-        values = kv[1, block]
-        seen = visible_pairs(block, first, start, rows)
+    def step(i, _):
+        b = index - i
+
+        @pl.when(b > 0)
+        def _():
+            there = kv.at[k, b - 1]
+            describe(there, there, ks.at[0], kr.at[b - 1], me.sibling).wait_recv()
+            keys_share(b - 1).start()
+
+        keys_share(b).wait_recv()
+        keys = kv[0, b]
+        values = kv[1, b]
+        seen = visible_pairs(b, first, start, rows)
         for h in range(heads):
             s = by_columns(keys, q[:, h * size : (h + 1) * size])
             s = jnp.where(seen, s, masked_score)
@@ -305,33 +373,105 @@
         return 0
 
     lax.fori_loop(0, index + 1, step, 0)
+    for half in (0, 1):
+        for i in range(4):
+            gates[half].forward(i)
     lse[...] = jnp.zeros_like(lse)
     for h in range(heads):
         sums = total[h : h + 1]
         lse[h : h + 1] = top[h : h + 1] + jnp.log(sums)
         out = acc[h] / sums
         exact[h] = out
-        o[:, h * size : (h + 1) * size] = out.T.astype(BF)
-
-
-def attend(start, q, kv, heads):
-    rows, width = q.shape
+        ob[:, h * size : (h + 1) * size] = out.T.astype(BF)
+    outward = w_all[:, :, :, rowed:].reshape(model, width)
+    part[...] = by_columns(ob[...], outward).astype(BF).reshape(part.shape)
+
+    for i, (dz, to) in enumerate(targets):
+
+        @pl.when(z + dz < 4)
+        def _():
+            keys_copy(i, target(dz, to)).wait_send()
+
+    @pl.when(lo == 0)
+    def _():
+        keys_copy(6, {"ctx": 2 + k}).wait_send()
+
+    def shared(b, _):
+        keys_share(b).wait_send()
+        return 0
+
+    lax.fori_loop(0, index + 1, shared, 0)
+    for i in (1, 2):
+        for half in (0, 1):
+            for j in offsets:
+                ffn_hop(i, half, j).wait()
+    for ring in gates:
+        ring.finish()
+    for copy in rest:
+        copy.wait()
+
+
+def front(heads, w, ffn, tok, dy, segments, gain, bias, frequency):
+    shard, total = w.shape
+    hidden = ffn.shape[2]
+    count, model = tok.shape
+    rows = 2 * count
+    width = bias.shape[1] - frequency.shape[1]
+    size = frequency.shape[1]
+    args = (w, ffn, tok, dy, segments, gain, bias, frequency)
+    outs = [
+        shape((4, 4, shard, total), BF),
+        shape((4, 4, 2, shard // 2, hidden), BF),
+        shape((3, 2, 4, shard // 2, hidden), BF),
+        shape((2, 2, 2, count // 2, model), BF),
+        shape((rows, model), BF),
+        shape((rows, width), BF),
+        shape((2, 8, rows, size), BF),
+        shape((heads, size, rows), F32),
+        shape((rows, width), BF),
+        shape((8, rows), F32),
+        shape((1, rows), jnp.int32),
+        shape((rows, size), F32),
+        shape((rows, size), F32),
+        shape((2, 2, count // 2, model), BF),
+    ]
     return pl.pallas_call(
-        functools.partial(attend_kernel, heads),
-        out_shape=[
-            shape((rows, width), BF),
-            shape((heads, width // heads, rows), F32),
-            shape((8, rows), F32),
-        ],
-        in_specs=[VM] * 3,
-        out_specs=[VM] * 3,
+        functools.partial(front_kernel, heads),
+        out_shape=outs,
+        in_specs=[VM] * len(args),
+        out_specs=[VM] * len(outs),
         scratch_shapes=[
+            pltpu.VMEM((count, model), BF),
             pltpu.VMEM((8, rows), F32),
             pltpu.VMEM((8, rows), F32),
-            pltpu.VMEM((heads, width // heads, rows), F32),
+            pltpu.VMEM((heads, size, rows), F32),
+            DMA((2, 3)),
+            DMA((2, 3)),
+            DMA((2, 4, 2)),
+            DMA((2, 4, 2)),
+            DMA((2, 4)),
+            DMA((2, 4)),
+            DMA((3, 2, 3)),
+            DMA((3, 2, 3)),
+            DMA((2, 4, 2)),
+            DMA((2, 4, 2)),
+            DMA((2, 4)),
+            DMA((2, 4)),
+            DMA,
+            DMA,
+            DMA((2,)),
+            DMA((2,)),
+            DMA((4,)),
+            DMA((4,)),
+            DMA((7,)),
+            DMA((8,)),
+            DMA((8,)),
+            DMA((8,)),
         ],
-        compiler_params=pltpu.CompilerParams(vmem_limit_bytes=32 << 20),
-    )(start, q, kv)
+        compiler_params=pltpu.CompilerParams(
+            collective_id=1, has_side_effects=True, vmem_limit_bytes=56 << 20
+        ),
+    )(*args)
 
 
 def norm_back(grad_normed, normed, factor):
@@ -339,10 +479,10 @@
 
 
 def block_kernel(
-    part, tok, gain, downs, dy_hbm, w_hbm,
+    part, tok, gain, dy_hbm, gate_hbm, halves,
     x1, dx1, dxl, gnf, ysum, down_sum, g_hbm,
     w, dy, dy_t, h2, h2_t, hid, gate_back, up_back, whole, m1, m2, m3, pb, s1, r1, r2, yb, ry, pd,
-    bs, br, cs, cr, ls, ms, hs, hr, fs, fr, ps, pr, xs, xr, ys, yr, gs, gr,
+    ba, bb, bc, bd, cs, cr, ls, ms, hs, hr, fs, fr, ps, pr, xs, xr, ys, yr, gs, gr,
 ):
     me = Place()
     y, z, lo, k, t = me.y, me.z, me.lo, me.k, me.t
@@ -358,7 +498,10 @@
         return pl.ds(pl.multiple_of(i * both, both), both)
 
     loads = [pltpu.make_async_copy(dy_hbm, dy, ls.at[3])]
-    loads += [pltpu.make_async_copy(w_hbm.at[i], w.at[i], ls.at[i]) for i in range(2)]
+    loads.append(pltpu.make_async_copy(gate_hbm, w.at[0], ls.at[0]))
+    for i in (1, 2):
+        loads.append(pltpu.make_async_copy(halves.at[i, 0], w.at[i, y, :, 0], ls.at[2 * i + 2]))
+        loads.append(pltpu.make_async_copy(halves.at[i, 1], w.at[i, :, z, 1], ls.at[2 * i + 3]))
     for copy in loads:
         copy.start()
     greet(
@@ -369,16 +512,30 @@
     )
     cores = send(part.at[1 - k], m1, ms.at[0], ms.at[1], me.sibling)
     here = w.at[2]
-    downs_out = []
-    for j in offsets:
-        downs_out.append(
-            send(downs.at[0], here.at[y, :, 0], bs.at[0, j - 1], br.at[0, j - 1], me.along_y(j))
-        )
-        downs_out.append(
-            send(downs.at[1], here.at[:, z, 1], bs.at[1, j - 1], br.at[1, j - 1], me.along_z(j))
-        )
-    w[2, y, :, 0] = downs[0]
-    w[2, :, z, 1] = downs[1]
+
+    def weight_place(i, half, position, piece):
+        if half == 0:
+            return w.at[i, position, lax.rem(z + 4 - piece, 4), 0]
+        return w.at[i, lax.rem(y + 4 - piece, 4), position, 1]
+
+    def weight_source(i, half, piece):
+        return halves.at[i, half, lax.rem((z if half == 0 else y) + 4 - piece, 4)]
+
+    rings = [
+        RingGather(
+            me.along_y if half == 0 else me.along_z,
+            y if half == 0 else z,
+            4,
+            functools.partial(weight_place, i, half),
+            functools.partial(weight_source, i, half),
+            [sem.at[i - 1, half] for sem in (ba, bb, bc, bd)],
+        )
+        for i in (1, 2)
+        for half in (0, 1)
+    ]
+    for ring in rings:
+        for piece in range(4):
+            ring.start(piece)
     loads[0].wait()
 
     def weight(i):
@@ -424,8 +581,13 @@
     for i in (1, 2, 3):
         hidden_copy(i).start()
     hidden_share(0).start()
-    for copy in loads[1:] + downs_out:
+    for ring in rings:
+        for piece in range(4):
+            ring.forward(piece)
+    for copy in loads[1:]:
         copy.wait()
+    for ring in rings:
+        ring.finish()
 
     def finish(i):
         part_share(i).wait_recv()
@@ -546,11 +708,10 @@
         copy.wait()
 
 
-def block(part, tok, gain, downs, dy, w):
+def block(part, tok, gain, dy, gate, halves):
     rows, model = tok.shape
-    hidden = w.shape[2]
-    half_rows = model // 32
-    w = w.reshape(2, 4, 4, 2, half_rows, hidden)
+    hidden = gate.shape[-1]
+    sums = halves.shape[1:]
     any_place = pl.BlockSpec(memory_space=pl.ANY)
     quarter = pltpu.VMEM((4, rows, model), BF)
     inner = pltpu.VMEM((4, 2 * rows, hidden), BF)
@@ -563,13 +724,13 @@
             shape((2, 2, rows, model), BF),
             shape((1, model), F32),
             shape((4, rows, model), BF),
-            shape(downs.shape, BF),
-            shape(w.shape, BF),
+            shape(sums, BF),
+            shape((2,) + gate.shape, BF),
         ],
-        in_specs=[VM] * 4 + [any_place] * 2,
+        in_specs=[VM] * 3 + [any_place] * 3,
         out_specs=[VM] * 6 + [any_place],
         scratch_shapes=[
-            pltpu.VMEM((3,) + w.shape[1:], BF),
+            pltpu.VMEM((3,) + gate.shape, BF),
             pltpu.VMEM(dy.shape, BF),
             turned,
             pltpu.VMEM(dy.shape, BF),
@@ -587,12 +748,14 @@
             pltpu.VMEM((3, rows, model), BF),
             quarter,
             quarter,
-            pltpu.VMEM((2, 3) + downs.shape[1:], BF),
+            pltpu.VMEM((2, 3) + sums[1:], BF),
+            DMA((2, 2, 4, 2)),
+            DMA((2, 2, 4, 2)),
+            DMA((2, 2, 4)),
+            DMA((2, 2, 4)),
             DMA((2, 3)),
             DMA((2, 3)),
-            DMA((2, 3)),
-            DMA((2, 3)),
-            DMA((4,)),
+            DMA((8,)),
             DMA((4,)),
             DMA((3,)),
             DMA((3,)),
@@ -610,11 +773,7 @@
         compiler_params=pltpu.CompilerParams(
             collective_id=3, has_side_effects=True, vmem_limit_bytes=62 << 20
         ),
-    )(part, tok, gain, downs, dy, w)
-
-
-def turned(values, cosines, sines):
-    return values * cosines - pltpu.roll(values, values.shape[-1] // 2, 1) * sines
+    )(part, tok, gain, dy, gate, halves)
 
 
 def rear_kernel(
@@ -1022,12 +1181,6 @@
     )(g, *args)
 
 
-def rotate(values_in, cosine, sine):
-    half_size = values_in.shape[-1] // 2
-    front, back = values_in[..., :half_size], values_in[..., half_size:]
-    return jnp.concatenate([front * cosine - back * sine, back * cosine + front * sine], axis=-1)
-
-
 def shards(
     tokens,
     segments,
@@ -1048,8 +1201,7 @@
     f = lax.axis_index("fsdp")
     c = lax.axis_index("ctx")
     t = lax.axis_index("tp")
-    seq, quarter = f // 4, f % 4
-    lo, k = c // 2, c % 2
+    k = c % 2
     is_key = k == 0
     size = key_matrix.shape[1]
     query_width = w_query.shape[1] // 2
@@ -1068,9 +1220,13 @@
     def widened(w):
         return jnp.pad(w, ((0, 0), (0, padded - hidden)))
 
-    own_ffn = jnp.stack([widened(hidden_slice(w_gate, 1)), widened(hidden_slice(w_up, 1))])
-    ffn_weights = lax.all_gather(own_ffn, "fsdp", axis=1, tiled=True)
-    own_down = widened(hidden_slice(w_down, 0).T)
+    own_ffn = jnp.stack(
+        [
+            widened(hidden_slice(w_gate, 1)),
+            widened(hidden_slice(w_up, 1)),
+            widened(hidden_slice(w_down, 0).T),
+        ]
+    )
 
     own_attn = jnp.concatenate(
         [
@@ -1080,55 +1236,44 @@
         ],
         axis=1,
     )
-    attn_all, downs, tok2, dy_all = opening(own_attn, own_down, tokens, cotangent)
-    attn_all = attn_all.reshape(model, own_width + query_width)
-    in_all, out_all = attn_all[:, :own_width], attn_all[:, own_width:]
     own_tokens = lax.dynamic_slice_in_dim(tokens, t * slice_rows, slice_rows, 0)
-
-    seg_row = lax.dynamic_index_in_dim(segments, seq, 0, keepdims=False)
     rows = 2 * count
-    first = (quarter * 2 + lo) * rows
-    seg_mine = lax.dynamic_slice_in_dim(seg_row, first, rows)
-    starts = jnp.zeros((rows,), jnp.int32)
-    for number in range(1, 4):
-        begin = jnp.sum((seg_row < number).astype(jnp.int32))
-        starts = jnp.where(seg_mine == number, begin, starts)
-    pos = (first + jnp.arange(rows, dtype=jnp.int32) - starts).astype(F32)
-    frequency = jnp.exp(
-        jnp.arange(size // 2, dtype=F32) * (-2.0 * math.log(rope_base) / size)
-    )
-    angles = pos[:, None, None] * frequency
-    cosine, sine = jnp.cos(angles), jnp.sin(angles)
-    kv_cosine = jnp.where(is_key, cosine[:, 0], 1.0)
-    kv_sine = jnp.where(is_key, sine[:, 0], 0.0)
-    starts = starts[None, :]
-    query_scale = 1.0 / math.sqrt(size)
-
-    gain_attn = norm_attn.astype(F32)
-    gain_ffn = norm_ffn.astype(F32)
-    x = tok2.reshape(rows, model).astype(F32)
-    h1 = (x * lax.rsqrt(jnp.mean(x * x, axis=-1, keepdims=True) + epsilon) * gain_attn).astype(BF)
+    half_size = size // 2
+    frequency = jnp.exp(jnp.arange(half_size, dtype=F32) * (-2.0 * math.log(rope_base) / size))
+    frequency = jnp.concatenate([frequency, frequency])[None]
+    gain_attn = norm_attn.astype(F32)[None]
+    gain_ffn = norm_ffn.astype(F32)[None]
     bias = jnp.concatenate(
         [
             lax.dynamic_slice_in_dim(b_query, k * query_width, query_width, 0),
             jnp.where(is_key, key_bias_vector, value_bias_vector),
         ]
-    ).astype(F32)
-    linear = plain(h1, in_all) + bias
-    q_lin = linear[:, :query_width].reshape(rows, heads, size)
-    q = (rotate(q_lin, cosine, sine) * query_scale).astype(BF).reshape(rows, query_width)
-    kv = share_keys(rotate(linear[:, query_width:], kv_cosine, kv_sine).astype(BF))
-    ob, exact, lse = attend(starts, q, kv, heads)
-    part = by_columns(ob, out_all).astype(BF).reshape(2, 2, slice_rows, model)
+    ).astype(F32)[None]
+    (
+        attn_all,
+        gate_all,
+        halves,
+        dy_all,
+        h1,
+        q,
+        kv,
+        exact,
+        ob,
+        lse,
+        starts,
+        cosines,
+        sines,
+        part,
+    ) = front(heads, own_attn, own_ffn, tokens, cotangent, segments, gain_attn, bias, frequency)
     x1, dx1, dxl, grad_norm_two, ysum, down_sum, ffn_grads = block(
-        part, own_tokens, gain_ffn[None], downs, dy_all, ffn_weights
+        part, own_tokens, gain_ffn, dy_all, gate_all, halves
     )
     a_all, ext_all, ffn_all, down_all, output, grad_tokens = rear(
         heads,
         ffn_grads,
         down_sum,
         dxl.reshape(rows, model),
-        attn_all,
+        attn_all.reshape(model, own_width + query_width),
         q,
         kv,
         exact,
@@ -1136,13 +1281,13 @@
         starts,
         ob,
         h1,
-        jnp.concatenate([cosine[:, 0], cosine[:, 0]], axis=1),
-        jnp.concatenate([sine[:, 0], -sine[:, 0]], axis=1),
+        cosines,
+        sines,
         ysum,
         x1,
         dx1,
         own_tokens,
-        gain_attn[None],
+        gain_attn,
         grad_norm_two,
     )
     owner_rows = shard_rows // 4

time: 342 us -> 308 us (0.901)
  between operations: 14.6 us -> 0.86 us
  local copies, waits for them, and re-layouts: 25.7 us -> 14 us
  other arithmetic: 18.6 us -> 9.5 us
  Pallas kernels: 278 us -> 283 us
  matrix products: 4.4 us -> 0 us
    unnamed x60 -> x15, local copies, waits for them, and re-layouts: 13 us -> 0.92 us
    pallas_call x3 -> x1, Pallas kernels: 65.7 us -> 72.1 us  [front(): pl.pallas_call(functools.partial(front_kernel, heads), out_shape=outs, in...]
    dot_general x2 -> x0, matrix products: 4.4 us -> none  [the longest x1 3.43 us: by_columns(): lax.dot_general(a, b, (((1,), (1,)), ((), ())), preferred_element_type=F32)]
  transfers between devices with their start and end apart: 1 -> 0, of which waited for: 0 -> 0; matrix products, arithmetic and copies ran while one was open for 6% -> 0% of each run, Pallas kernels for 19% -> 0%
where the time goes in v2:
time: 308 us; the launch traced here: 307 us
  Pallas kernels  283 us (92%)
  local copies, waits for them, and re-layouts  14 us (5%)
  other arithmetic  9.5 us (3%)
    pallas_call x1, Pallas kernels, rear(): pl.pallas_call(functools.partial(rear_kernel, heads), out_shape=outs, in_...  109 us
    pallas_call x1, Pallas kernels, block(): pl.pallas_call(block_kernel, out_shape=[shape((rows, model), F32), shape(...  101 us
    pallas_call x1, Pallas kernels, front(): pl.pallas_call(functools.partial(front_kernel, heads), out_shape=outs, in...  72.1 us

profile of v2, /device:TPU:1, one launch (start us, length us, event | category | flops | bytes accessed | tf_op | source)
XLA Modules:
  0.0 307.1 jit_solution(14263309524682729420)
XLA Ops:
  0.6 0.0 copy-start
  0.7 1.0 constant_dynamic-slice_fusion.6
  1.6 0.9 dynamic-slice_bitcast_fusion.1
  2.5 0.7 broadcast_select_fusion
  3.3 0.7 pad_maximum_fusion.1.w
  4.0 0.8 dynamic_slice.36
  4.7 0.7 fusion
  5.4 0.6 maximum_convert_fusion.bias
  6.0 1.3 constant_dynamic-slice_fusion.4
  7.3 0.0 copy-done
  7.3 0.1 dynamic-slice_bitcast_fusion
  7.5 0.0 copy-start.1
  7.5 0.0 copy-start.6
  7.5 0.9 pad_maximum_fusion.ffn
  8.4 0.0 copy-done.5
  8.4 0.6 reshape.101.gain
  9.1 0.6 maximum_bitcast_fusion.1.frequency
  9.6 72.1 %shard_map.254 = (bf16[4,4,96,896]{3,2,1,0:T(8,128)(2,1)}, bf16[4,4,2,48,1152]{4,3,2,1,0:T(8,128)(2,1)}, bf16[3,2,4,48,1152]{4,3,2,1,0:T(8,128)(2,1)}, bf16[2,2,...) custom-call(bf16[96,896]{1,0:T(8,128)(2,1)} %pad_maximum_fusion.1.w,, ...), custom_call_target="tpu_custom_call" | custom-call | tf_op jit(solution)/shard_map/pallas_call | solution.py:438
  81.8 0.0 copy-done.1
  81.8 0.8 constant_dynamic-slice_fusion.3.tok
  82.5 0.0 copy-done.6
  82.5 0.6 reshape.102.gain
  83.1 101.4 %shard_map.255 = (f32[128,1536]{1,0:T(8,128)}, f32[128,1536]{1,0:T(8,128)}, bf16[2,2,128,1536]{3,2,1,0:T(8,128)(2,1)}, f32[1,1536]{1,0:T(1,128)}, bf16[4,128,153...) custom-call(bf16[2,2,128,1536]{3,2,1,0:T(8,128)(2,1)} %get-tuple-element.41.part, ...), custom_call_target="tpu_custom_call" | custom-call | tf_op jit(solution)/shard_map/pallas_call | solution.py:719
  184.5 109.3 %shard_map.256 = (f32[4,24,896]{2,1,0:T(8,128)}, f32[2,4,8,1536]{3,2,1,0:T(8,128)}, bf16[4,48,1152]{2,1,0:T(8,128)(2,1)}, f32[4,24,1152]{2,1,0:T(8,128)}, bf16[2...) custom-call(bf16[2,4,4,2,48,1152]{5,4,3,2,1,0:T(8,128)(2,1)} %get-tuple-element.45.g_hbm, ...), custom_call_target="tpu_custom_call" | custom-call | tf_op jit(solution)/shard_map/pallas_call | solution.py:1113
  293.8 1.1 slice_bitcast_fusion
  294.9 0.0 copy-start.4
  294.9 0.9 concatenate.52
  295.8 1.1 slice_bitcast_fusion.4
  297.0 0.2 concatenate.50
  297.1 0.8 concatenate.51
  297.9 0.2 concatenate.48
  298.1 0.0 copy-start.2
  298.1 0.8 concatenate.49
  298.9 0.0 copy-done.4
  298.9 0.6 maximum_bitcast_fusion
  299.6 0.6 pad_maximum_fusion.2
  300.2 0.0 copy-done.3
  300.2 1.4 bitcast_convert_fusion
  301.6 0.6 slice_bitcast_fusion.16
  302.2 0.9 slice.105
  303.2 0.1 constant_dynamic-slice_fusion
  303.2 0.1 copy.29
  303.3 0.6 reshape.100
  304.0 0.6 dynamic-slice_bitcast_fusion.2
  304.6 1.0 slice_reduce_fusion
  305.6 0.1 constant_dynamic-slice_fusion.2
  305.7 0.5 slice_bitcast_fusion.18
  306.2 0.9 copy.31
  (11 shorter events, 0.1 us)
Async XLA Ops:
  0.6 6.7 %copy-start = (bf16[4480,96]{0,1:T(8,128)(2,1)S(1)}, bf16[4480,96]{0,1:T(8,128)(2,1)}, u32[]{:S(2)}) copy-start(bf16[4480,96]{0,1:T(8,128)(2,1)} %param.28) | copy-start | bytes 2580484
  3.3 5.2 %copy-start.5 = (bf16[1536]{0:T(1024)(128)(2,1)S(1)}, bf16[1536]{0:T(1024)(128)(2,1)}, u32[]{:S(2)}) copy-start(bf16[1536]{0:T(1024)(128)(2,1)} %param.24) | copy-start | bytes 9220
  7.5 74.3 %copy-start.1 = (bf16[256,1536]{1,0:T(8,128)(2,1)S(1)}, bf16[256,1536]{1,0:T(8,128)(2,1)}, u32[]{:S(2)}) copy-start(bf16[256,1536]{1,0:T(8,128)(2,1)} %tok.1) | copy-start | bytes 2359300
  7.5 75.0 %copy-start.6 = (bf16[1536]{0:T(1024)(128)(2,1)S(1)}, bf16[1536]{0:T(1024)(128)(2,1)}, u32[]{:S(2)}) copy-start(bf16[1536]{0:T(1024)(128)(2,1)} %param.25) | copy-start | bytes 9220
  294.9 4.0 %copy-start.4 = (f32[4,24,896]{2,1,0:T(8,128)S(1)}, f32[4,24,896]{2,1,0:T(8,128)}, u32[]{:S(2)}) copy-start(f32[4,24,896]{2,1,0:T(8,128)} %get-tuple-element.64) | copy-start | bytes 1032196
  295.8 4.4 %copy-start.3 = (bf16[2,128,1536]{2,1,0:T(8,128)(2,1)S(1)}, bf16[2,128,1536]{2,1,0:T(8,128)(2,1)}, u32[]{:S(2)}) copy-start(bf16[2,128,1536]{2,1,0:T(8,128)(2,1)} %get-tuple-element.63) | copy-start | bytes 2359300
  298.1 8.1 %copy-start.2 = (bf16[2,128,1536]{2,1,0:T(8,128)(2,1)S(1)}, bf16[2,128,1536]{2,1,0:T(8,128)(2,1)}, u32[]{:S(2)}) copy-start(bf16[2,128,1536]{2,1,0:T(8,128)(2,1)} %get-tuple-element.62) | copy-start | bytes 2359300

commit v3 on v2

--- a/solution.py
+++ b/solution.py
@@ -142,6 +142,50 @@
             self.hop(i, 1).wait_send()
 
 
+class RingSum:
+    def __init__(self, along, position, source, passing, got, sems):
+        self.along, self.position, self.source = along, position, source
+        self.passing, self.got, self.sems = passing, got, sems
+
+    def at(self, offset):
+        return lax.rem(self.position + offset, 4)
+
+    def first(self, way):
+        s, r = self.sems[:2]
+        return describe(
+            self.source(self.at(2), 2 * way, 2),
+            self.passing.at[way],
+            s.at[way],
+            r.at[way],
+            self.along(1 if way == 0 else 3),
+        )
+
+    def second(self, way):
+        s, r = self.sems[2:]
+        offset = 1 if way == 0 else 3
+        return describe(
+            self.source(self.at(offset), 0, 4), self.got.at[way], s.at[way], r.at[way], self.along(offset)
+        )
+
+    def start(self):
+        for way in (0, 1):
+            self.first(way).start()
+
+    def middle(self):
+        for way in (0, 1):
+            self.first(way).wait()
+            near = self.source(self.at(1 if way == 0 else 3), 2 * way, 2)
+            near[...] = (near[...].astype(F32) + self.passing[way].astype(F32)).astype(BF)
+            self.second(way).start()
+
+    def finish(self):
+        total = self.source(self.position, 0, 4)[...].astype(F32)
+        for way in (0, 1):
+            self.second(way).wait()
+            total = total + self.got[way].astype(F32)
+        return total
+
+
 def turned(values, cosines, sines):
     return values * cosines - pltpu.roll(values, values.shape[-1] // 2, 1) * sines
 
@@ -149,9 +193,9 @@
 def front_kernel(
     heads,
     w, ffn, tok, dy, segments, gain, bias, frequency,
-    w_all, gate_all, halves, dy_all, h1, q, kv, exact, ob, lse, starts, cosines, sines, part,
+    w_all, halves, dy_all, h1, q, kv, exact, ob, lse, starts, cosines, sines, part,
     tok2, top, total, acc,
-    s1, r1, wa, wb, wc, wd, s3, r3, ga, gb, gc, gd, ts, tr, ds, dr, fs, fr, ks, kr, cs, cr,
+    s1, r1, wa, wb, wc, wd, s3, r3, ts, tr, ds, dr, fs, fr, ks, kr, cs, cr,
 ):
     me = Place()
     y, z, lo, k, t = me.y, me.z, me.lo, me.k, me.t
@@ -265,11 +309,13 @@
             along(j),
         )
 
-    for i in range(3):
+    def ffn_hops(i):
         for half in (0, 1):
             for j in offsets:
                 ffn_hop(i, half, j).start()
             halves[i, half, z if half == 0 else y] = ffn[i, parts[half]]
+
+    ffn_hops(0)
     for ring in rings:
         ring.finish()
 
@@ -283,10 +329,10 @@
         jnp.where(is_key, sines[...], 0.0),
     )
     kv[k, index] = own.astype(BF)
-    block = kv.at[k, index]
+    own_keys = kv.at[k, index]
 
     def keys_copy(i, device):
-        return describe(block, block, ks.at[i], kr.at[index], device)
+        return describe(own_keys, own_keys, ks.at[i], kr.at[index], device)
 
     targets = [(dz, to) for dz in (1, 2, 3) for to in (0, 1)]
 
@@ -312,32 +358,8 @@
         here = slice(h * size, (h + 1) * size)
         q[:, here] = (turned(linear[:, here], cosines[...], sines[...]) * scale).astype(BF)
 
-    def gate_place(half, position, i):
-        if half == 0:
-            return gate_all.at[position, lax.rem(z + 4 - i, 4), 0]
-        return gate_all.at[lax.rem(y + 4 - i, 4), position, 1]
-
-    def gate_source(half, i):
-        return halves.at[0, half, lax.rem((z if half == 0 else y) + 4 - i, 4)]
-
-    gates = [
-        RingGather(
-            me.along_y if half == 0 else me.along_z,
-            y if half == 0 else z,
-            4,
-            functools.partial(gate_place, half),
-            functools.partial(gate_source, half),
-            [sem.at[half] for sem in (ga, gb, gc, gd)],
-        )
-        for half in (0, 1)
-    ]
-    for half in (0, 1):
-        for j in offsets:
-            ffn_hop(0, half, j).wait()
-        for i in range(4):
-            gates[half].start(i)
-    gate_all[y, :, 0] = halves[0, 0]
-    gate_all[:, z, 1] = halves[0, 1]
+    ffn_hops(1)
+    ffn_hops(2)
     for i, half in ((0, t), (1, 1 - t)):
         near_copies[i].wait()
         there = dy_all.at[1 - lo, half, k]
@@ -373,9 +395,6 @@
         return 0
 
     lax.fori_loop(0, index + 1, step, 0)
-    for half in (0, 1):
-        for i in range(4):
-            gates[half].forward(i)
     lse[...] = jnp.zeros_like(lse)
     for h in range(heads):
         sums = total[h : h + 1]
@@ -401,12 +420,10 @@
         return 0
 
     lax.fori_loop(0, index + 1, shared, 0)
-    for i in (1, 2):
+    for i in range(3):
         for half in (0, 1):
             for j in offsets:
                 ffn_hop(i, half, j).wait()
-    for ring in gates:
-        ring.finish()
     for copy in rest:
         copy.wait()
 
@@ -421,7 +438,6 @@
     args = (w, ffn, tok, dy, segments, gain, bias, frequency)
     outs = [
         shape((4, 4, shard, total), BF),
-        shape((4, 4, 2, shard // 2, hidden), BF),
         shape((3, 2, 4, shard // 2, hidden), BF),
         shape((2, 2, 2, count // 2, model), BF),
         shape((rows, model), BF),
@@ -453,10 +469,6 @@
             DMA((2, 4)),
             DMA((3, 2, 3)),
             DMA((3, 2, 3)),
-            DMA((2, 4, 2)),
-            DMA((2, 4, 2)),
-            DMA((2, 4)),
-            DMA((2, 4)),
             DMA,
             DMA,
             DMA((2,)),
@@ -479,10 +491,10 @@
 
 
 def block_kernel(
-    part, tok, gain, dy_hbm, gate_hbm, halves,
-    x1, dx1, dxl, gnf, ysum, down_sum, g_hbm,
-    w, dy, dy_t, h2, h2_t, hid, gate_back, up_back, whole, m1, m2, m3, pb, s1, r1, r2, yb, ry, pd,
-    ba, bb, bc, bd, cs, cr, ls, ms, hs, hr, fs, fr, ps, pr, xs, xr, ys, yr, gs, gr,
+    part, tok, gain, dy_hbm, halves,
+    x1, dx1, dxl, gnf, ysum, gate_sum, down_sum, up_grad,
+    w, dy, dy_t, h2, h2_t, hid, gate_back, up_back, whole, pb, s1, r1, r2, ry, passing, got, gx,
+    ba, bb, bc, bd, ca, cb, cc, cd, ls, ms, hs, hr, fs, fr, ps, pr, xs, xr, ys, yr, gs, gr,
 ):
     me = Place()
     y, z, lo, k, t = me.y, me.z, me.lo, me.k, me.t
@@ -497,11 +509,10 @@
     def columns(i):
         return pl.ds(pl.multiple_of(i * both, both), both)
 
-    loads = [pltpu.make_async_copy(dy_hbm, dy, ls.at[3])]
-    loads.append(pltpu.make_async_copy(gate_hbm, w.at[0], ls.at[0]))
-    for i in (1, 2):
-        loads.append(pltpu.make_async_copy(halves.at[i, 0], w.at[i, y, :, 0], ls.at[2 * i + 2]))
-        loads.append(pltpu.make_async_copy(halves.at[i, 1], w.at[i, :, z, 1], ls.at[2 * i + 3]))
+    loads = [pltpu.make_async_copy(dy_hbm, dy, ls.at[6])]
+    for i in range(3):
+        loads.append(pltpu.make_async_copy(halves.at[i, 0], w.at[i, y, :, 0], ls.at[2 * i]))
+        loads.append(pltpu.make_async_copy(halves.at[i, 1], w.at[i, :, z, 1], ls.at[2 * i + 1]))
     for copy in loads:
         copy.start()
     greet(
@@ -510,8 +521,8 @@
         + [me.along_z(j) for j in (1, 2, 3)]
         + [me.along_y(j) for j in (1, 2, 3)]
     )
+    m1, m2, m3 = r1.at[pl.ds(0, 2)], s1.at[0], r2.at[2]
     cores = send(part.at[1 - k], m1, ms.at[0], ms.at[1], me.sibling)
-    here = w.at[2]
 
     def weight_place(i, half, position, piece):
         if half == 0:
@@ -522,25 +533,41 @@
         return halves.at[i, half, lax.rem((z if half == 0 else y) + 4 - piece, 4)]
 
     rings = [
-        RingGather(
-            me.along_y if half == 0 else me.along_z,
-            y if half == 0 else z,
-            4,
-            functools.partial(weight_place, i, half),
-            functools.partial(weight_source, i, half),
-            [sem.at[i - 1, half] for sem in (ba, bb, bc, bd)],
-        )
-        for i in (1, 2)
-        for half in (0, 1)
+        [
+            RingGather(
+                me.along_y if half == 0 else me.along_z,
+                y if half == 0 else z,
+                4,
+                functools.partial(weight_place, i, half),
+                functools.partial(weight_source, i, half),
+                [sem.at[i, half] for sem in (ba, bb, bc, bd)],
+            )
+            for half in (0, 1)
+        ]
+        for i in range(3)
     ]
-    for ring in rings:
-        for piece in range(4):
-            ring.start(piece)
-    loads[0].wait()
+
+    def gather_start(i):
+        for ring in rings[i]:
+            for piece in range(4):
+                ring.start(piece)
+
+    def gather_forward(i):
+        for ring in rings[i]:
+            for piece in range(4):
+                ring.forward(piece)
+
+    def gather_finish(i):
+        for ring in rings[i]:
+            ring.finish()
+        for copy in loads[2 * i + 1 : 2 * i + 3]:
+            copy.wait()
 
     def weight(i):
         return w[i].reshape(model, inner)
 
+    gather_start(0)
+    loads[0].wait()
 
     def turn_dy(i, _):
         lo_i, t_i = chip(i)
@@ -552,6 +579,8 @@
     across = send(m2, m3, ms.at[2], ms.at[3], me.in_ring(lo, 1 - t))
     lax.fori_loop(0, 4, turn_dy, 0)
     x = tok[...].astype(F32) + part[k, t].astype(F32) + m1[t].astype(F32)
+    gather_forward(0)
+    gather_start(1)
     across.wait()
     x = x + m3[...].astype(F32)
     x1[...] = x
@@ -576,55 +605,110 @@
         )
 
     def result_share(i):
-        return describe(yb.at[i], ry.at[i], ys.at[i], yr.at[i], me.sibling)
+        return describe(pb.at[i], ry.at[i], ys.at[i], yr.at[i], me.sibling)
 
     for i in (1, 2, 3):
         hidden_copy(i).start()
     hidden_share(0).start()
-    for ring in rings:
-        for piece in range(4):
-            ring.forward(piece)
-    for copy in loads[1:]:
-        copy.wait()
-    for ring in rings:
-        ring.finish()
-
-    def finish(i):
-        part_share(i).wait_recv()
-        s1[i] = (s1[i].astype(F32) + r1[i].astype(F32)).astype(BF)
-
-        @pl.when(i > 0)
+    gather_forward(1)
+    gather_start(2)
+
+    def inward(i, _):
+        lo_i, t_i = chip(i)
+        hidden_share(i).wait_recv()
+
+        @pl.when(i == 0)
         def _():
-            part_copy(i).start()
-
-        whole[...] = by_columns(hid[i], weight(2)).reshape(2, rows, model)
-        yb[i] = whole[1 - k].astype(BF)
-        ysum[i] = whole[k].astype(BF)
-        result_share(i).start()
-        lo_i, t_i = chip(i)
-        h2_t[:, columns(i)] = h2[lo_i, t_i].reshape(both, model).T
-
-    def step(i, _):
-        lo_i, t_i = chip(i)
-
-        @pl.when(i > 0)
+            gather_finish(0)
+
+        h = h2[lo_i, t_i].reshape(both, model)
+        gate = plain(h, weight(0))
+        h2_t[:, columns(i)] = h.T
+
+        @pl.when(i == 0)
         def _():
-            hidden_copy(i).wait_recv()
-            hidden_share(i).start()
-            finish(i - 1)
-
-        hidden_share(i).wait_recv()
-        h = h2[lo_i, t_i].reshape(both, model)
-        d = dy[lo_i, t_i].reshape(both, model)
-        gate = plain(h, weight(0))
+            gather_finish(1)
+
         up = plain(h, weight(1))
         sigmoid_gate = jax.nn.sigmoid(gate)
         silu_gate = gate * sigmoid_gate
         hid[i] = (silu_gate * up).astype(BF)
-        grad_inner = plain(d, weight(2))
         slope = sigmoid_gate * (1.0 + gate * (1.0 - sigmoid_gate))
-        gate_back[i] = (grad_inner * up * slope).astype(BF)
-        up_back[i] = (grad_inner * silu_gate).astype(BF)
+        gate_back[i] = (up * slope).astype(BF)
+        up_back[i] = silu_gate.astype(BF)
+
+        @pl.when(i < 3)
+        def _():
+            hidden_copy(i + 1).wait_recv()
+            hidden_share(i + 1).start()
+
+        return 0
+
+    def gradient(target, left_t, right):
+        flat = right.shape[0] * right.shape[1]
+        step_rows = model // 4
+
+        def some(m, _):
+            r = pl.ds(pl.multiple_of(m * step_rows, step_rows), step_rows)
+            value = plain(left_t[r, :], right[...].reshape(flat, inner))
+            target[m] = value.astype(BF).reshape(target.shape[1:])
+            return 0
+
+        lax.fori_loop(0, 4, some, 0)
+
+    def ring_sums(n, target):
+        def along_z(position, piece, count):
+            return target.at[pl.ds(piece, count), position, 0]
+
+        def along_y(position, piece, count):
+            return target.at[position, pl.ds(piece, count), 1]
+
+        return [
+            RingSum(
+                along,
+                position,
+                source,
+                passing.at[n, half],
+                got.at[n, half],
+                [sem.at[n, half] for sem in (ca, cb, cc, cd)],
+            )
+            for half, (along, position, source) in enumerate(
+                ((me.along_z, z, along_z), (me.along_y, y, along_y))
+            )
+        ]
+
+    lax.fori_loop(0, 4, inward, 0)
+    gather_forward(2)
+    down_rings, gate_rings = ring_sums(0, gx), ring_sums(1, w.at[0])
+    gradient(gx, dy_t, hid)
+    for one in down_rings:
+        one.start()
+    gather_finish(2)
+
+    def homeward(i):
+        part_share(i).wait_recv()
+        s1[i] = (s1[i].astype(F32) + r1[i].astype(F32)).astype(BF)
+
+        @pl.when(i > 0)
+        def _():
+            part_copy(i).start()
+
+    def outward(n, _):
+        i = lax.rem(n + 1, 4)
+        lo_i, t_i = chip(i)
+        grad_inner = plain(dy[lo_i, t_i].reshape(both, model), weight(2))
+
+        @pl.when(n > 0)
+        def _():
+            homeward(n)
+
+        @pl.when(n == 2)
+        def _():
+            for one in down_rings:
+                one.middle()
+
+        gate_back[i] = (grad_inner * gate_back[i].astype(F32)).astype(BF)
+        up_back[i] = (grad_inner * up_back[i].astype(F32)).astype(BF)
         whole[...] = (
             by_columns(gate_back[i], weight(0)) + by_columns(up_back[i], weight(1))
         ).reshape(2, rows, model)
@@ -633,39 +717,12 @@
         part_share(i).start()
         return 0
 
-    lax.fori_loop(0, 4, step, 0)
-    finish(3)
-
-    def gradient(i, left_t, right):
-        flat = right.shape[0] * right.shape[1]
-        step_rows = model // 4
-
-        def some(m, _):
-            r = pl.ds(pl.multiple_of(m * step_rows, step_rows), step_rows)
-            value = plain(left_t[r, :], right[...].reshape(flat, inner))
-            w[i, m] = value.astype(BF).reshape(w.shape[2:])
-            return 0
-
-        lax.fori_loop(0, 4, some, 0)
-
-    def gradient_out(i):
-        copy = pltpu.make_async_copy(w.at[i], g_hbm.at[i], ls.at[i])
-        copy.start()
-        return copy
-
-    gradient(2, dy_t, hid)
-    downs_back = []
-    for j in offsets:
-        downs_back.append(
-            send(
-                here.at[:, lax.rem(z + j, 4), 0], pd.at[0, j - 1], cs.at[0, j - 1], cr.at[0, j - 1], me.along_z(j)
-            )
-        )
-        downs_back.append(
-            send(
-                here.at[lax.rem(y + j, 4), :, 1], pd.at[1, j - 1], cs.at[1, j - 1], cr.at[1, j - 1], me.along_y(j)
-            )
-        )
+    lax.fori_loop(0, 4, outward, 0)
+    gradient(w.at[0], h2_t, gate_back)
+    for one in gate_rings:
+        one.start()
+
+    homeward(0)
 
     grad = s1[0].astype(F32)
     for i in (1, 2, 3):
@@ -681,41 +738,49 @@
     block = dxl.at[k, t]
     across = send(block, block, gs.at[0], gr.at[0], me.in_ring(lo, 1 - t))
     rest = [send(block, block, gs.at[1], gr.at[1], me.sibling)]
-    gradient(0, h2_t, gate_back)
-    outs = [gradient_out(0)]
+    def result(i, _):
+        whole[...] = by_columns(hid[i], weight(2)).reshape(2, rows, model)
+        part_share(i).wait_send()
+        pb[i] = whole[1 - k].astype(BF)
+        ysum[i] = whole[k].astype(BF)
+        result_share(i).start()
+        return 0
+
+    lax.fori_loop(0, 4, result, 0)
+
+    for one in gate_rings:
+        one.middle()
+    gradient(w.at[1], h2_t, up_back)
+    last = pltpu.make_async_copy(w.at[1], up_grad, ls.at[0])
+    last.start()
+    rest.append(last)
     across.wait()
     block = dxl.at[k, 1 - t]
     rest.append(send(block, block, gs.at[2], gr.at[2], me.sibling))
-    gradient(1, h2_t, up_back)
-    outs.append(gradient_out(1))
     for i in range(4):
         result_share(i).wait()
         ysum[i] = (ysum[i].astype(F32) + ry[i].astype(F32)).astype(BF)
         hidden_share(i).wait_send()
-        part_share(i).wait_send()
     for i in (1, 2, 3):
         hidden_copy(i).wait_send()
         part_copy(i).wait_send()
-    for copy in downs_back:
+    for half in (0, 1):
+        down_sum[half] = down_rings[half].finish().astype(BF)
+    for half in (0, 1):
+        gate_sum[half] = gate_rings[half].finish().astype(BF)
+    for copy in rest:
         copy.wait()
-    for half in (0, 1):
-        mine = w[2, :, z, 0] if half == 0 else w[2, y, :, 1]
-        total = mine.astype(F32)
-        for j in range(3):
-            total = total + pd[half, j].astype(F32)
-        down_sum[half] = total.astype(BF)
-    for copy in rest + outs:
-        copy.wait()
-
-
-def block(part, tok, gain, dy, gate, halves):
+
+
+def block(part, tok, gain, dy, halves):
     rows, model = tok.shape
-    hidden = gate.shape[-1]
+    half_rows, hidden = halves.shape[-2:]
     sums = halves.shape[1:]
+    weights = (3, 4, 4, 2, half_rows, hidden)
     any_place = pl.BlockSpec(memory_space=pl.ANY)
     quarter = pltpu.VMEM((4, rows, model), BF)
     inner = pltpu.VMEM((4, 2 * rows, hidden), BF)
-    turned = pltpu.VMEM((model, 8 * rows), BF)
+    flipped = pltpu.VMEM((model, 8 * rows), BF)
     return pl.pallas_call(
         block_kernel,
         out_shape=[
@@ -725,37 +790,38 @@
             shape((1, model), F32),
             shape((4, rows, model), BF),
             shape(sums, BF),
-            shape((2,) + gate.shape, BF),
+            shape(sums, BF),
+            shape(weights[1:], BF),
         ],
-        in_specs=[VM] * 3 + [any_place] * 3,
-        out_specs=[VM] * 6 + [any_place],
+        in_specs=[VM] * 3 + [any_place] * 2,
+        out_specs=[VM] * 7 + [any_place],
         scratch_shapes=[
-            pltpu.VMEM((3,) + gate.shape, BF),
+            pltpu.VMEM(weights, BF),
             pltpu.VMEM(dy.shape, BF),
-            turned,
+            flipped,
             pltpu.VMEM(dy.shape, BF),
-            turned,
+            flipped,
             inner,
             inner,
             inner,
             pltpu.VMEM((2, rows, model), F32),
-            pltpu.VMEM((2, rows, model), BF),
-            pltpu.VMEM((rows, model), BF),
-            pltpu.VMEM((rows, model), BF),
             quarter,
             quarter,
             quarter,
             pltpu.VMEM((3, rows, model), BF),
             quarter,
-            quarter,
-            pltpu.VMEM((2, 3) + sums[1:], BF),
-            DMA((2, 2, 4, 2)),
-            DMA((2, 2, 4, 2)),
-            DMA((2, 2, 4)),
-            DMA((2, 2, 4)),
-            DMA((2, 3)),
-            DMA((2, 3)),
-            DMA((8,)),
+            pltpu.VMEM((2, 2, 2, 2, half_rows, hidden), BF),
+            pltpu.VMEM((2, 2, 2, 4, half_rows, hidden), BF),
+            pltpu.VMEM(weights[1:], BF),
+            DMA((3, 2, 4, 2)),
+            DMA((3, 2, 4, 2)),
+            DMA((3, 2, 4)),
+            DMA((3, 2, 4)),
+            DMA((2, 2, 2)),
+            DMA((2, 2, 2)),
+            DMA((2, 2, 2)),
+            DMA((2, 2, 2)),
+            DMA((7,)),
             DMA((4,)),
             DMA((3,)),
             DMA((3,)),
@@ -773,16 +839,16 @@
         compiler_params=pltpu.CompilerParams(
             collective_id=3, has_side_effects=True, vmem_limit_bytes=62 << 20
         ),
-    )(part, tok, gain, dy, gate, halves)
+    )(part, tok, gain, dy, halves)
 
 
 def rear_kernel(
     heads,
-    g_hbm, down_sum, dxl, attn, q, kv, exact, lse, start_ref, ob, h1, cosines, sines, ysum, x1, dx1, tok, gain, gnf,
-    a_all, ext_all, ffn_all, down_all, out, grad,
+    g_hbm, gate_sum, down_sum, dxl, attn, q, kv, exact, lse, start_ref, ob, h1, cosines, sines, ysum, x1, dx1, tok, gain, gnf,
+    a_all, ext_all, ffn_all, out, grad,
     do, dots, acc, keep, give, arrived, sums, landed, back, part, m1, m2, m3, left_t, ga,
-    own, p1, p2, q1, sm, q2, fin, fin_d, wide, narrow, e0, e1, es, e2, y2,
-    ls, d1, d2, d3, d4, ms, fs1, fr1, fs2, fr2, as1, ar1, as2, ar2, as3, ar3, xs, xr, ss, sr, ts, tr, us, ur, ys, yr,
+    g, own, passing, got, p2, q1, sm, q2, fin, fin_w, e0, e1, es, e2, y2,
+    ls, d1, d2, d3, d4, ms, ca, cb, cc, cd, fs2, fr2, as1, ar1, as2, ar2, as3, ar3, xs, xr, ss, sr, ts, tr, ys, yr,
     gs, gr,
 ):
     me = Place()
@@ -803,49 +869,62 @@
 
     ring = [(dt, dc) for dt in (0, 1) for dc in range(4) if dt or dc]
 
-    def first_hop(w, half, j):
-        if half == 0:
-            source, device = g_hbm.at[w, :, lax.rem(z + j, 4), 0], me.along_z(j)
-        else:
-            source, device = g_hbm.at[w, lax.rem(y + j, 4), :, 1], me.along_y(j)
-        return describe(
-            source, p1.at[w, half, j - 1], fs1.at[w, half, j - 1], fr1.at[w, half, j - 1], device
-        )
+    summed_once = (gate_sum, own, down_sum)
 
     def second_hop(w, half, j):
         if half == 0:
-            source, device = own.at[w, 0, lax.rem(y + j, 4)], me.along_y(j)
+            source, device = summed_once[w].at[0, lax.rem(y + j, 4)], me.along_y(j)
         else:
-            source, device = own.at[w, 1, lax.rem(z + j, 4)], me.along_z(j)
+            source, device = summed_once[w].at[1, lax.rem(z + j, 4)], me.along_z(j)
         return describe(
             source, p2.at[w, half, j - 1], fs2.at[w, half, j - 1], fr2.at[w, half, j - 1], device
         )
 
-    def own_load(w, half):
-        source = g_hbm.at[w, :, z, 0] if half == 0 else g_hbm.at[w, y, :, 1]
-        return pltpu.make_async_copy(source, own.at[w, half], ls.at[w, half])
-
-    def start_hop(half, *span):
-        def some(w, _):
-            for j in offsets:
-                first_hop(w, half, j).start()
-            own_load(w, half).start()
-            return 0
-
-        lax.fori_loop(*span, some, 0)
-
+    def second_hops(w, half):
+        for j in offsets:
+            second_hop(w, half, j).start()
+
+    def up_along_z(position, piece, count):
+        return g.at[pl.ds(piece, count), position, 0]
+
+    def up_along_y(position, piece, count):
+        return g.at[position, pl.ds(piece, count), 1]
+
+    up_rings = [
+        RingSum(
+            along,
+            position,
+            source,
+            passing.at[half],
+            got.at[half],
+            [sem.at[half] for sem in (ca, cb, cc, cd)],
+        )
+        for half, (along, position, source) in enumerate(
+            ((me.along_z, z, up_along_z), (me.along_y, y, up_along_y))
+        )
+    ]
+
+    def up_end(half):
+        own[half] = up_rings[half].finish().astype(BF)
+        second_hops(1, half)
+
+    def early():
+        for one in up_rings:
+            one.middle()
+
+    load = pltpu.make_async_copy(g_hbm, g, ls)
+    load.start()
     greet(
         [me.along_z(j) for j in (1, 2, 3)]
         + [me.along_y(j) for j in (1, 2, 3)]
         + [in_x(dt, dc) for dt, dc in ring]
         + [{"fsdp": y * 4 + lax.rem(z + j, 4), "ctx": (1 - lo) * 2 + k} for j in (1, 2, 3)]
     )
-    own[2] = down_sum[...]
-    for half in (0, 1):
-        for j in offsets:
-            second_hop(2, half, j).start()
-    start_hop(1, 0, 2)
-    start_hop(0, 0, 1)
+    load.wait()
+    for one in up_rings:
+        one.start()
+    second_hops(0, 0)
+    second_hops(2, 0)
     near = [(1 - lo, t), (1 - lo, 1 - t), (lo, 1 - t)]
     results = [
         send(ysum.at[i + 1], y2.at[i], ys.at[i], yr.at[i], me.in_ring(*near[i])) for i in range(3)
@@ -887,6 +966,10 @@
 
         @pl.when(b > 0)
         def _():
+            @pl.when(b == 2)
+            def _():
+                early()
+
             core_share(b - 1).wait_recv()
             sums[b - 1] = (keep[b - 1] + arrived[b - 1]).astype(BF)
             home(b - 1).start()
@@ -894,7 +977,23 @@
         return 0
 
     lax.fori_loop(0, index + 1, step, 0)
-    start_hop(0, 1, 2)
+
+    @pl.when(index < 2)
+    def _():
+        early()
+
+    second_hops(0, 1)
+    second_hops(2, 1)
+
+    result = x1[...] + ysum[0].astype(F32)
+    for i in range(3):
+        results[i].wait()
+        result = result + y2[i].astype(F32)
+    out[t] = result.astype(BF)
+    mine = out.at[t]
+    rest = [send(mine, mine, gs.at[1], gr.at[1], me.in_ring(lo, 1 - t))]
+    up_end(1)
+    up_end(0)
 
     scale = 1.0 / math.sqrt(size)
     for h in range(heads):
@@ -949,6 +1048,32 @@
     cores.wait()
     m2[...] = (part[k, 1 - t].astype(F32) + m1[1 - t].astype(F32)).astype(BF)
     across = send(m2, m3, ms.at[2], ms.at[3], me.in_ring(lo, 1 - t))
+    quarter = sm.shape[2] // 2
+
+    def summed(w, half):
+        for j in offsets:
+            second_hop(w, half, j).wait()
+        here = summed_once[w][0, y] if half == 0 else summed_once[w][1, z]
+        total = here.astype(F32)
+        for j in range(3):
+            total = total + p2[w, half, j].astype(F32)
+        return total
+
+    def to_owners(w):
+        for half in (0, 1):
+            total = summed(w, half)
+            fin_w[w, 2 * half] = total[:quarter]
+            fin_w[w, 2 * half + 1] = total[quarter:]
+        ffn_all[w, c] = fin_w[w, c]
+        return [
+            send(
+                fin_w.at[w, lax.rem(c + j, 4)], ffn_all.at[w, c], ts.at[w, j - 1], tr.at[w, j - 1], in_x(0, j)
+            )
+            for j in (2, 1, 3)
+        ]
+
+    rest += to_owners(2) + to_owners(0) + to_owners(1)
+
     x = tok[...].astype(F32)
     factor = lax.rsqrt(jnp.mean(x * x, axis=-1, keepdims=True) + epsilon)
     normed = x * factor
@@ -964,66 +1089,8 @@
     ]
     grad[t] = (dx1[...] + norm_back(dh1 * gain[...], normed, factor)).astype(BF)
     mine = grad.at[t]
-    rest = [send(mine, mine, gs.at[0], gr.at[0], me.in_ring(lo, 1 - t))]
-
-    quarter = sm.shape[2] // 2
-
-    def summed(w, half):
-        for j in offsets:
-            second_hop(w, half, j).wait()
-        here = own[w, 0, y] if half == 0 else own[w, 1, z]
-        total = here.astype(F32)
-        for j in range(3):
-            total = total + p2[w, half, j].astype(F32)
-        return total
-
-    for half in (0, 1):
-        total = summed(2, half)
-        fin_d[2 * half] = total[:quarter]
-        fin_d[2 * half + 1] = total[quarter:]
-    down_all[c] = fin_d[c]
-    rest += [
-        send(fin_d.at[lax.rem(c + j, 4)], down_all.at[c], us.at[j - 1], ur.at[j - 1], in_x(0, j))
-        for j in (2, 1, 3)
-    ]
-
-    result = x1[...] + ysum[0].astype(F32)
-    for i in range(3):
-        results[i].wait()
-        result = result + y2[i].astype(F32)
-    out[t] = result.astype(BF)
-    mine = out.at[t]
-    rest.append(send(mine, mine, gs.at[1], gr.at[1], me.in_ring(lo, 1 - t)))
-
-    for copy in small:
-        copy.wait()
-    es[...] = (e0[...] + e1[0]) + (e1[1] + e1[2])
-    small = [
-        send(es, e2.at[j - 1], ss.at[1, j - 1], sr.at[1, j - 1], me.along_y(j)) for j in offsets
-    ]
-
-    def first_sum(w, _):
-        for half in (0, 1):
-            own_load(w, half).wait()
-            for j in offsets:
-                first_hop(w, half, j).wait()
-            total = own[w, half].astype(F32)
-            for j in range(3):
-                total = total + p1[w, half, j].astype(F32)
-            own[w, half] = total.astype(BF)
-            for j in offsets:
-                second_hop(w, half, j).start()
-        return 0
-
-    lax.fori_loop(0, 2, first_sum, 0)
-
-    for copy in small:
-        copy.wait()
-    ext_all[t, c] = (es[...] + e2[0]) + (e2[1] + e2[2])
-    mine = ext_all.at[t, c]
-    rest += [
-        send(mine, mine, xs.at[i], xr.at[i], in_x(dt, dc)) for i, (dt, dc) in enumerate(ring)
-    ]
+    rest.append(send(mine, mine, gs.at[0], gr.at[0], me.in_ring(lo, 1 - t)))
+
     for copy in large:
         copy.wait()
     for half in (0, 1):
@@ -1044,21 +1111,19 @@
                 sm.at[1, lax.rem(z + j, 4)], q2.at[1, j - 1], as2.at[1, j - 1], ar2.at[1, j - 1], me.along_z(j)
             )
         )
-
-    def second_sum(w, _):
-        for half in (0, 1):
-            total = summed(w, half)
-            place = pl.ds(pl.multiple_of(w * quarter, 8), quarter)
-            wide[2 * half, place] = total[:quarter]
-            wide[2 * half + 1, place] = total[quarter:]
-        return 0
-
-    lax.fori_loop(0, 2, second_sum, 0)
-    narrow[...] = wide[...].astype(BF)
-    ffn_all[c] = narrow[c]
+    for copy in small:
+        copy.wait()
+    es[...] = (e0[...] + e1[0]) + (e1[1] + e1[2])
+    small = [
+        send(es, e2.at[j - 1], ss.at[1, j - 1], sr.at[1, j - 1], me.along_y(j)) for j in offsets
+    ]
+
+    for copy in small:
+        copy.wait()
+    ext_all[t, c] = (es[...] + e2[0]) + (e2[1] + e2[2])
+    mine = ext_all.at[t, c]
     rest += [
-        send(narrow.at[lax.rem(c + j, 4)], ffn_all.at[c], ts.at[j - 1], tr.at[j - 1], in_x(0, j))
-        for j in (2, 1, 3)
+        send(mine, mine, xs.at[i], xr.at[i], in_x(dt, dc)) for i, (dt, dc) in enumerate(ring)
     ]
     for copy in last:
         copy.wait()
@@ -1089,7 +1154,7 @@
         copy.wait()
 
 
-def rear(heads, g, down_sum, dxl, attn, q, kv, exact, lse, start, ob, h1, cosines, sines, ysum, x1, dx1, tok, gain, gnf):
+def rear(heads, g, gate_sum, down_sum, dxl, attn, q, kv, exact, lse, start, ob, h1, cosines, sines, ysum, x1, dx1, tok, gain, gnf):
     rows, width = q.shape
     size = width // heads
     slice_rows, model = tok.shape
@@ -1097,16 +1162,14 @@
     total = attn.shape[1]
     half_rows = model // 32
     quarter = half_rows // 2
-    packed = 2 * quarter
     shared = pltpu.VMEM(kv.shape[1:], F32)
     shared_low = pltpu.VMEM(kv.shape[1:], BF)
     slab = pltpu.VMEM((slice_rows, model), BF)
-    args = (down_sum, dxl, attn, q, kv, exact, lse, start, ob, h1, cosines, sines, ysum, x1, dx1, tok, gain, gnf)
+    args = (gate_sum, down_sum, dxl, attn, q, kv, exact, lse, start, ob, h1, cosines, sines, ysum, x1, dx1, tok, gain, gnf)
     outs = [
         shape((4, quarter, total), F32),
         shape((2, 4, 8, model), F32),
-        shape((4, packed, hidden), BF),
-        shape((4, quarter, hidden), F32),
+        shape((3, 4, quarter, hidden), F32),
         shape((2, slice_rows, model), BF),
         shape((2, slice_rows, model), BF),
     ]
@@ -1131,29 +1194,31 @@
             slab,
             pltpu.VMEM((model, rows), BF),
             pltpu.VMEM((4, 4, 2, half_rows, total), BF),
-            pltpu.VMEM((3, 2, 4, half_rows, hidden), BF),
-            pltpu.VMEM((2, 2, 3, 4, half_rows, hidden), BF),
+            pltpu.VMEM(g.shape, BF),
+            pltpu.VMEM((2, 4, half_rows, hidden), BF),
+            pltpu.VMEM((2, 2, 2, half_rows, hidden), BF),
+            pltpu.VMEM((2, 2, 4, half_rows, hidden), BF),
             pltpu.VMEM((3, 2, 3, half_rows, hidden), BF),
             pltpu.VMEM((2, 3, 4, half_rows, total), BF),
             pltpu.VMEM((2, 4, half_rows, total), BF),
             pltpu.VMEM((2, 3, half_rows, total), BF),
             pltpu.VMEM((4, quarter, total), F32),
-            pltpu.VMEM((4, quarter, hidden), F32),
-            pltpu.VMEM((4, packed, hidden), F32),
-            pltpu.VMEM((4, packed, hidden), BF),
+            pltpu.VMEM((3, 4, quarter, hidden), F32),
             pltpu.VMEM((8, model), F32),
             pltpu.VMEM((3, 8, model), F32),
             pltpu.VMEM((8, model), F32),
             pltpu.VMEM((3, 8, model), F32),
             pltpu.VMEM((3, slice_rows, model), BF),
-            DMA((2, 2)),
+            DMA,
             DMA((8,)),
             DMA((8,)),
             DMA((8,)),
             DMA((8,)),
             DMA((4,)),
-            DMA((2, 2, 3)),
-            DMA((2, 2, 3)),
+            DMA((2, 2)),
+            DMA((2, 2)),
+            DMA((2, 2)),
+            DMA((2, 2)),
             DMA((3, 2, 3)),
             DMA((3, 2, 3)),
             DMA((2, 3)),
@@ -1166,10 +1231,8 @@
             DMA((7,)),
             DMA((2, 3)),
             DMA((2, 3)),
-            DMA((3,)),
-            DMA((3,)),
-            DMA((3,)),
-            DMA((3,)),
+            DMA((3, 3)),
+            DMA((3, 3)),
             DMA((3,)),
             DMA((3,)),
             DMA((2,)),
@@ -1215,16 +1278,15 @@
     padded = -(-hidden // 128) * 128
 
     def hidden_slice(w, axis):
-        return lax.dynamic_slice_in_dim(w, c * hidden, hidden, axis)
-
-    def widened(w):
-        return jnp.pad(w, ((0, 0), (0, padded - hidden)))
+        widths = [(0, 0), (0, 0)]
+        widths[axis] = (0, 4 * padded - 4 * hidden)
+        return lax.dynamic_slice_in_dim(jnp.pad(w, widths), c * padded, padded, axis)
 
     own_ffn = jnp.stack(
         [
-            widened(hidden_slice(w_gate, 1)),
-            widened(hidden_slice(w_up, 1)),
-            widened(hidden_slice(w_down, 0).T),
+            hidden_slice(w_gate, 1),
+            hidden_slice(w_up, 1),
+            hidden_slice(w_down, 0).T,
         ]
     )
 
@@ -1251,7 +1313,6 @@
     ).astype(F32)[None]
     (
         attn_all,
-        gate_all,
         halves,
         dy_all,
         h1,
@@ -1265,12 +1326,13 @@
         sines,
         part,
     ) = front(heads, own_attn, own_ffn, tokens, cotangent, segments, gain_attn, bias, frequency)
-    x1, dx1, dxl, grad_norm_two, ysum, down_sum, ffn_grads = block(
-        part, own_tokens, gain_ffn, dy_all, gate_all, halves
+    x1, dx1, dxl, grad_norm_two, ysum, gate_sum, down_sum, up_grad = block(
+        part, own_tokens, gain_ffn, dy_all, halves
     )
-    a_all, ext_all, ffn_all, down_all, output, grad_tokens = rear(
+    a_all, ext_all, ffn_all, output, grad_tokens = rear(
         heads,
-        ffn_grads,
+        up_grad,
+        gate_sum,
         down_sum,
         dxl.reshape(rows, model),
         attn_all.reshape(model, own_width + query_width),
@@ -1294,7 +1356,7 @@
     a_all = a_all[:2] + a_all[2:]
 
     def side_by_side(pieces):
-        return jnp.concatenate([pieces[i, :, :hidden].astype(F32) for i in range(4)], axis=1)
+        return jnp.concatenate([pieces[i] for i in range(4)], axis=1)[:, : 4 * hidden]
 
     owner = f * 4 + c
     norms = lax.dynamic_slice_in_dim(
@@ -1315,9 +1377,9 @@
         jnp.concatenate([a_all[0, :, own_width:], a_all[1, :, own_width:]], axis=1).T,
         norms[0],
         norms[1],
-        side_by_side(ffn_all[:, :owner_rows]),
-        side_by_side(ffn_all[:, owner_rows:]),
-        side_by_side(down_all).T,
+        side_by_side(ffn_all[0]),
+        side_by_side(ffn_all[1]),
+        side_by_side(ffn_all[2]).T,
     )
 
 

time: 308 us -> 290 us (0.942)
  Pallas kernels: 283 us -> 267 us
    pallas_call x1, Pallas kernels: 72.1 us -> 54.8 us  [front(): pl.pallas_call(functools.partial(front_kernel, heads), out_shape=outs, in...]
    pallas_call x1, Pallas kernels: 101 us -> 115 us  [block(): pl.pallas_call(block_kernel, out_shape=[shape((rows, model), F32), shape(...]
    pallas_call x1, Pallas kernels: 109 us -> 97.1 us  [rear(): pl.pallas_call(functools.partial(rear_kernel, heads), out_shape=outs, in_...]
where the time goes in v3:
time: 290 us
  Pallas kernels  267 us (92%)
  local copies, waits for them, and re-layouts  11.6 us (4%)
  other arithmetic  10.3 us (4%)
    pallas_call x1, Pallas kernels, block(): pl.pallas_call(block_kernel, out_shape=[shape((rows, model), F32), shape(...  115 us
    pallas_call x1, Pallas kernels, rear(): pl.pallas_call(functools.partial(rear_kernel, heads), out_shape=outs, in_...  97.1 us
    pallas_call x1, Pallas kernels, front(): pl.pallas_call(functools.partial(front_kernel, heads), out_shape=outs, in...  54.8 us

profile of v3, /device:TPU:1, one launch (start us, length us, event | category | flops | bytes accessed | tf_op | source)
XLA Modules:
  0.0 289.8 jit_solution(13579558928530546621)
XLA Ops:
  0.6 0.0 copy-start
  0.7 0.0 copy-start.2
  0.7 0.9 copy-done
  1.6 0.9 dynamic-slice_bitcast_fusion
  2.5 0.7 broadcast_select_fusion
  3.2 0.7 pad_maximum_fusion.10.w
  3.9 0.8 dynamic_slice.36
  4.7 0.7 fusion.4
  5.3 0.6 maximum_convert_fusion.bias
  5.9 1.1 fusion.1
  7.0 0.0 copy-start.6
  7.0 0.0 copy-done.2
  7.1 0.9 pad_maximum_fusion.ffn
  8.0 0.0 copy-done.6
  8.0 0.0 copy-start.1
  8.0 0.6 reshape.109.gain
  8.6 0.6 maximum_bitcast_fusion.1.frequency
  9.2 0.0 copy-start.7
  9.2 54.8 %shard_map.254 = (bf16[4,4,96,896]{3,2,1,0:T(8,128)(2,1)}, bf16[3,2,4,48,1152]{4,3,2,1,0:T(8,128)(2,1)}, bf16[2,2,2,128,1536]{4,3,2,1,0:T(8,128)(2,1)}, bf16[512...) custom-call(bf16[96,896]{1,0:T(8,128)(2,1)} %pad_maximum_fusion.10.w, ...), custom_call_target="tpu_custom_call" | custom-call | tf_op jit(solution)/shard_map/pallas_call | solution.py:454
  64.0 0.0 copy-done.1
  64.1 0.8 constant_dynamic-slice_fusion.3.tok
  64.8 0.0 copy-done.7
  64.8 0.6 reshape.110.gain
  65.4 115.2 %shard_map.255 = (f32[128,1536]{1,0:T(8,128)}, f32[128,1536]{1,0:T(8,128)}, bf16[2,2,128,1536]{3,2,1,0:T(8,128)(2,1)}, f32[1,1536]{1,0:T(1,128)}, bf16[4,128,153...) custom-call(bf16[2,2,128,1536]{3,2,1,0:T(8,128)(2,1)} %get-tuple-ele, ...), custom_call_target="tpu_custom_call" | custom-call | tf_op jit(solution)/shard_map/pallas_call | solution.py:784
  180.7 97.1 %shard_map.256 = (f32[4,24,896]{2,1,0:T(8,128)}, f32[2,4,8,1536]{3,2,1,0:T(8,128)}, f32[3,4,24,1152]{3,2,1,0:T(8,128)}, bf16[2,128,1536]{2,1,0:T(8,128)(2,1)}, bf16[2,128,1536]{2,1,0:T(8,128)(2,1)}) custom-call(bf16[4,4,2,48,1152]{4,3,2,1,0:T(8,128)(2,1)} %get-tuple-element.43.g_hbm, bf16[2,4,48,1152]{3,2,1,0:T(8,128)(2,1)} %get-tuple-element.44.gate_sum, ...), custom_call_target="tpu_custom_call" | custom-call | tf_op jit(solution)/shard_map/pallas_call | solution.py:1176
  277.8 1.5 slice_bitcast_fusion.3
  279.2 0.0 copy-start.5
  279.2 0.8 fusion
  280.0 0.0 copy-start.4
  280.0 0.8 pad_maximum_fusion.4
  280.8 0.8 pad_maximum_fusion.7
  281.6 0.0 copy-done.5
  281.6 0.0 copy-start.3
  281.7 0.6 maximum_bitcast_fusion
  282.3 0.6 pad_maximum_fusion.11
  282.9 0.0 copy-done.4
  282.9 1.4 bitcast_convert_fusion
  284.3 0.6 slice_bitcast_fusion.16
  284.9 0.9 slice.131
  285.9 0.1 constant_dynamic-slice_fusion
  285.9 0.1 copy.29
  286.1 0.6 reshape.108
  286.7 0.6 dynamic-slice_bitcast_fusion.1
  287.3 1.0 slice_reduce_fusion
  288.3 0.1 constant_dynamic-slice_fusion.2
  288.4 0.5 slice_bitcast_fusion.18
  288.9 0.0 copy-done.3
  288.9 0.9 copy.31
  (7 shorter events, 0.1 us)
Async XLA Ops:
  0.6 0.9 copy-start
  0.7 6.4 %copy-start.2 = (bf16[4480,96]{0,1:T(8,128)(2,1)S(1)}, bf16[4480,96]{0,1:T(8,128)(2,1)}, u32[]{:S(2)}) copy-start(bf16[4480,96]{0,1:T(8,128)(2,1)} %param.28) | copy-start | bytes 2580484
  7.0 1.0 copy-start.6
  8.0 56.1 %copy-start.1 = (bf16[256,1536]{1,0:T(8,128)(2,1)S(1)}, bf16[256,1536]{1,0:T(8,128)(2,1)}, u32[]{:S(2)}) copy-start(bf16[256,1536]{1,0:T(8,128)(2,1)} %tok.1) | copy-start | bytes 2359300
  9.2 55.6 %copy-start.7 = (bf16[1536]{0:T(1024)(128)(2,1)S(1)}, bf16[1536]{0:T(1024)(128)(2,1)}, u32[]{:S(2)}) copy-start(bf16[1536]{0:T(1024)(128)(2,1)} %param.25) | copy-start | bytes 9220
  279.2 2.4 copy-start.5
  280.0 2.9 %copy-start.4 = (bf16[2,128,1536]{2,1,0:T(8,128)(2,1)S(1)}, bf16[2,128,1536]{2,1,0:T(8,128)(2,1)}, u32[]{:S(2)}) copy-start(bf16[2,128,1536]{2,1,0:T(8,128)(2,1)} %get-tuple-element.62) | copy-start | bytes 2359300
  281.6 7.3 %copy-start.3 = (bf16[2,128,1536]{2,1,0:T(8,128)(2,1)S(1)}, bf16[2,128,1536]{2,1,0:T(8,128)(2,1)}, u32[]{:S(2)}) copy-start(bf16[2,128,1536]{2,1,0:T(8,128)(2,1)} %get-tuple-element.61) | copy-start | bytes 2359300

commit v4 on v3

--- a/solution.py
+++ b/solution.py
@@ -3,6 +3,7 @@
 
 import jax
 import jax.numpy as jnp
+import numpy as np
 from jax import lax
 from jax.experimental import pallas as pl
 from jax.experimental.pallas import tpu as pltpu
@@ -193,9 +194,9 @@
 def front_kernel(
     heads,
     w, ffn, tok, dy, segments, gain, bias, frequency,
-    w_all, halves, dy_all, h1, q, kv, exact, ob, lse, starts, cosines, sines, part,
-    tok2, top, total, acc,
-    s1, r1, wa, wb, wc, wd, s3, r3, ts, tr, ds, dr, fs, fr, ks, kr, cs, cr,
+    w_out, halves, dy_all, h1_out, q, kv_out, exact, ob, lse, starts, cosines, sines, part,
+    w_all, h1, kv, tok2, top, total, acc,
+    s1, r1, wa, wb, wc, wd, s3, r3, ts, tr, ds, dr, fs, fr, ks, kr, cs, cr, ls, os,
 ):
     me = Place()
     y, z, lo, k, t = me.y, me.z, me.lo, me.k, me.t
@@ -263,8 +264,12 @@
         for h in (0, 1)
     ]
     w_all[y, z] = w[...]
-    for h in (0, 1):
-        dy_all[lo, h, k] = dy[pl.ds(h * slab, slab)]
+    stores = [
+        pltpu.make_async_copy(dy.at[pl.ds(h * slab, slab)], dy_all.at[lo, h, k], os.at[h])
+        for h in (0, 1)
+    ]
+    for copy in stores:
+        copy.start()
 
     first = pl.multiple_of(index * rows, rows)
     everyone = segments[pl.ds(y, 1), :]
@@ -313,11 +318,18 @@
         for half in (0, 1):
             for j in offsets:
                 ffn_hop(i, half, j).start()
-            halves[i, half, z if half == 0 else y] = ffn[i, parts[half]]
+            there = halves.at[i, half, z if half == 0 else y]
+            copy = pltpu.make_async_copy(ffn.at[i, parts[half]], there, ls.at[i, half])
+            copy.start()
+            stores.append(copy)
 
     ffn_hops(0)
     for ring in rings:
         ring.finish()
+    for i, (source, there) in enumerate(((w_all, w_out), (h1, h1_out))):
+        copy = pltpu.make_async_copy(source, there, os.at[2 + i])
+        copy.start()
+        stores.append(copy)
 
     inward = w_all[:, :, :, :rowed].reshape(model, rowed)
     linear = plain(h1[...], inward) + bias[...]
@@ -395,6 +407,9 @@
         return 0
 
     lax.fori_loop(0, index + 1, step, 0)
+    copy = pltpu.make_async_copy(kv, kv_out, os.at[4])
+    copy.start()
+    stores.append(copy)
     lse[...] = jnp.zeros_like(lse)
     for h in range(heads):
         sums = total[h : h + 1]
@@ -424,7 +439,7 @@
         for half in (0, 1):
             for j in offsets:
                 ffn_hop(i, half, j).wait()
-    for copy in rest:
+    for copy in rest + stores:
         copy.wait()
 
 
@@ -435,6 +450,7 @@
     rows = 2 * count
     width = bias.shape[1] - frequency.shape[1]
     size = frequency.shape[1]
+    far = pl.BlockSpec(memory_space=pl.ANY)
     args = (w, ffn, tok, dy, segments, gain, bias, frequency)
     outs = [
         shape((4, 4, shard, total), BF),
@@ -455,8 +471,11 @@
         functools.partial(front_kernel, heads),
         out_shape=outs,
         in_specs=[VM] * len(args),
-        out_specs=[VM] * len(outs),
+        out_specs=[far] * 4 + [VM, far] + [VM] * (len(outs) - 6),
         scratch_shapes=[
+            pltpu.VMEM((4, 4, shard, total), BF),
+            pltpu.VMEM((rows, model), BF),
+            pltpu.VMEM((2, 8, rows, size), BF),
             pltpu.VMEM((count, model), BF),
             pltpu.VMEM((8, rows), F32),
             pltpu.VMEM((8, rows), F32),
@@ -479,6 +498,8 @@
             DMA((8,)),
             DMA((8,)),
             DMA((8,)),
+            DMA((3, 2)),
+            DMA((5,)),
         ],
         compiler_params=pltpu.CompilerParams(
             collective_id=1, has_side_effects=True, vmem_limit_bytes=56 << 20
@@ -567,6 +588,7 @@
         return w[i].reshape(model, inner)
 
     gather_start(0)
+    gather_start(1)
     loads[0].wait()
 
     def turn_dy(i, _):
@@ -580,7 +602,6 @@
     lax.fori_loop(0, 4, turn_dy, 0)
     x = tok[...].astype(F32) + part[k, t].astype(F32) + m1[t].astype(F32)
     gather_forward(0)
-    gather_start(1)
     across.wait()
     x = x + m3[...].astype(F32)
     x1[...] = x
@@ -738,6 +759,9 @@
     block = dxl.at[k, t]
     across = send(block, block, gs.at[0], gr.at[0], me.in_ring(lo, 1 - t))
     rest = [send(block, block, gs.at[1], gr.at[1], me.sibling)]
+    for one in gate_rings:
+        one.middle()
+
     def result(i, _):
         whole[...] = by_columns(hid[i], weight(2)).reshape(2, rows, model)
         part_share(i).wait_send()
@@ -748,8 +772,6 @@
 
     lax.fori_loop(0, 4, result, 0)
 
-    for one in gate_rings:
-        one.middle()
     gradient(w.at[1], h2_t, up_back)
     last = pltpu.make_async_copy(w.at[1], up_grad, ls.at[0])
     last.start()
@@ -844,13 +866,17 @@
 
 def rear_kernel(
     heads,
-    g_hbm, gate_sum, down_sum, dxl, attn, q, kv, exact, lse, start_ref, ob, h1, cosines, sines, ysum, x1, dx1, tok, gain, gnf,
-    a_all, ext_all, ffn_all, out, grad,
-    do, dots, acc, keep, give, arrived, sums, landed, back, part, m1, m2, m3, left_t, ga,
-    g, own, passing, got, p2, q1, sm, q2, fin, fin_w, e0, e1, es, e2, y2,
+    lse, start_ref, cosines, sines, tok, gain, gnf, *more,
+):
+    far, outs, near_refs, rest_refs = more[:13], more[13:19], more[19:32], more[32:]
+    a_all, norm_sum, bias_sum, ffn_all, out, grad = outs
+    g, gate_sum, down_sum, ysum, dxl, attn, exact, q, kv, x1, ob, h1, dx1 = near_refs
+    (
+    ext_all, do, dots, acc, keep, give, arrived, sums, landed, back, part, m1, m2, m3, left_t, ga,
+    own, passing, got, p2, q1, sm, q2, fin, fin_w, e0, e1, es, e2, y2,
     ls, d1, d2, d3, d4, ms, ca, cb, cc, cd, fs2, fr2, as1, ar1, as2, ar2, as3, ar3, xs, xr, ss, sr, ts, tr, ys, yr,
     gs, gr,
-):
+    ) = rest_refs
     me = Place()
     y, z, lo, k, t = me.y, me.z, me.lo, me.k, me.t
     c = lo * 2 + k
@@ -912,24 +938,33 @@
         for one in up_rings:
             one.middle()
 
-    load = pltpu.make_async_copy(g_hbm, g, ls)
-    load.start()
+    loads = [
+        pltpu.make_async_copy(source, target, ls.at[i])
+        for i, (source, target) in enumerate(zip(far, near_refs, strict=True))
+    ]
+    for copy in loads:
+        copy.start()
     greet(
         [me.along_z(j) for j in (1, 2, 3)]
         + [me.along_y(j) for j in (1, 2, 3)]
         + [in_x(dt, dc) for dt, dc in ring]
         + [{"fsdp": y * 4 + lax.rem(z + j, 4), "ctx": (1 - lo) * 2 + k} for j in (1, 2, 3)]
     )
-    load.wait()
+    loads[0].wait()
     for one in up_rings:
         one.start()
-    second_hops(0, 0)
-    second_hops(2, 0)
+    for copy in loads[1:4]:
+        copy.wait()
+    for half in (0, 1):
+        second_hops(0, half)
+        second_hops(2, half)
     near = [(1 - lo, t), (1 - lo, 1 - t), (lo, 1 - t)]
     results = [
         send(ysum.at[i + 1], y2.at[i], ys.at[i], yr.at[i], me.in_ring(*near[i])) for i in range(3)
     ]
 
+    for copy in loads[4:9]:
+        copy.wait()
     do[...] = plain(dxl[...], attn[:, rowed:]).astype(BF)
     for h in range(heads):
         product = exact[h] * do[:, h * size : (h + 1) * size].astype(F32).T
@@ -982,9 +1017,9 @@
     def _():
         early()
 
-    second_hops(0, 1)
-    second_hops(2, 1)
-
+
+    for copy in loads[9:]:
+        copy.wait()
     result = x1[...] + ysum[0].astype(F32)
     for i in range(3):
         results[i].wait()
@@ -1064,10 +1099,12 @@
             total = summed(w, half)
             fin_w[w, 2 * half] = total[:quarter]
             fin_w[w, 2 * half + 1] = total[quarter:]
-        ffn_all[w, c] = fin_w[w, c]
+        width = fin_w.shape[3]
+        place = pl.ds(pl.multiple_of(c * width, 128), width)
+        ffn_all[w, :, place] = fin_w[w, c]
         return [
             send(
-                fin_w.at[w, lax.rem(c + j, 4)], ffn_all.at[w, c], ts.at[w, j - 1], tr.at[w, j - 1], in_x(0, j)
+                fin_w.at[w, lax.rem(c + j, 4)], ffn_all.at[w, :, place], ts.at[w, j - 1], tr.at[w, j - 1], in_x(0, j)
             )
             for j in (2, 1, 3)
         ]
@@ -1152,6 +1189,12 @@
     lax.fori_loop(0, index + 1, sent, 0)
     for copy in rest:
         copy.wait()
+    total = ext_all[0, 0]
+    for i in range(1, 8):
+        total = total + ext_all[i // 4, i % 4]
+    norm_sum[...] = total
+    for core in (0, 1):
+        bias_sum[core] = ext_all[t, core] + ext_all[t, 2 + core]
 
 
 def rear(heads, g, gate_sum, down_sum, dxl, attn, q, kv, exact, lse, start, ob, h1, cosines, sines, ysum, x1, dx1, tok, gain, gnf):
@@ -1165,20 +1208,24 @@
     shared = pltpu.VMEM(kv.shape[1:], F32)
     shared_low = pltpu.VMEM(kv.shape[1:], BF)
     slab = pltpu.VMEM((slice_rows, model), BF)
-    args = (gate_sum, down_sum, dxl, attn, q, kv, exact, lse, start, ob, h1, cosines, sines, ysum, x1, dx1, tok, gain, gnf)
+    args = (lse, start, cosines, sines, tok, gain, gnf)
+    far = (g, gate_sum, down_sum, ysum, dxl, attn, exact, q, kv, x1, ob, h1, dx1)
     outs = [
         shape((4, quarter, total), F32),
-        shape((2, 4, 8, model), F32),
-        shape((3, 4, quarter, hidden), F32),
+        shape((8, model), F32),
+        shape((2, 8, model), F32),
+        shape((3, quarter, 4 * hidden), F32),
         shape((2, slice_rows, model), BF),
         shape((2, slice_rows, model), BF),
     ]
     return pl.pallas_call(
         functools.partial(rear_kernel, heads),
         out_shape=outs,
-        in_specs=[pl.BlockSpec(memory_space=pl.ANY)] + [VM] * len(args),
+        in_specs=[VM] * len(args) + [pl.BlockSpec(memory_space=pl.ANY)] * len(far),
         out_specs=[VM] * len(outs),
-        scratch_shapes=[
+        scratch_shapes=[pltpu.VMEM(array.shape, array.dtype) for array in far]
+        + [
+            pltpu.VMEM((2, 4, 8, model), F32),
             pltpu.VMEM((rows, width), BF),
             pltpu.VMEM((8, rows), F32),
             pltpu.VMEM((heads, size, rows), F32),
@@ -1194,7 +1241,6 @@
             slab,
             pltpu.VMEM((model, rows), BF),
             pltpu.VMEM((4, 4, 2, half_rows, total), BF),
-            pltpu.VMEM(g.shape, BF),
             pltpu.VMEM((2, 4, half_rows, hidden), BF),
             pltpu.VMEM((2, 2, 2, half_rows, hidden), BF),
             pltpu.VMEM((2, 2, 4, half_rows, hidden), BF),
@@ -1209,7 +1255,7 @@
             pltpu.VMEM((8, model), F32),
             pltpu.VMEM((3, 8, model), F32),
             pltpu.VMEM((3, slice_rows, model), BF),
-            DMA,
+            DMA((13,)),
             DMA((8,)),
             DMA((8,)),
             DMA((8,)),
@@ -1241,7 +1287,7 @@
         compiler_params=pltpu.CompilerParams(
             collective_id=7, has_side_effects=True, vmem_limit_bytes=62 << 20
         ),
-    )(g, *args)
+    )(*args, *far)
 
 
 def shards(
@@ -1301,8 +1347,8 @@
     own_tokens = lax.dynamic_slice_in_dim(tokens, t * slice_rows, slice_rows, 0)
     rows = 2 * count
     half_size = size // 2
-    frequency = jnp.exp(jnp.arange(half_size, dtype=F32) * (-2.0 * math.log(rope_base) / size))
-    frequency = jnp.concatenate([frequency, frequency])[None]
+    frequency = np.exp(np.arange(half_size) * (-2.0 * math.log(rope_base) / size))
+    frequency = jnp.asarray(np.concatenate([frequency, frequency])[None].astype(np.float32))
     gain_attn = norm_attn.astype(F32)[None]
     gain_ffn = norm_ffn.astype(F32)[None]
     bias = jnp.concatenate(
@@ -1329,7 +1375,7 @@
     x1, dx1, dxl, grad_norm_two, ysum, gate_sum, down_sum, up_grad = block(
         part, own_tokens, gain_ffn, dy_all, halves
     )
-    a_all, ext_all, ffn_all, output, grad_tokens = rear(
+    a_all, norm_sum, bias_sum, ffn_all, output, grad_tokens = rear(
         heads,
         up_grad,
         gate_sum,
@@ -1355,15 +1401,9 @@
     owner_rows = shard_rows // 4
     a_all = a_all[:2] + a_all[2:]
 
-    def side_by_side(pieces):
-        return jnp.concatenate([pieces[i] for i in range(4)], axis=1)[:, : 4 * hidden]
-
     owner = f * 4 + c
-    norms = lax.dynamic_slice_in_dim(
-        jnp.sum(ext_all[:, :, :2].reshape(8, 2, model), axis=0), owner * owner_rows, owner_rows, 1
-    )
-    biases = lax.dynamic_index_in_dim(ext_all[:, :, 2, :own_width], t, 0, keepdims=False)
-    biases = (biases[:2] + biases[2:]).reshape(2, heads + 1, size)
+    norms = lax.dynamic_slice_in_dim(norm_sum[:2], owner * owner_rows, owner_rows, 1)
+    biases = bias_sum[:, 2, :own_width].reshape(2, heads + 1, size)
     biases = lax.dynamic_slice_in_dim(biases, owner * 2, 2, 2)
     return (
         output.reshape(count, model),
@@ -1377,9 +1417,9 @@
         jnp.concatenate([a_all[0, :, own_width:], a_all[1, :, own_width:]], axis=1).T,
         norms[0],
         norms[1],
-        side_by_side(ffn_all[0]),
-        side_by_side(ffn_all[1]),
-        side_by_side(ffn_all[2]).T,
+        ffn_all[0, :, : 4 * hidden],
+        ffn_all[1, :, : 4 * hidden],
+        ffn_all[2, :, : 4 * hidden].T,
     )
 
 

time: 290 us -> 273 us (0.941)
  Pallas kernels: 267 us -> 252 us
  other arithmetic: 10.3 us -> 7.35 us
    pallas_call x1, Pallas kernels: 115 us -> 108 us  [block(): pl.pallas_call(block_kernel, out_shape=[shape((rows, model), F32), shape(...]
    pallas_call x1, Pallas kernels: 54.8 us -> 51 us  [front(): pl.pallas_call(functools.partial(front_kernel, heads), out_shape=outs, in...]
    pallas_call x1, Pallas kernels: 97.1 us -> 93.3 us  [rear(): pl.pallas_call(functools.partial(rear_kernel, heads), out_shape=outs, in_...]
where the time goes in v4:
time: 273 us; the launch traced here: 272 us
  Pallas kernels  252 us (92%)
  local copies, waits for them, and re-layouts  11.8 us (4%)
  other arithmetic  7.35 us (3%)
    pallas_call x1, Pallas kernels, block(): pl.pallas_call(block_kernel, out_shape=[shape((rows, model), F32), shape(...  108 us
    pallas_call x1, Pallas kernels, rear(): pl.pallas_call(functools.partial(rear_kernel, heads), out_shape=outs, in_...  93.3 us
    pallas_call x1, Pallas kernels, front(): pl.pallas_call(functools.partial(front_kernel, heads), out_shape=outs, in...  51 us

profile of v4, /device:TPU:1, one launch (start us, length us, event | category | flops | bytes accessed | tf_op | source)
XLA Modules:
  0.0 271.9 jit_solution(5151285791098629890)
XLA Ops:
  0.6 0.0 copy-start
  0.7 0.0 copy-start.3
  0.7 0.9 copy-done
  1.6 0.9 dynamic-slice_bitcast_fusion
  2.5 0.7 broadcast_select_fusion
  3.2 0.7 pad_maximum_fusion.1.w
  3.9 0.8 dynamic_slice.32
  4.7 0.7 fusion.3
  5.3 0.6 maximum_convert_fusion.bias
  5.9 1.1 fusion
  7.0 0.0 copy-start.6
  7.0 0.0 copy-done.3
  7.1 0.9 pad_maximum_fusion.ffn
  8.0 0.0 copy-done.6
  8.0 0.0 copy-start.1
  8.0 0.6 reshape.76.gain
  8.6 0.0 copy-start.7
  8.6 51.0 %shard_map.263 = (bf16[4,4,96,896]{3,2,1,0:T(8,128)(2,1)}, bf16[3,2,4,48,1152]{4,3,2,1,0:T(8,128)(2,1)}, bf16[2,2,2,128,1536]{4,3,2,1,0:T(8,128)(2,1)}, bf16[512...) custom-call(bf16[96,896]{1,0:T(8,128)(2,1)} %pad_maximum_fusion.1.w,, ...), custom_call_target="tpu_custom_call" | custom-call | tf_op jit(solution)/shard_map/pallas_call | solution.py:470
  59.6 0.0 copy-done.1
  59.6 0.8 constant_dynamic-slice_fusion.3.tok
  60.3 0.0 copy-done.7
  60.3 0.6 reshape.77.gain
  60.9 107.7 %shard_map.264 = (f32[128,1536]{1,0:T(8,128)}, f32[128,1536]{1,0:T(8,128)}, bf16[2,2,128,1536]{3,2,1,0:T(8,128)(2,1)}, f32[1,1536]{1,0:T(1,128)}, bf16[4,128,153...) custom-call(bf16[2,2,128,1536]{3,2,1,0:T(8,128)(2,1)} %get-tuple-ele, ...), custom_call_target="tpu_custom_call" | custom-call | tf_op jit(solution)/shard_map/pallas_call | solution.py:806
  168.6 93.3 %shard_map.265 = (f32[4,24,896]{2,1,0:T(8,128)}, f32[8,1536]{1,0:T(8,128)}, f32[2,8,1536]{2,1,0:T(8,128)}, f32[3,24,4608]{2,1,0:T(8,128)}, bf16[2,128,1536]{2,1,0:T(8,128)(2,1)}, /*index=5*/bf16[2,128,1536]{2,1,0:T(8,128)(2,1)}) custom-call(f32[8,512]{1,0:T(8,128)} %get-tuple-element.41.lse, s32[1,512]{1,0:T(1,128)} %get-tuple-element.42.start_ref, ...), custom_call_target="tpu_custom_call" | custom-call | tf_op jit(solution)/shard_map/pallas_call | solution.py:1221
  262.0 0.0 copy-start.5
  262.0 1.1 slice_add_fusion
  263.1 0.0 copy-start.2
  263.1 0.6 maximum_bitcast_fusion
  263.8 0.6 pad_maximum_fusion.2
  264.4 0.0 copy-done.5
  264.4 1.4 bitcast_convert_fusion
  265.8 0.0 copy-start.4
  265.8 0.0 copy-done.2
  265.8 1.1 slice_bitcast_fusion
  266.9 0.6 slice_bitcast_fusion.7
  267.5 0.8 slice.66
  268.3 0.1 constant_dynamic-slice_fusion.2
  268.3 0.5 slice_bitcast_fusion.9
  268.9 0.8 slice.60
  269.6 0.1 constant_dynamic-slice_fusion.1
  269.7 0.1 copy.30
  269.8 0.6 reshape.75
  270.4 0.6 dynamic-slice_bitcast_fusion.1
  271.0 0.0 copy-done.4
  271.0 0.9 copy.32
  (4 shorter events, 0.1 us)
Async XLA Ops:
  0.6 0.9 copy-start
  0.7 6.4 %copy-start.3 = (bf16[4480,96]{0,1:T(8,128)(2,1)S(1)}, bf16[4480,96]{0,1:T(8,128)(2,1)}, u32[]{:S(2)}) copy-start(bf16[4480,96]{0,1:T(8,128)(2,1)} %param.29) | copy-start | bytes 2580484
  7.0 1.0 copy-start.6
  8.0 51.6 %copy-start.1 = (bf16[256,1536]{1,0:T(8,128)(2,1)S(1)}, bf16[256,1536]{1,0:T(8,128)(2,1)}, u32[]{:S(2)}) copy-start(bf16[256,1536]{1,0:T(8,128)(2,1)} %tok.1) | copy-start | bytes 2359300
  8.6 51.8 %copy-start.7 = (bf16[1536]{0:T(1024)(128)(2,1)S(1)}, bf16[1536]{0:T(1024)(128)(2,1)}, u32[]{:S(2)}) copy-start(bf16[1536]{0:T(1024)(128)(2,1)} %param.26) | copy-start | bytes 9220
  262.0 2.4 copy-start.5
  263.1 2.7 copy-start.2
  265.8 5.3 %copy-start.4 = (bf16[2,128,1536]{2,1,0:T(8,128)(2,1)S(1)}, bf16[2,128,1536]{2,1,0:T(8,128)(2,1)}, u32[]{:S(2)}) copy-start(bf16[2,128,1536]{2,1,0:T(8,128)(2,1)} %get-tuple-element.62) | copy-start | bytes 2359300

commit v5 on v4

--- a/solution.py
+++ b/solution.py
@@ -868,11 +868,11 @@
     heads,
     lse, start_ref, cosines, sines, tok, gain, gnf, *more,
 ):
-    far, outs, near_refs, rest_refs = more[:13], more[13:19], more[19:32], more[32:]
-    a_all, norm_sum, bias_sum, ffn_all, out, grad = outs
+    far, outs, near_refs, rest_refs = more[:13], more[13:22], more[22:35], more[35:]
+    q_grad, k_grad, v_grad, o_grad, norm_sum, bias_sum, ffn_all, out, grad = outs
     g, gate_sum, down_sum, ysum, dxl, attn, exact, q, kv, x1, ob, h1, dx1 = near_refs
     (
-    ext_all, do, dots, acc, keep, give, arrived, sums, landed, back, part, m1, m2, m3, left_t, ga,
+    a_all, ext_all, do, dots, acc, keep, give, arrived, sums, landed, back, part, m1, m2, m3, left_t, ga,
     own, passing, got, p2, q1, sm, q2, fin, fin_w, e0, e1, es, e2, y2,
     ls, d1, d2, d3, d4, ms, ca, cb, cc, cd, fs2, fr2, as1, ar1, as2, ar2, as3, ar3, xs, xr, ss, sr, ts, tr, ys, yr,
     gs, gr,
@@ -1001,7 +1001,7 @@
 
         @pl.when(b > 0)
         def _():
-            @pl.when(b == 2)
+            @pl.when(b == 1)
             def _():
                 early()
 
@@ -1013,7 +1013,7 @@
 
     lax.fori_loop(0, index + 1, step, 0)
 
-    @pl.when(index < 2)
+    @pl.when(index < 1)
     def _():
         early()
 
@@ -1195,6 +1195,11 @@
     norm_sum[...] = total
     for core in (0, 1):
         bias_sum[core] = ext_all[t, core] + ext_all[t, 2 + core]
+        total = a_all[core] + a_all[2 + core]
+        place = slice(core * width, (core + 1) * width)
+        q_grad[:, place] = total[:, :width]
+        (k_grad, v_grad)[core][...] = total[:, width:rowed]
+        o_grad[:, place] = total[:, rowed:]
 
 
 def rear(heads, g, gate_sum, down_sum, dxl, attn, q, kv, exact, lse, start, ob, h1, cosines, sines, ysum, x1, dx1, tok, gain, gnf):
@@ -1211,7 +1216,10 @@
     args = (lse, start, cosines, sines, tok, gain, gnf)
     far = (g, gate_sum, down_sum, ysum, dxl, attn, exact, q, kv, x1, ob, h1, dx1)
     outs = [
-        shape((4, quarter, total), F32),
+        shape((quarter, 2 * width), F32),
+        shape((quarter, size), F32),
+        shape((quarter, size), F32),
+        shape((quarter, 2 * width), F32),
         shape((8, model), F32),
         shape((2, 8, model), F32),
         shape((3, quarter, 4 * hidden), F32),
@@ -1225,6 +1233,7 @@
         out_specs=[VM] * len(outs),
         scratch_shapes=[pltpu.VMEM(array.shape, array.dtype) for array in far]
         + [
+            pltpu.VMEM((4, quarter, total), F32),
             pltpu.VMEM((2, 4, 8, model), F32),
             pltpu.VMEM((rows, width), BF),
             pltpu.VMEM((8, rows), F32),
@@ -1375,7 +1384,7 @@
     x1, dx1, dxl, grad_norm_two, ysum, gate_sum, down_sum, up_grad = block(
         part, own_tokens, gain_ffn, dy_all, halves
     )
-    a_all, norm_sum, bias_sum, ffn_all, output, grad_tokens = rear(
+    q_grad, k_grad, v_grad, o_grad, norm_sum, bias_sum, ffn_all, output, grad_tokens = rear(
         heads,
         up_grad,
         gate_sum,
@@ -1399,7 +1408,6 @@
         grad_norm_two,
     )
     owner_rows = shard_rows // 4
-    a_all = a_all[:2] + a_all[2:]
 
     owner = f * 4 + c
     norms = lax.dynamic_slice_in_dim(norm_sum[:2], owner * owner_rows, owner_rows, 1)
@@ -1408,13 +1416,13 @@
     return (
         output.reshape(count, model),
         grad_tokens.reshape(count, model).astype(F32),
-        jnp.concatenate([a_all[0, :, :query_width], a_all[1, :, :query_width]], axis=1),
-        a_all[0, :, query_width:own_width],
-        a_all[1, :, query_width:own_width],
+        q_grad,
+        k_grad,
+        v_grad,
         biases[:, :heads].reshape(2 * heads, 2),
         biases[0, heads:],
         biases[1, heads:],
-        jnp.concatenate([a_all[0, :, own_width:], a_all[1, :, own_width:]], axis=1).T,
+        o_grad.T,
         norms[0],
         norms[1],
         ffn_all[0, :, : 4 * hidden],

time: 273 us -> 272 us (level)
  no operation moved by 1% of the time
where the time goes in v5:
time: 272 us
  Pallas kernels  251 us (92%)
  local copies, waits for them, and re-layouts  13.7 us (5%)
  other arithmetic  6.17 us (2%)
    pallas_call x1, Pallas kernels, block(): pl.pallas_call(block_kernel, out_shape=[shape((rows, model), F32), shape(...  108 us
    pallas_call x1, Pallas kernels, rear(): pl.pallas_call(functools.partial(rear_kernel, heads), out_shape=outs, in_...  92.3 us
    pallas_call x1, Pallas kernels, front(): pl.pallas_call(functools.partial(front_kernel, heads), out_shape=outs, in...  50.9 us

profile of v5, /device:TPU:1, one launch (start us, length us, event | category | flops | bytes accessed | tf_op | source)
XLA Modules:
  0.0 271.6 jit_solution(8342850763323374457)
XLA Ops:
  0.6 0.0 copy-start
  0.7 0.0 copy-start.3
  0.7 0.9 copy-done
  1.6 0.9 dynamic-slice_bitcast_fusion
  2.5 0.7 broadcast_select_fusion
  3.2 0.7 pad_maximum_fusion.1.w
  3.9 0.8 dynamic_slice.32
  4.7 0.7 fusion.3
  5.3 0.6 maximum_convert_fusion.bias
  5.9 1.1 fusion
  7.0 0.0 copy-start.9
  7.0 0.0 copy-done.3
  7.1 0.9 pad_maximum_fusion.ffn
  8.0 0.0 copy-done.9
  8.0 0.0 copy-start.1
  8.0 0.6 reshape.76.gain
  8.6 0.0 copy-start.10
  8.6 50.9 %shard_map.263 = (bf16[4,4,96,896]{3,2,1,0:T(8,128)(2,1)}, bf16[3,2,4,48,1152]{4,3,2,1,0:T(8,128)(2,1)}, bf16[2,2,2,128,1536]{4,3,2,1,0:T(8,128)(2,1)}, bf16[512...) custom-call(bf16[96,896]{1,0:T(8,128)(2,1)} %pad_maximum_fusion.1.w,, ...), custom_call_target="tpu_custom_call" | custom-call | tf_op jit(solution)/shard_map/pallas_call | solution.py:470
  59.6 0.0 copy-done.1
  59.6 0.8 constant_dynamic-slice_fusion.3.tok
  60.3 0.0 copy-done.10
  60.3 0.6 reshape.77.gain
  60.9 107.7 %shard_map.264 = (f32[128,1536]{1,0:T(8,128)}, f32[128,1536]{1,0:T(8,128)}, bf16[2,2,128,1536]{3,2,1,0:T(8,128)(2,1)}, f32[1,1536]{1,0:T(1,128)}, bf16[4,128,153...) custom-call(bf16[2,2,128,1536]{3,2,1,0:T(8,128)(2,1)} %get-tuple-ele, ...), custom_call_target="tpu_custom_call" | custom-call | tf_op jit(solution)/shard_map/pallas_call | solution.py:806
  168.6 92.3 %shard_map.265 = (f32[24,768]{1,0:T(8,128)}, f32[24,128]{1,0:T(8,128)}, f32[24,128]{1,0:T(8,128)}, f32[24,768]{1,0:T(8,128)}, f32[8,1536]{1,0:T(8,128)}, /*index...) custom-call(f32[8,512]{1,0:T(8,128)} %get-tuple-element.44.lse, ...), custom_call_target="tpu_custom_call" | custom-call | tf_op jit(solution)/shard_map/pallas_call | solution.py:1229
  261.0 0.0 copy-start.2
  261.0 2.6 bitcast_convert_fusion
  263.6 0.0 copy-start.4
  263.6 0.0 copy-done.2
  263.6 0.0 copy-start.6
  263.6 1.1 slice_bitcast_fusion
  264.7 0.8 slice.34
  265.5 0.1 constant_dynamic-slice_fusion.2
  265.6 0.5 slice_bitcast_fusion.3
  266.1 0.8 slice.30
  266.9 0.1 constant_dynamic-slice_fusion.1
  266.9 0.1 copy.30
  267.0 0.6 reshape.75
  267.7 0.6 dynamic-slice_bitcast_fusion.1
  268.3 0.0 copy-done.4
  268.3 0.9 copy.36
  269.1 0.0 copy-done.6
  269.1 0.6 copy.37
  269.8 0.0 copy-done.8
  269.8 0.6 copy.38
  270.4 0.0 copy-done.7
  270.4 0.6 copy.39
  271.0 0.0 copy-done.5
  271.0 0.6 copy.40
  (6 shorter events, 0.1 us)
Async XLA Ops:
  0.6 0.9 copy-start
  0.7 6.4 %copy-start.3 = (bf16[4480,96]{0,1:T(8,128)(2,1)S(1)}, bf16[4480,96]{0,1:T(8,128)(2,1)}, u32[]{:S(2)}) copy-start(bf16[4480,96]{0,1:T(8,128)(2,1)} %param.29) | copy-start | bytes 2580484
  7.0 1.0 copy-start.9
  8.0 51.6 %copy-start.1 = (bf16[256,1536]{1,0:T(8,128)(2,1)S(1)}, bf16[256,1536]{1,0:T(8,128)(2,1)}, u32[]{:S(2)}) copy-start(bf16[256,1536]{1,0:T(8,128)(2,1)} %tok.1) | copy-start | bytes 2359300
  8.6 51.7 %copy-start.10 = (bf16[1536]{0:T(1024)(128)(2,1)S(1)}, bf16[1536]{0:T(1024)(128)(2,1)}, u32[]{:S(2)}) copy-start(bf16[1536]{0:T(1024)(128)(2,1)} %param.26) | copy-start | bytes 9220
  261.0 2.6 copy-start.2
  263.6 4.7 %copy-start.4 = (bf16[2,128,1536]{2,1,0:T(8,128)(2,1)S(1)}, bf16[2,128,1536]{2,1,0:T(8,128)(2,1)}, u32[]{:S(2)}) copy-start(bf16[2,128,1536]{2,1,0:T(8,128)(2,1)} %get-tuple-element.65) | copy-start | bytes 2359300
  263.6 5.6 %copy-start.6 = (f32[24,768]{1,0:T(8,128)S(1)}, f32[24,768]{1,0:T(8,128)}, u32[]{:S(2)}) copy-start(f32[24,768]{1,0:T(8,128)} %get-tuple-element.99) | copy-start | bytes 221188
  263.6 6.2 %copy-start.8 = (f32[24,128]{1,0:T(8,128)S(1)}, f32[24,128]{1,0:T(8,128)}, u32[]{:S(2)}) copy-start(f32[24,128]{1,0:T(8,128)} %get-tuple-element.100) | copy-start | bytes 36868
  264.7 5.7 %copy-start.7 = (f32[24,128]{1,0:T(8,128)S(1)}, f32[24,128]{1,0:T(8,128)}, u32[]{:S(2)}) copy-start(f32[24,128]{1,0:T(8,128)} %get-tuple-element.101) | copy-start | bytes 36868
  264.7 6.3 %copy-start.5 = (f32[24,768]{1,0:T(8,128)S(1)}, f32[24,768]{1,0:T(8,128)}, u32[]{:S(2)}) copy-start(f32[24,768]{1,0:T(8,128)} %get-tuple-element.71) | copy-start | bytes 221188

commit v6 on v5

--- a/solution.py
+++ b/solution.py
@@ -1155,13 +1155,6 @@
         send(es, e2.at[j - 1], ss.at[1, j - 1], sr.at[1, j - 1], me.along_y(j)) for j in offsets
     ]
 
-    for copy in small:
-        copy.wait()
-    ext_all[t, c] = (es[...] + e2[0]) + (e2[1] + e2[2])
-    mine = ext_all.at[t, c]
-    rest += [
-        send(mine, mine, xs.at[i], xr.at[i], in_x(dt, dc)) for i, (dt, dc) in enumerate(ring)
-    ]
     for copy in last:
         copy.wait()
     for half in (0, 1):
@@ -1175,6 +1168,13 @@
     rest += [
         send(fin.at[lax.rem(c + j, 4)], a_all.at[c], as3.at[j - 1], ar3.at[j - 1], in_x(0, j))
         for j in (2, 1, 3)
+    ]
+    for copy in small:
+        copy.wait()
+    ext_all[t, c] = (es[...] + e2[0]) + (e2[1] + e2[2])
+    mine = ext_all.at[t, c]
+    rest += [
+        send(mine, mine, xs.at[i], xr.at[i], in_x(dt, dc)) for i, (dt, dc) in enumerate(ring)
     ]
 
     def sent(b, _):

time: 272 us -> 273 us (level)
  no operation moved by 1% of the time
where the time goes in v6:
time: 273 us; the launch traced here: 272 us
  Pallas kernels  252 us (92%)
  local copies, waits for them, and re-layouts  13.7 us (5%)
  other arithmetic  6.17 us (2%)
    pallas_call x1, Pallas kernels, block(): pl.pallas_call(block_kernel, out_shape=[shape((rows, model), F32), shape(...  108 us
    pallas_call x1, Pallas kernels, rear(): pl.pallas_call(functools.partial(rear_kernel, heads), out_shape=outs, in_...  93.2 us
    pallas_call x1, Pallas kernels, front(): pl.pallas_call(functools.partial(front_kernel, heads), out_shape=outs, in...  50.9 us

profile of v6, /device:TPU:1, one launch (start us, length us, event | category | flops | bytes accessed | tf_op | source)
XLA Modules:
  0.0 272.5 jit_solution(2401998475502188616)
XLA Ops:
  0.6 0.0 copy-start
  0.7 0.0 copy-start.3
  0.7 0.9 copy-done
  1.6 0.9 dynamic-slice_bitcast_fusion
  2.5 0.7 broadcast_select_fusion
  3.2 0.7 pad_maximum_fusion.1.w
  3.9 0.8 dynamic_slice.32
  4.7 0.7 fusion.3
  5.3 0.6 maximum_convert_fusion.bias
  5.9 1.1 fusion
  7.0 0.0 copy-start.9
  7.0 0.0 copy-done.3
  7.1 0.9 pad_maximum_fusion.ffn
  8.0 0.0 copy-done.9
  8.0 0.0 copy-start.1
  8.0 0.6 reshape.76.gain
  8.6 0.0 copy-start.10
  8.6 50.9 %shard_map.263 = (bf16[4,4,96,896]{3,2,1,0:T(8,128)(2,1)}, bf16[3,2,4,48,1152]{4,3,2,1,0:T(8,128)(2,1)}, bf16[2,2,2,128,1536]{4,3,2,1,0:T(8,128)(2,1)}, bf16[512...) custom-call(bf16[96,896]{1,0:T(8,128)(2,1)} %pad_maximum_fusion.1.w,, ...), custom_call_target="tpu_custom_call" | custom-call | tf_op jit(solution)/shard_map/pallas_call | solution.py:470
  59.6 0.0 copy-done.1
  59.6 0.8 constant_dynamic-slice_fusion.3.tok
  60.3 0.0 copy-done.10
  60.3 0.6 reshape.77.gain
  60.9 107.7 %shard_map.264 = (f32[128,1536]{1,0:T(8,128)}, f32[128,1536]{1,0:T(8,128)}, bf16[2,2,128,1536]{3,2,1,0:T(8,128)(2,1)}, f32[1,1536]{1,0:T(1,128)}, bf16[4,128,153...) custom-call(bf16[2,2,128,1536]{3,2,1,0:T(8,128)(2,1)} %get-tuple-ele, ...), custom_call_target="tpu_custom_call" | custom-call | tf_op jit(solution)/shard_map/pallas_call | solution.py:806
  168.6 93.2 %shard_map.265 = (f32[24,768]{1,0:T(8,128)}, f32[24,128]{1,0:T(8,128)}, f32[24,128]{1,0:T(8,128)}, f32[24,768]{1,0:T(8,128)}, f32[8,1536]{1,0:T(8,128)}, /*index...) custom-call(f32[8,512]{1,0:T(8,128)} %get-tuple-element.44.lse, ...), custom_call_target="tpu_custom_call" | custom-call | tf_op jit(solution)/shard_map/pallas_call | solution.py:1229
  261.8 0.0 copy-start.2
  261.8 2.6 bitcast_convert_fusion
  264.4 0.0 copy-start.4
  264.4 0.0 copy-done.2
  264.4 0.0 copy-start.6
  264.4 1.1 slice_bitcast_fusion
  265.5 0.8 slice.34
  266.3 0.1 constant_dynamic-slice_fusion.2
  266.4 0.5 slice_bitcast_fusion.3
  266.9 0.8 slice.30
  267.7 0.1 constant_dynamic-slice_fusion.1
  267.8 0.1 copy.30
  267.9 0.6 reshape.75
  268.5 0.6 dynamic-slice_bitcast_fusion.1
  269.1 0.0 copy-done.4
  269.1 0.9 copy.36
  270.0 0.0 copy-done.6
  270.0 0.6 copy.37
  270.6 0.0 copy-done.8
  270.6 0.6 copy.38
  271.2 0.0 copy-done.7
  271.2 0.6 copy.39
  271.8 0.0 copy-done.5
  271.8 0.6 copy.40
  (6 shorter events, 0.1 us)
Async XLA Ops:
  0.6 0.9 copy-start
  0.7 6.4 %copy-start.3 = (bf16[4480,96]{0,1:T(8,128)(2,1)S(1)}, bf16[4480,96]{0,1:T(8,128)(2,1)}, u32[]{:S(2)}) copy-start(bf16[4480,96]{0,1:T(8,128)(2,1)} %param.29) | copy-start | bytes 2580484
  7.0 1.0 copy-start.9
  8.0 51.6 %copy-start.1 = (bf16[256,1536]{1,0:T(8,128)(2,1)S(1)}, bf16[256,1536]{1,0:T(8,128)(2,1)}, u32[]{:S(2)}) copy-start(bf16[256,1536]{1,0:T(8,128)(2,1)} %tok.1) | copy-start | bytes 2359300
  8.6 51.7 %copy-start.10 = (bf16[1536]{0:T(1024)(128)(2,1)S(1)}, bf16[1536]{0:T(1024)(128)(2,1)}, u32[]{:S(2)}) copy-start(bf16[1536]{0:T(1024)(128)(2,1)} %param.26) | copy-start | bytes 9220
  261.8 2.6 copy-start.2
  264.4 4.7 %copy-start.4 = (bf16[2,128,1536]{2,1,0:T(8,128)(2,1)S(1)}, bf16[2,128,1536]{2,1,0:T(8,128)(2,1)}, u32[]{:S(2)}) copy-start(bf16[2,128,1536]{2,1,0:T(8,128)(2,1)} %get-tuple-element.65) | copy-start | bytes 2359300
  264.4 5.6 %copy-start.6 = (f32[24,768]{1,0:T(8,128)S(1)}, f32[24,768]{1,0:T(8,128)}, u32[]{:S(2)}) copy-start(f32[24,768]{1,0:T(8,128)} %get-tuple-element.99) | copy-start | bytes 221188
  264.4 6.2 %copy-start.8 = (f32[24,128]{1,0:T(8,128)S(1)}, f32[24,128]{1,0:T(8,128)}, u32[]{:S(2)}) copy-start(f32[24,128]{1,0:T(8,128)} %get-tuple-element.100) | copy-start | bytes 36868
  265.5 5.7 %copy-start.7 = (f32[24,128]{1,0:T(8,128)S(1)}, f32[24,128]{1,0:T(8,128)}, u32[]{:S(2)}) copy-start(f32[24,128]{1,0:T(8,128)} %get-tuple-element.101) | copy-start | bytes 36868
  265.5 6.3 %copy-start.5 = (f32[24,768]{1,0:T(8,128)S(1)}, f32[24,768]{1,0:T(8,128)}, u32[]{:S(2)}) copy-start(f32[24,768]{1,0:T(8,128)} %get-tuple-element.71) | copy-start | bytes 221188
